TPU v7x, 128 devices: a whole 4x4x4 slice. The times are simulated.
128 devices in a mesh: wide: 8 (over y, core), narrow: 16 (over z, x).
Axes of the slice: x: 4, y: 4, z: 4, core: 2. Of those that a mesh axis runs over, the one named last changes fastest.
Arguments:
- token_ids: int32 [2, 16, 1024], P(None, 'narrow'), may hold values from 0 to 49151
- target_ids: int32 [2, 16, 1024], P(None, 'narrow'), may hold values from 0 to 49151
- prefix_lengths: int32 [2, 16], P(None, 'narrow'), may hold values from 102 to 512
- loss_positions: int32 [2, 16, 128], P(None, 'narrow'), may hold values from 0 to 1023, as said below
- w_input: float32 [1, 960, 1600], P(None, 'wide', 'narrow'), may hold values from -0.1875 to 0.1875
- w_output: float32 [1, 960, 960], P(None, 'wide', 'narrow'), may hold values from -0.375 to 0.375
- w_gate_up: float32 [1, 960, 5120], P(None, 'wide', 'narrow'), may hold values from -0.1875 to 0.1875
- w_down: float32 [1, 960, 2560], P(None, 'wide', 'narrow'), may hold values from -0.125 to 0.125
- norm_gains: float32 [3, 960], replicated, may hold values from 0.35 to 2.55
- embed_table: float32 [49152, 960], P(('wide', 'narrow')), may hold values from -0.5163978 to 0.5163978
- moment_input: float32 [1, 960, 1600], P(None, 'wide', 'narrow'), may hold values from -1.5258789e-05 to 1.5258789e-05
- moment_output: float32 [1, 960, 960], P(None, 'wide', 'narrow'), may hold values from -1.5258789e-05 to 1.5258789e-05
- moment_gate_up: float32 [1, 960, 5120], P(None, 'wide', 'narrow'), may hold values from -1.5258789e-05 to 1.5258789e-05
- moment_down: float32 [1, 960, 2560], P(None, 'wide', 'narrow'), may hold values from -1.5258789e-05 to 1.5258789e-05
- table_first: float32 [49152, 960], P(('wide', 'narrow')), may hold values from -1.66893e-06 to 1.66893e-06
- table_second: float32 [49152, 960], P(('wide', 'narrow')), may hold values from 3.68297e-13 to 1.473188e-12
- gains_first: float32 [3, 960], replicated, may hold values from -1.5258789e-05 to 1.5258789e-05
- gains_second: float32 [3, 960], replicated, may hold values from 3.68297e-11 to 1.473188e-10
Outputs:
- loss_sum: float32 [], replicated
- loss_count: float32 [], replicated
- grad_norm: float32 [], replicated
- new_moment_input: float32 [1, 960, 1600], P(None, 'wide', 'narrow')
- new_moment_output: float32 [1, 960, 960], P(None, 'wide', 'narrow')
- new_moment_gate_up: float32 [1, 960, 5120], P(None, 'wide', 'narrow')
- new_moment_down: float32 [1, 960, 2560], P(None, 'wide', 'narrow')
- new_w_input: float32 [1, 960, 1600], P(None, 'wide', 'narrow')
- new_w_output: float32 [1, 960, 960], P(None, 'wide', 'narrow')
- new_w_gate_up: float32 [1, 960, 5120], P(None, 'wide', 'narrow')
- new_w_down: float32 [1, 960, 2560], P(None, 'wide', 'narrow')
- low_w_input: bfloat16 [1, 960, 1600], P(None, 'wide', 'narrow')
- low_w_output: bfloat16 [1, 960, 960], P(None, 'wide', 'narrow')
- low_w_gate_up: bfloat16 [1, 960, 5120], P(None, 'wide', 'narrow')
- low_w_down: bfloat16 [1, 960, 2560], P(None, 'wide', 'narrow')
- new_table_first: float32 [49152, 960], P(('wide', 'narrow'))
- new_table_second: float32 [49152, 960], P(('wide', 'narrow'))
- new_table: float32 [49152, 960], P(('wide', 'narrow'))
- low_table: bfloat16 [49152, 960], P(('wide', 'narrow'))
- new_gains_first: float32 [3, 960], replicated
- new_gains_second: float32 [3, 960], replicated
- new_gains: float32 [3, 960], replicated
Inputs may be any that keep to these rules, and one draw needn't show every extreme that they name: Entry j of loss_positions[m, s] lies among positions (j // 16) * 128 to (j // 16) * 128 + 127.
All inputs are finite; a program needn't handle non-finite values.
Results may differ from a plain program's by a relative error of at most 0.007.
The roundings to bfloat16 on the way count: a program that leaves them out, or rounds other values in their place, can miss the bound.
Values may be sent and summed in bfloat16 or wider, within the bound.
A program may use at most 320 MiB of HBM per device.

v0:
```python
import math

import jax
import jax.numpy as jnp
from jax import lax
from jax.sharding import PartitionSpec as P

H = 15
KVH = 5
HD = 64
FF = 2560
V = 49152
ITERS = 5
STEP = 10


HIGHEST_PRECISION = lax.Precision.HIGHEST
NORM_EPS = 1e-05
ROPE_THETA = 100000.0
SMOOTH = 0.1
ZLOSS_WEIGHT = 0.0001
CLIP_NORM = 0.02
MOMENTUM = 0.95
NS_A = 3.4445
NS_B = -4.775
NS_C = 2.0315
MUON_RATE = 0.1
WEIGHT_DECAY = 0.1
BETA_ONE = 0.9
BETA_TWO = 0.95
TABLE_RATE = 0.03
GAIN_RATE = 0.4
ADAM_EPS = 1e-08
NEGATIVE = -1e30


def combined_all(value, axis, combine):
    everything = jax.tree.map(lambda part: lax.all_gather(part, axis), value)
    initial = jax.tree.map(lambda part: part[0], everything)

    def hop(k, so_far):
        return combine(so_far, jax.tree.map(lambda part: part[k], everything))

    return lax.fori_loop(1, lax.axis_size(axis), hop, initial)


def rms_norm(values, gain_row):
    return (
        values * lax.rsqrt(jnp.mean(values * values, axis=-1, keepdims=True) + NORM_EPS) * gain_row
    )


def rotate(values, places):
    half_width = HD // 2
    frequency = ROPE_THETA ** (-2.0 * jnp.arange(half_width).astype(jnp.float32) / HD)
    angles = places.astype(jnp.float32)[:, None] * frequency[None, :]
    cosine = jnp.concatenate([jnp.cos(angles), jnp.cos(angles)], axis=-1)[:, None, :]
    sine_part = jnp.concatenate([jnp.sin(angles), jnp.sin(angles)], axis=-1)[:, None, :]
    turned = jnp.concatenate([-values[..., half_width:], values[..., :half_width]], axis=-1)
    return values * cosine + turned * sine_part


def gated(gate_up):
    return gate_up[:, :FF] * jax.nn.sigmoid(gate_up[:, :FF]) * gate_up[:, FF:]


def contract(left_side, right_side, left_axis, right_axis):
    return lax.dot_general(
        left_side,
        right_side,
        (((left_axis,), (right_axis,)), ((), ())),
        preferred_element_type=jnp.float32,
    )


def combine_stats(first_stats, second_stats):
    highest = jnp.maximum(first_stats[0], second_stats[0])
    exp_total = first_stats[1] * jnp.exp(first_stats[0] - highest) + second_stats[1] * jnp.exp(
        second_stats[0] - highest
    )
    return (highest, exp_total, first_stats[2] + second_stats[2])


def adam_update(weight, first_moment, second_moment, gradient, step_rate, decay_rate):
    first_new = BETA_ONE * first_moment + (1.0 - BETA_ONE) * gradient
    second_new = BETA_TWO * second_moment + (1.0 - BETA_TWO) * gradient * gradient
    update = (
        first_new
        / (1.0 - BETA_ONE**STEP)
        / (jnp.sqrt(second_new / (1.0 - BETA_TWO**STEP)) + ADAM_EPS)
    )
    return (first_new, second_new, weight * (1.0 - step_rate * decay_rate) - step_rate * update)


def body(
    token_ids,
    target_ids,
    prefix_lengths,
    loss_positions,
    w_input,
    w_output,
    w_gate_up,
    w_down,
    norm_gains,
    embed_table,
    moment_input,
    moment_output,
    moment_gate_up,
    moment_down,
    table_first,
    table_second,
    gains_first,
    gains_second,
):
    wide_count = lax.axis_size("wide")
    narrow_count = lax.axis_size("narrow")
    wide_index = lax.axis_index("wide")
    seq_length = token_ids.shape[2]
    block_rows = seq_length // wide_count
    pick_rows = loss_positions.shape[2] // wide_count
    layer_count = w_input.shape[0]
    group_size = H // KVH
    kv_width = KVH * HD
    scale_factor = HD ** (-0.5)
    masters = (w_input, w_output, w_gate_up, w_down)
    moments = (moment_input, moment_output, moment_gate_up, moment_down)
    own_places = wide_index * block_rows + jnp.arange(block_rows)
    key_places = jnp.arange(seq_length)

    def attend_scores(query, key_rows, allowed):
        scores = (
            jnp.einsum("qkgd,tkd->kgqt", query, key_rows, preferred_element_type=jnp.float32)
            * scale_factor
        )
        return jnp.where(allowed, scores, NEGATIVE)

    def unrotate(gradient, heads):
        primal = jnp.zeros((block_rows, heads, HD), jnp.float32)
        return jax.vjp(lambda values: rotate(values, own_places), primal)[1](gradient)[0]

    def layer_backward(d_output, weights, layer_idx, allowed, stored):
        (
            residual,
            normed,
            query,
            key_rows,
            value_rows,
            log_total,
            attn_mixed,
            middle,
            normed_mid,
            gate_up,
            activated,
        ) = stored
        d_branch = d_output.astype(jnp.bfloat16)
        grad_down = contract(d_branch, activated, 0, 0)
        d_activated = jnp.dot(d_branch, weights[3][layer_idx], preferred_element_type=jnp.float32)
        d_gate_up = jax.vjp(gated, gate_up)[1](d_activated)[0].astype(jnp.bfloat16)
        grad_gate_up = contract(normed_mid, d_gate_up, 0, 0)
        d_normed_mid = contract(d_gate_up, weights[2][layer_idx], 1, 1)
        d_middle_part, d_gain_mlp = jax.vjp(rms_norm, middle, norm_gains[2 * layer_idx + 1])[1](
            d_normed_mid
        )
        d_middle = d_output + d_middle_part
        d_attn_out = d_middle.astype(jnp.bfloat16)
        grad_output = contract(attn_mixed, d_attn_out, 0, 0)
        d_mixed = (
            contract(d_attn_out, weights[1][layer_idx], 1, 1)
            .astype(jnp.bfloat16)
            .reshape(block_rows, KVH, group_size, HD)
        )
        scores = attend_scores(query, key_rows, allowed)
        probs_exact = jnp.exp(scores - log_total)
        d_probs = jnp.einsum(
            "qkgd,tkd->kgqt", d_mixed, value_rows, preferred_element_type=jnp.float32
        )
        d_scores = (
            probs_exact * (d_probs - jnp.sum(probs_exact * d_probs, axis=-1, keepdims=True))
        ).astype(jnp.bfloat16)
        d_query = (
            jnp.einsum("kgqt,tkd->qkgd", d_scores, key_rows, preferred_element_type=jnp.float32)
            * scale_factor
        )
        d_keys = (
            jnp.einsum("kgqt,qkgd->tkd", d_scores, query, preferred_element_type=jnp.float32)
            * scale_factor
        )
        d_values = jnp.einsum(
            "kgqt,qkgd->tkd",
            probs_exact.astype(jnp.bfloat16),
            d_mixed,
            preferred_element_type=jnp.float32,
        )
        d_key_own, d_value_own = (
            lax.psum_scatter(
                d_keys.reshape(seq_length, kv_width), "wide", scatter_dimension=0, tiled=True
            ),
            lax.psum_scatter(
                d_values.reshape(seq_length, kv_width), "wide", scatter_dimension=0, tiled=True
            ),
        )
        d_projected = jnp.concatenate(
            [
                unrotate(d_query.reshape(block_rows, H, HD), H).reshape(block_rows, H * HD),
                unrotate(d_key_own.reshape(block_rows, KVH, HD), KVH).reshape(block_rows, kv_width),
                d_value_own,
            ],
            axis=1,
        ).astype(jnp.bfloat16)
        grad_input = contract(normed, d_projected, 0, 0)
        d_normed = contract(d_projected, weights[0][layer_idx], 1, 1)
        d_residual_part, d_gain_attn = jax.vjp(rms_norm, residual, norm_gains[2 * layer_idx])[1](
            d_normed
        )
        return (
            d_middle + d_residual_part,
            (grad_input, grad_output, grad_gate_up, grad_down),
            (d_gain_attn, d_gain_mlp),
        )

    totals = None
    gain_grads = jnp.zeros(norm_gains.shape, jnp.float32)
    loss_local = jnp.zeros((), jnp.float32)
    count_local = jnp.zeros((), jnp.float32)
    counted_rows = jnp.zeros((norm_gains.shape[1],), jnp.float32)
    for batch_idx in range(token_ids.shape[0]):
        whole = (
            lax.all_gather(
                lax.all_gather(w_input.astype(jnp.bfloat16), "narrow", axis=2, tiled=True),
                "wide",
                axis=1,
                tiled=True,
            ),
            lax.all_gather(
                lax.all_gather(w_output.astype(jnp.bfloat16), "narrow", axis=2, tiled=True),
                "wide",
                axis=1,
                tiled=True,
            ),
            lax.all_gather(
                lax.all_gather(w_gate_up.astype(jnp.bfloat16), "narrow", axis=2, tiled=True),
                "wide",
                axis=1,
                tiled=True,
            ),
            lax.all_gather(
                lax.all_gather(w_down.astype(jnp.bfloat16), "narrow", axis=2, tiled=True),
                "wide",
                axis=1,
                tiled=True,
            ),
        )
        fetched = (
            whole,
            lax.all_gather(embed_table.astype(jnp.bfloat16), "narrow", axis=0, tiled=True),
        )
        weights, table_slab = fetched
        slab_rows = table_slab.shape[0]
        tokens = token_ids[batch_idx, 0]
        targets = target_ids[batch_idx, 0]
        prefix = prefix_lengths[batch_idx, 0]
        positions = loss_positions[batch_idx, 0]
        allowed = (key_places[None, :] <= own_places[:, None]) | (key_places[None, :] < prefix)
        local_ids = tokens - wide_index * slab_rows
        inside = (local_ids >= 0) & (local_ids < slab_rows)
        safe_ids = jnp.clip(local_ids, 0, slab_rows - 1)
        looked_up = jnp.where(inside[:, None], table_slab[safe_ids].astype(jnp.float32), 0.0)
        residual = lax.psum_scatter(
            looked_up.astype(jnp.bfloat16), "wide", scatter_dimension=0, tiled=True
        ).astype(jnp.float32)
        layer_idx = 0
        layer_normed = rms_norm(residual, norm_gains[2 * layer_idx]).astype(jnp.bfloat16)
        projected = jnp.dot(layer_normed, weights[0][layer_idx], preferred_element_type=jnp.float32)
        layer_query = (
            rotate(projected[:, : H * HD].reshape(block_rows, H, HD), own_places)
            .astype(jnp.bfloat16)
            .reshape(block_rows, KVH, group_size, HD)
        )
        key_own = (
            rotate(
                projected[:, H * HD : H * HD + kv_width].reshape(block_rows, KVH, HD), own_places
            )
            .astype(jnp.bfloat16)
            .reshape(block_rows, kv_width)
        )
        value_own = projected[:, H * HD + kv_width :].astype(jnp.bfloat16)
        layer_key_rows = lax.all_gather(key_own, "wide", axis=0, tiled=True)
        layer_value_rows = lax.all_gather(value_own, "wide", axis=0, tiled=True)
        layer_key_rows = layer_key_rows.reshape(seq_length, KVH, HD)
        layer_value_rows = layer_value_rows.reshape(seq_length, KVH, HD)
        layer_scores = attend_scores(layer_query, layer_key_rows, allowed)
        highest = jnp.max(layer_scores, axis=-1, keepdims=True)
        exp_part = jnp.exp(layer_scores - highest)
        exp_total = jnp.sum(exp_part, axis=-1, keepdims=True)
        layer_log_total = highest + jnp.log(exp_total)
        attn_probs = (exp_part / exp_total).astype(jnp.bfloat16)
        layer_attn_mixed = (
            jnp.einsum(
                "kgqt,tkd->qkgd", attn_probs, layer_value_rows, preferred_element_type=jnp.float32
            )
            .reshape(block_rows, H * HD)
            .astype(jnp.bfloat16)
        )
        layer_middle = residual + jnp.dot(
            layer_attn_mixed, weights[1][layer_idx], preferred_element_type=jnp.float32
        )
        layer_normed_mid = rms_norm(layer_middle, norm_gains[2 * layer_idx + 1]).astype(
            jnp.bfloat16
        )
        layer_gate_up = jnp.dot(
            layer_normed_mid, weights[2][layer_idx], preferred_element_type=jnp.float32
        )
        layer_activated = gated(layer_gate_up).astype(jnp.bfloat16)
        output = layer_middle + contract(layer_activated, weights[3][layer_idx], 1, 1)
        layer_stored = (
            residual,
            layer_normed,
            layer_query,
            layer_key_rows,
            layer_value_rows,
            layer_log_total,
            layer_attn_mixed,
            layer_middle,
            layer_normed_mid,
            layer_gate_up,
            layer_activated,
        )
        residual = output
        stored = layer_stored
        stored_list = [stored]
        final_gain = norm_gains[2 * layer_count]
        final_rows = rms_norm(residual, final_gain).astype(jnp.bfloat16)
        own_offsets = (
            lax.dynamic_slice_in_dim(positions, wide_index * pick_rows, pick_rows)
            - wide_index * block_rows
        )
        own_picked = final_rows[own_offsets]
        rows_all = lax.all_gather(own_picked, "wide", axis=0, tiled=True)
        counted = (positions >= prefix).astype(jnp.float32)
        target_hit = (
            jnp.arange(slab_rows)[None, :] == (targets[positions] - wide_index * slab_rows)[:, None]
        ).astype(jnp.float32)
        logits = contract(rows_all, table_slab, 1, 1)
        highest = jnp.max(logits, axis=-1)
        row_stats = (
            highest,
            jnp.sum(jnp.exp(logits - highest[:, None]), axis=-1),
            jnp.sum(logits * target_hit, axis=-1),
        )
        merged = combined_all(row_stats, "wide", combine_stats)
        log_total = merged[0] + jnp.log(merged[1])
        per_row = (
            (1.0 - SMOOTH) * (log_total - merged[2])
            + SMOOTH * log_total
            + ZLOSS_WEIGHT * log_total * log_total
        )
        own_counted = lax.dynamic_slice_in_dim(counted, wide_index * pick_rows, pick_rows)
        loss_local = loss_local + jnp.sum(
            lax.dynamic_slice_in_dim(per_row, wide_index * pick_rows, pick_rows) * own_counted
        )
        count_local = count_local + jnp.sum(own_counted)
        counted_rows = counted_rows + jnp.sum(
            own_picked.astype(jnp.float32) * own_counted[:, None], axis=0
        )
        d_logits = (
            counted[:, None]
            * (
                (1.0 + 2.0 * ZLOSS_WEIGHT * log_total)[:, None]
                * jnp.exp(logits - log_total[:, None])
                - (1.0 - SMOOTH) * target_hit
                - SMOOTH / V
            )
        ).astype(jnp.bfloat16)
        d_rows = lax.psum_scatter(
            jnp.dot(d_logits, table_slab, preferred_element_type=jnp.float32),
            "wide",
            scatter_dimension=0,
            tiled=True,
        )
        table_grad = contract(d_logits, rows_all, 0, 0)
        d_final = (
            jnp.zeros((block_rows, final_rows.shape[1]), jnp.float32).at[own_offsets].add(d_rows)
        )
        d_residual, d_gain_final = jax.vjp(rms_norm, residual, final_gain)[1](d_final)
        gain_grads = gain_grads.at[2 * layer_count].add(d_gain_final)
        layer_grads = [None] * layer_count
        for layer_idx in reversed(range(layer_count)):
            d_residual, layer_grads[layer_idx], gain_pair = layer_backward(
                d_residual, weights, layer_idx, allowed, stored_list[layer_idx]
            )
            gain_grads = (
                gain_grads.at[2 * layer_idx]
                .add(gain_pair[0])
                .at[2 * layer_idx + 1]
                .add(gain_pair[1])
            )
        d_embed = lax.all_gather(d_residual.astype(jnp.bfloat16), "wide", axis=0, tiled=True)
        table_grad = table_grad.at[safe_ids].add(
            jnp.where(inside[:, None], d_embed.astype(jnp.float32), 0.0)
        )
        batch_grads = tuple(
            (jnp.stack([grad_set[kind_idx] for grad_set in layer_grads]) for kind_idx in range(4))
        ) + (table_grad,)
        totals = (
            batch_grads
            if totals is None
            else tuple(
                (earlier_sum + addition for earlier_sum, addition in zip(totals, batch_grads))
            )
        )
    totals = (
        lax.psum_scatter(
            lax.psum_scatter(totals[0], "narrow", scatter_dimension=2, tiled=True),
            "wide",
            scatter_dimension=1,
            tiled=True,
        ),
        lax.psum_scatter(
            lax.psum_scatter(totals[1], "narrow", scatter_dimension=2, tiled=True),
            "wide",
            scatter_dimension=1,
            tiled=True,
        ),
        lax.psum_scatter(
            lax.psum_scatter(totals[2], "narrow", scatter_dimension=2, tiled=True),
            "wide",
            scatter_dimension=1,
            tiled=True,
        ),
        lax.psum_scatter(
            lax.psum_scatter(totals[3], "narrow", scatter_dimension=2, tiled=True),
            "wide",
            scatter_dimension=1,
            tiled=True,
        ),
        lax.psum_scatter(totals[4], "narrow", scatter_dimension=0, tiled=True),
    )
    column_sums = jnp.sum(embed_table.astype(jnp.bfloat16).astype(jnp.float32), axis=0)
    grad_squares = jnp.stack(
        [jnp.sum(totals[kind_idx] * totals[kind_idx], axis=(1, 2)) for kind_idx in range(4)]
    )
    cross_terms = jnp.stack(
        [jnp.sum(totals[kind_idx] * moments[kind_idx], axis=(1, 2)) for kind_idx in range(4)]
    )
    moment_squares = jnp.stack(
        [jnp.sum(moments[kind_idx] * moments[kind_idx], axis=(1, 2)) for kind_idx in range(4)]
    )
    table_squares = jnp.sum(totals[4] * totals[4])
    summed = lax.psum(
        (
            grad_squares,
            cross_terms,
            moment_squares,
            table_squares,
            gain_grads,
            loss_local,
            count_local,
            counted_rows,
            column_sums,
        ),
        ("wide", "narrow"),
    )
    token_count = summed[6]
    loss_total = summed[5] - SMOOTH / V * jnp.sum(summed[7] * summed[8])
    grad_norm = (
        jnp.sqrt(jnp.sum(summed[0]) + summed[3] + jnp.sum(summed[4] * summed[4])) / token_count
    )
    factor = jnp.minimum(1.0, CLIP_NORM / grad_norm) / token_count
    frobenius = jnp.sqrt(
        MOMENTUM * MOMENTUM * summed[2]
        + 2.0 * MOMENTUM * factor * summed[1]
        + factor * factor * summed[0]
    )
    new_moments = tuple(
        (MOMENTUM * moments[kind_idx] + factor * totals[kind_idx] for kind_idx in range(4))
    )
    current = tuple(
        (
            new_moments[kind_idx] / (frobenius[kind_idx][:, None, None] + 1e-07)
            for kind_idx in range(4)
        )
    )

    def columns_of(matrices):
        return (
            lax.all_gather(matrices[0], "wide", axis=1, tiled=True),
            lax.all_gather(matrices[1], "wide", axis=1, tiled=True),
            lax.all_gather(matrices[2], "wide", axis=1, tiled=True),
            lax.all_gather(matrices[3], "wide", axis=1, tiled=True),
        )

    for ns_step in range(ITERS):
        full_columns = columns_of(current)
        partial_grams = [
            jnp.einsum(
                "lrc,lsc->lrs",
                current[kind_idx],
                full_columns[kind_idx],
                precision=HIGHEST_PRECISION,
            )
            for kind_idx in range(4)
        ]
        gram_rows = lax.psum(
            (partial_grams[0], partial_grams[1], partial_grams[2], partial_grams[3]), "narrow"
        )
        applied = [
            jnp.einsum(
                "lrs,lsc->lrc",
                gram_rows[kind_idx],
                full_columns[kind_idx],
                precision=HIGHEST_PRECISION,
            )
            for kind_idx in range(4)
        ]
        applied_columns = columns_of(applied)
        current = tuple(
            (
                NS_A * current[kind_idx]
                + NS_B * applied[kind_idx]
                + NS_C
                * jnp.einsum(
                    "lrs,lsc->lrc",
                    gram_rows[kind_idx],
                    applied_columns[kind_idx],
                    precision=HIGHEST_PRECISION,
                )
                for kind_idx in range(4)
            )
        )
    new_weights = tuple(
        (
            masters[kind_idx] * (1.0 - MUON_RATE * WEIGHT_DECAY)
            - MUON_RATE
            * 0.2
            * math.sqrt(masters[kind_idx].shape[2] * narrow_count)
            * current[kind_idx]
            for kind_idx in range(4)
        )
    )
    table_m, table_v, table_new = adam_update(
        embed_table, table_first, table_second, factor * totals[4], TABLE_RATE, WEIGHT_DECAY
    )
    gains_m, gains_v, gains_new = adam_update(
        norm_gains, gains_first, gains_second, factor * summed[4], GAIN_RATE, 0.0
    )
    return (
        loss_total,
        token_count,
        grad_norm,
        new_moments[0],
        new_moments[1],
        new_moments[2],
        new_moments[3],
        new_weights[0],
        new_weights[1],
        new_weights[2],
        new_weights[3],
        new_weights[0].astype(jnp.bfloat16),
        new_weights[1].astype(jnp.bfloat16),
        new_weights[2].astype(jnp.bfloat16),
        new_weights[3].astype(jnp.bfloat16),
        table_m,
        table_v,
        table_new,
        table_new.astype(jnp.bfloat16),
        gains_m,
        gains_v,
        gains_new,
    )


def solution(mesh):
    placed = (
        P(None, "narrow", None),
        P(None, "narrow", None),
        P(None, "narrow"),
        P(None, "narrow", None),
        P(None, "wide", "narrow"),
        P(None, "wide", "narrow"),
        P(None, "wide", "narrow"),
        P(None, "wide", "narrow"),
        P(),
        P(("wide", "narrow"), None),
        P(None, "wide", "narrow"),
        P(None, "wide", "narrow"),
        P(None, "wide", "narrow"),
        P(None, "wide", "narrow"),
        P(("wide", "narrow"), None),
        P(("wide", "narrow"), None),
        P(),
        P(),
    )
    return jax.shard_map(
        body,
        mesh=mesh,
        in_specs=placed,
        out_specs=(
            P(),
            P(),
            P(),
            P(None, "wide", "narrow"),
            P(None, "wide", "narrow"),
            P(None, "wide", "narrow"),
            P(None, "wide", "narrow"),
            P(None, "wide", "narrow"),
            P(None, "wide", "narrow"),
            P(None, "wide", "narrow"),
            P(None, "wide", "narrow"),
            P(None, "wide", "narrow"),
            P(None, "wide", "narrow"),
            P(None, "wide", "narrow"),
            P(None, "wide", "narrow"),
            P(("wide", "narrow"), None),
            P(("wide", "narrow"), None),
            P(("wide", "narrow"), None),
            P(("wide", "narrow"), None),
            P(),
            P(),
            P(),
        ),
        check_vma=False,
    )
```

profile of v0, /device:TPU:1, one launch (start us, length us, event | category | flops | bytes accessed | tf_op | source)
XLA Modules:
  0.0 2783.4 jit_solution(9321731135677187108)
XLA Ops:
  11.9 92.6 %all-gather.73.cloned.1.call-done = bf16[6144,960]{1,0:T(8,128)(2,1)} async-done(((bf16[384,960]{1,0:T(8,128)(2,1)}), bf16[6144,960]{1,0:T(8,128)(2,1)}) %all-gather.73.cloned.1.call-update) | async-done | bytes 11796496 | tf_op jit(solution)/shard_map/all_gather | solution.py:255
  125.6 21.2 all_gather.217
  167.2 18.4 all_gather.221
  189.5 19.5 all_gather.225
  256.4 18.1 all_gather.220
  296.5 41.8 %all-gather.81.cloned.1.call-done = bf16[1,960,5120]{2,1,0:T(8,128)(2,1)} async-done(((bf16[1,120,5120]{2,1,0:T(8,128)(2,1)}), bf16[1,960,5120]{2,1,0:T(8,128)(2,1)}) %all-gather.81.cloned.1.call-update) | async-done | bytes 9830416 | tf_op jit(solution)/shard_map/all_gather | solution.py:240
  345.2 30.7 %all-gather.83.cloned.1.call-done = bf16[1,960,2560]{2,1,0:T(8,128)(2,1)} async-done(((bf16[1,120,2560]{2,1,0:T(8,128)(2,1)}), bf16[1,960,2560]{2,1,0:T(8,128)(2,1)}) %all-gather.83.cloned.1.call-update) | async-done | bytes 4915216 | tf_op jit(solution)/shard_map/all_gather | solution.py:246
  541.8 24.8 reduce-scatter.35.cloned.1.call-done
  660.6 33.5 %reduce-scatter.37.cloned.1.call-done = f32[128,320]{0,1:T(8,128)} async-done(((f32[1024,320]{0,1:T(8,128)}), f32[128,320]{0,1:T(8,128)}) %reduce-scatter.37.cloned.1.call-update) | async-done | bytes 163856 | tf_op jit(solution)/shard_map/reduce_scatter | solution.py:195
  700.1 27.4 reduce-scatter.39.cloned.1.call-done
  735.2 16.4 copy.413
  773.7 22.2 copy.419
  820.6 43.0 %copy.417 = f32[1,960,5120]{1,0,2:T(1,128)} copy(f32[1,960,5120]{2,1,0:T(8,128)} %add_bitcast_fusion) | data formatting | bytes 39321600 | tf_op jit(solution)/shard_map/add | solution.py:408
  881.0 198.0 %all-reduce.52.cloned.1.call-done = (f32[1,960,2560]{1,0,2:T(1,128)}, f32[1,960,960]{1,0,2:T(1,128)}) async-done(((f32[1,960,2560]{1,0,2:T(1,128)}, f32[1,960,960]{1,0,2:T(1,128)}), (f32[1,960,2560]{1,0,2:T(1,128)}, f32[1,960,960]{1,0,2:T(1,128)})) %all-reduce.52.cloned.1.call-update) | async-done | bytes 13516816
  1102.2 243.3 %all-reduce.40.cloned.1.call-done = f32[1,960,5120]{1,0,2:T(1,128)} async-done(((f32[1,960,5120]{1,0,2:T(1,128)}), f32[1,960,5120]{1,0,2:T(1,128)}) %all-reduce.40.cloned.1.call-update) | async-done | bytes 19660816
  1368.7 24.2 copy.421
  1419.0 35.6 %scatter_fusion = f32[6144,960]{1,0:T(8,128)} fusion(f32[6144,960]{1,0:T(8,128)} %copy.421, s32[2048]{0:T(1024)S(1)} %bitcast.937, f32[2048,960]{1,0:T(8,128)} %copy.422), kind=kCustom, calls=%fused_computation.8 | custom fusion | flops 1966080 | bytes 23601152 | tf_op jit(solution)/shard_map/add | solution.py:408
  1468.3 32.1 %reduce-scatter.47.cloned.1.call-done = f32[120,160]{1,0:T(8,128)} async-done(((f32[960,160]{1,0:T(8,128)}), f32[120,160]{1,0:T(8,128)}) %reduce-scatter.47.cloned.1.call-update) | async-done | bytes 76816
  1504.8 29.8 %reduce-scatter.53.cloned.1.call-done = f32[1,120,320]{2,1,0:T(8,128)} async-done(((f32[1,960,320]{2,1,0:T(8,128)}), f32[1,120,320]{2,1,0:T(8,128)}) %reduce-scatter.53.cloned.1.call-update) | async-done | bytes 153616
  1542.6 150.4 %reduce-scatter.41.cloned.1.call-done = f32[384,960]{1,0:T(8,128)} async-done(((f32[6144,960]{1,0:T(8,128)}), f32[384,960]{1,0:T(8,128)}) %reduce-scatter.41.cloned.1.call-update) | async-done | bytes 1474576 | tf_op jit(solution)/shard_map/reduce_scatter | solution.py:436
  1695.4 65.0 %all-reduce.22 = (f32[]{:T(128)}, f32[960]{0:T(1024)}, f32[960]{0:T(1024)}, f32[]{:T(128)}, f32[4,1]{0,1:T(1,128)S(1)}, /*index=5*/f32[]{:T(128)}, f32[3,960]{1,...) all-reduce(f32[]{:T(128)S(6)} %add.774, ...), channel_id=1, replica_groups=mesh['wide'=8,'narrow'=16] {'wide','narrow'}, use_global_device_ids=true, to_apply=%region_24.25 | all-reduce | flops 4815 | bytes 38520 | tf_op jit(solution)/shard_map/psum | solution.py:449
  1769.5 15.8 all_gather.275
  1825.1 85.3 %all-reduce.50.cloned.1.call-done = (f32[120,960]{1,0:T(8,128)}, f32[120,960]{1,0:T(8,128)}, f32[120,960]{1,0:T(8,128)}, f32[120,960]{1,0:T(8,128)}) async-done(((f32[120,960]{1,0:T(8,128)}, f32[120,960]{1,0:T(8,128)}, f32[120,960]{1,0:T(8,128)}, f32[120,960]{1,0:T(8,128)}), (f32[120,960]{1,0:T(8,128)}, f32[120,960]{1,0:T(8,128)}, f32[120,960]{1,0:T(8,128)}, ...) | async-done | bytes 1843216 | tf_op jit(solution)/shard_map/psum | solution.py:503
  1915.2 15.8 all-gather.49
  2022.6 87.1 %all-reduce.48.cloned.1.call-done = (f32[120,960]{1,0:T(8,128)}, f32[120,960]{1,0:T(8,128)}, f32[120,960]{1,0:T(8,128)}, f32[120,960]{1,0:T(8,128)}) async-done(((f32[120,960]{1,0:T(8,128)}, f32[120,960]{1,0:T(8,128)}, f32[120,960]{1,0:T(8,128)}, f32[120,960]{1,0:T(8,128)}), (f32[120,960]{1,0:T(8,128)}, f32[120,960]{1,0:T(8,128)}, f32[120,960]{1,0:T(8,128)}, ...) | async-done | bytes 1843216 | tf_op jit(solution)/shard_map/psum | solution.py:503
  2114.4 15.9 all-gather.50
  2221.7 87.6 %all-reduce.46.cloned.1.call-done = (f32[120,960]{1,0:T(8,128)}, f32[120,960]{1,0:T(8,128)}, f32[120,960]{1,0:T(8,128)}, f32[120,960]{1,0:T(8,128)}) async-done(((f32[120,960]{1,0:T(8,128)}, f32[120,960]{1,0:T(8,128)}, f32[120,960]{1,0:T(8,128)}, f32[120,960]{1,0:T(8,128)}), (f32[120,960]{1,0:T(8,128)}, f32[120,960]{1,0:T(8,128)}, f32[120,960]{1,0:T(8,128)}, ...) | async-done | bytes 1843216 | tf_op jit(solution)/shard_map/psum | solution.py:503
  2314.0 15.8 all-gather.51
  2421.3 87.1 %all-reduce.44.cloned.1.call-done = (f32[120,960]{1,0:T(8,128)}, f32[120,960]{1,0:T(8,128)}, f32[120,960]{1,0:T(8,128)}, f32[120,960]{1,0:T(8,128)}) async-done(((f32[120,960]{1,0:T(8,128)}, f32[120,960]{1,0:T(8,128)}, f32[120,960]{1,0:T(8,128)}, f32[120,960]{1,0:T(8,128)}), (f32[120,960]{1,0:T(8,128)}, f32[120,960]{1,0:T(8,128)}, f32[120,960]{1,0:T(8,128)}, ...) | async-done | bytes 1843216 | tf_op jit(solution)/shard_map/psum | solution.py:503
  2513.2 15.8 all-gather.52
  2647.7 59.7 %all-reduce.42.cloned.1.call-done = (f32[120,960]{1,0:T(8,128)}, f32[120,960]{1,0:T(8,128)}, f32[120,960]{1,0:T(8,128)}, f32[120,960]{1,0:T(8,128)}) async-done(((f32[120,960]{1,0:T(8,128)}, f32[120,960]{1,0:T(8,128)}, f32[120,960]{1,0:T(8,128)}, f32[120,960]{1,0:T(8,128)}), (f32[120,960]{1,0:T(8,128)}, f32[120,960]{1,0:T(8,128)}, f32[120,960]{1,0:T(8,128)}, ...) | async-done | bytes 1843216 | tf_op jit(solution)/shard_map/psum | solution.py:503
  2714.7 16.2 all-gather.53
  (993 shorter events, 1059.1 us)
Async XLA Ops:
  10.9 176.1 %all-gather.79.cloned.1.call-start = ((), (), s32[]{:S(2)}) async-start(), calls=%async_computation.16 | async-start | bytes 1392640 | tf_op jit(solution)/shard_map/all_gather | solution.py:241
  11.7 218.5 %reduce-scatter.43.cloned.1.call-start = ((), (), s32[]{:S(2)}) async-start(), calls=%async_computation.38 | async-start | bytes 2359296
  125.5 106.1 %all-gather.75.cloned.1.call-start = ((), (), s32[]{:S(2)}) async-start(), calls=%async_computation.14 | async-start | bytes 3594240 | tf_op jit(solution)/shard_map/all_gather | solution.py:228
  167.1 126.3 %all-gather.77.cloned.1.call-start = ((), (), s32[]{:S(2)}) async-start(), calls=%async_computation.15 | async-start | bytes 2211840 | tf_op jit(solution)/shard_map/all_gather | solution.py:234
  186.9 151.3 %all-gather.81.cloned.1.call-start = ((), (), s32[]{:S(2)}) async-start(), calls=%async_computation.17 | async-start | bytes 11059200 | tf_op jit(solution)/shard_map/all_gather | solution.py:240
  189.4 186.5 %all-gather.83.cloned.1.call-start = ((), (), s32[]{:S(2)}) async-start(), calls=%async_computation.18 | async-start | bytes 5529600 | tf_op jit(solution)/shard_map/all_gather | solution.py:246
  210.1 329.5 %reduce-scatter.29.cloned.1.call-start = ((), (), s32[]{:S(2)}) async-start(), calls=%async_computation.19 | async-start | bytes 589824 | tf_op jit(solution)/shard_map/reduce_scatter | solution.py:374
  539.5 109.4 %reduce-scatter.33.cloned.1.call-start = ((), (), s32[]{:S(2)}) async-start(), calls=%async_computation.21 | async-start | bytes 1474560 | tf_op jit(solution)/shard_map/reduce_scatter | solution.py:198
  645.3 232.9 %all-reduce.38.cloned.1.call-start = ((), (), s32[]{:S(2)}) async-start(), calls=%async_computation.41 | async-start | bytes 13107200
  751.7 327.4 %all-reduce.52.cloned.1.call-start = ((), (), s32[]{:S(2)}) async-start(), calls=%async_computation.51 | async-start | bytes 28835840
  795.9 549.5 %all-reduce.40.cloned.1.call-start = ((), (), s32[]{:S(2)}) async-start(), calls=%async_computation.42 | async-start | bytes 41943040
  863.7 529.2 %all-gather.85.cloned.1.call-start = ((), (), s32[]{:S(2)}) async-start(), calls=%async_computation.25 | async-start | bytes 2211840 | tf_op jit(solution)/shard_map/all_gather | solution.py:397
  870.2 533.3 %all-gather.87.cloned.1.call-start = ((), (), s32[]{:S(2)}) async-start(), calls=%async_computation.26 | async-start | bytes 2211840 | tf_op jit(solution)/shard_map/all_gather | solution.py:397
  870.9 592.3 %reduce-scatter.49.cloned.1.call-start = ((), (), s32[]{:S(2)}) async-start(), calls=%async_computation.43 | async-start | bytes 552960
  880.3 586.4 %reduce-scatter.51.cloned.1.call-start = ((), (), s32[]{:S(2)}) async-start(), calls=%async_computation.44 | async-start | bytes 552960
  1081.1 419.3 %reduce-scatter.47.cloned.1.call-start = ((), (), s32[]{:S(2)}) async-start(), calls=%async_computation.40 | async-start | bytes 1105920
  1092.0 442.6 %reduce-scatter.53.cloned.1.call-start = ((), (), s32[]{:S(2)}) async-start(), calls=%async_computation.45 | async-start | bytes 1658880
  1352.5 340.4 %reduce-scatter.41.cloned.1.call-start = ((), (), s32[]{:S(2)}) async-start(), calls=%async_computation.27 | async-start | bytes 26738688 | tf_op jit(solution)/shard_map/reduce_scatter | solution.py:436
  1454.7 364.9 %all-gather.89.cloned.1.call-start = ((), (), s32[]{:S(2)}) async-start(), calls=%async_computation.28 | async-start | bytes 1658880 | tf_op jit(solution)/shard_map/all_gather | solution.py:488
  1767.8 142.7 %all-reduce.50.cloned.1.call-start = ((), (), s32[]{:S(2)}) async-start(), calls=%async_computation.50 | async-start | bytes 3932160 | tf_op jit(solution)/shard_map/psum | solution.py:503
  1825.1 122.2 %all-gather.99.cloned.1.call-start = ((), (), s32[]{:S(2)}) async-start(), calls=%async_computation.33 | async-start | bytes 1474560 | tf_op jit(solution)/shard_map/all_gather | solution.py:488
  1913.5 103.6 %all-gather.91.cloned.1.call-start = ((), (), s32[]{:S(2)}) async-start(), calls=%async_computation.29 | async-start | bytes 1658880 | tf_op jit(solution)/shard_map/all_gather | solution.py:488
  1953.0 156.7 %all-reduce.48.cloned.1.call-start = ((), (), s32[]{:S(2)}) async-start(), calls=%async_computation.49 | async-start | bytes 3932160 | tf_op jit(solution)/shard_map/psum | solution.py:503
  2022.5 123.9 %all-gather.101.cloned.1.call-start = ((), (), s32[]{:S(2)}) async-start(), calls=%async_computation.34 | async-start | bytes 1474560 | tf_op jit(solution)/shard_map/all_gather | solution.py:488
  2152.1 157.2 %all-reduce.46.cloned.1.call-start = ((), (), s32[]{:S(2)}) async-start(), calls=%async_computation.48 | async-start | bytes 3932160 | tf_op jit(solution)/shard_map/psum | solution.py:503
  2221.6 124.5 %all-gather.103.cloned.1.call-start = ((), (), s32[]{:S(2)}) async-start(), calls=%async_computation.35 | async-start | bytes 1474560 | tf_op jit(solution)/shard_map/all_gather | solution.py:488
  2312.2 103.6 %all-gather.95.cloned.1.call-start = ((), (), s32[]{:S(2)}) async-start(), calls=%async_computation.31 | async-start | bytes 1658880 | tf_op jit(solution)/shard_map/all_gather | solution.py:488
  2351.7 156.7 %all-reduce.44.cloned.1.call-start = ((), (), s32[]{:S(2)}) async-start(), calls=%async_computation.47 | async-start | bytes 3932160 | tf_op jit(solution)/shard_map/psum | solution.py:503
  2421.3 124.3 %all-gather.105.cloned.1.call-start = ((), (), s32[]{:S(2)}) async-start(), calls=%async_computation.36 | async-start | bytes 1474560 | tf_op jit(solution)/shard_map/all_gather | solution.py:488
  2511.4 103.7 %all-gather.97.cloned.1.call-start = ((), (), s32[]{:S(2)}) async-start(), calls=%async_computation.32 | async-start | bytes 1658880 | tf_op jit(solution)/shard_map/all_gather | solution.py:488
  2551.3 156.2 %all-reduce.42.cloned.1.call-start = ((), (), s32[]{:S(2)}) async-start(), calls=%async_computation.46 | async-start | bytes 3932160 | tf_op jit(solution)/shard_map/psum | solution.py:503
  2620.5 148.2 %all-gather.107.cloned.1.call-start = ((), (), s32[]{:S(2)}) async-start(), calls=%async_computation.37 | async-start | bytes 1474560 | tf_op jit(solution)/shard_map/all_gather | solution.py:488
  (246 other events, 7652.1 us)
Sparse Core Ops, SparseCore 0:
  11.0 93.3 all-gather.72
  107.1 43.9 all-gather.78
  153.5 30.4 reduce-scatter.42
  186.2 30.2 all-gather.74
  218.7 30.0 reduce-scatter.44
  250.4 28.7 all-gather.76
  281.5 56.7 all-gather.80
  340.5 35.3 all-gather.82
  479.0 27.6 reduce-scatter.28
  539.6 26.8 reduce-scatter.34
  596.3 30.9 reduce-scatter.32
  629.5 31.0 reduce-scatter.30
  663.0 31.1 reduce-scatter.36
  696.4 31.1 reduce-scatter.38
  751.8 126.3 all-reduce.37
  882.4 196.5 all-reduce.51
  1082.6 262.8 all-reduce.39
  1347.1 26.7 all-gather.84
  1375.8 27.6 all-gather.86
  1405.8 28.6 reduce-scatter.48
  1436.9 29.8 reduce-scatter.50
  1469.9 30.4 reduce-scatter.46
  1503.4 31.2 reduce-scatter.52
  1537.9 155.0 reduce-scatter.40
  1825.2 85.2 all-reduce.49
  1913.6 25.5 all-gather.98
  2022.6 87.0 all-reduce.47
  2221.7 87.4 all-reduce.45
  2312.3 25.5 all-gather.102
  2421.4 86.9 all-reduce.43
  2511.5 25.2 all-gather.104
  2620.7 86.7 all-reduce.41
  (7 shorter events, 167.4 us)
where the time goes:
time: 2800 us; the launch traced here: 2780 us
  waiting for transfers between devices  1350 us (48%)
  blocking collectives  677 us (24%)
  local copies, waits for them, and re-layouts  292 us (10%)
  matrix products  286 us (10%)
  other arithmetic  129 us (5%)
  between operations  34.6 us (1%)
    unnamed x48, waiting for transfers between devices  525 us
    psum x5, waiting for transfers between devices, body(): lax.psum((partial_grams[0], partial_grams[1], partial_grams[2], partial_g...  407 us
    all_gather x10, blocking collectives, columns_of(): lax.all_gather(matrices[3], 'wide', axis=1, tiled=True)  155 us
    reduce_scatter x1, waiting for transfers between devices, body(): lax.psum_scatter(totals[4], 'narrow', scatter_dimension=0, tiled=True)  150 us
    all_gather x10, blocking collectives, columns_of(): lax.all_gather(matrices[0], 'wide', axis=1, tiled=True)  131 us
    all_gather x10, blocking collectives, columns_of(): lax.all_gather(matrices[1], 'wide', axis=1, tiled=True)  131 us
    dot_general x20, matrix products, contract(): lax.dot_general(left_side, right_side, (((left_axis,), (right_axis,)), ((...  105 us
    add x4, local copies, waits for them, and re-layouts, body(): earlier_sum + addition  92.8 us
  transfers between devices with their start and end apart: 39, of which 21 were waited for; matrix products, arithmetic and copies ran while one was open for 19% of the time, Pallas kernels for 0%

commit v1 on v0

v1 whole, which is shorter than its diff:
```python
import functools
import math

import jax
import jax.numpy as jnp
from jax import lax
from jax.experimental import pallas as pl
from jax.experimental.pallas import tpu as pltpu
from jax.sharding import PartitionSpec as P

D = 960
H = 15
KVH = 5
HD = 64
FF = 2560
V = 49152
QKV = 1600
ITERS = 5
STEP = 10
MB = 2
SEQ = 1024
ROWS = 128
PICK = 16
DP = 1024

NORM_EPS = 1e-05
ROPE_THETA = 100000.0
SMOOTH = 0.1
ZLOSS_WEIGHT = 0.0001
CLIP_NORM = 0.02
MOMENTUM = 0.95
NS_A = 3.4445
NS_B = -4.775
NS_C = 2.0315
MUON_RATE = 0.1
WEIGHT_DECAY = 0.1
BETA_ONE = 0.9
BETA_TWO = 0.95
TABLE_RATE = 0.03
GAIN_RATE = 0.4
ADAM_EPS = 1e-08
NEGATIVE = -1e30

HIGHEST = lax.Precision.HIGHEST
HIGH = lax.Precision.HIGH
F32 = jnp.float32
BF16 = jnp.bfloat16
MESH = pl.DeviceIdType.MESH
ANY = pl.BlockSpec(memory_space=pl.ANY)
VMEM = pl.BlockSpec(memory_space=pltpu.VMEM)

RI, RO, RG, RD = 112, 64, 320, 160


def my_place():
    wide = lax.axis_index("wide")
    narrow = lax.axis_index("narrow")
    return {
        "y": lax.div(wide, 2),
        "c": lax.rem(wide, 2),
        "z": lax.div(narrow, 4),
        "x": lax.rem(narrow, 4),
    }


def device(place):
    return (place["y"] * 2 + place["c"], place["z"] * 4 + place["x"])


def at_step(place, axis, step):
    return {**place, axis: lax.rem(place[axis] + step, 4)}


def other_core(place):
    return {**place, "c": 1 - place["c"]}


def greet(targets):
    barrier = pltpu.get_barrier_semaphore()
    for target in targets:
        pl.semaphore_signal(barrier, inc=1, device_id=device(target), device_id_type=MESH)
    pl.semaphore_wait(barrier, len(targets))


class Net:
    def __init__(self, send, recv):
        self.send = send
        self.recv = recv
        self.copies = []

    def put(self, src, dst, target):
        k = len(self.copies)
        copy = pltpu.make_async_remote_copy(
            src_ref=src,
            dst_ref=dst,
            send_sem=self.send.at[k],
            recv_sem=self.recv.at[k],
            device_id=device(target),
            device_id_type=MESH,
        )
        copy.start()
        self.copies.append(copy)
        return copy

    def finish(self):
        for copy in self.copies:
            copy.wait_send()


def gather_streams(net, place, streams, with_core):
    states = [{"sel": dict(place), "core": []} for _ in streams]
    phases = max(len(axes) for axes, _ in streams)
    for phase in range(phases):
        last = phase == phases - 1
        for (axes, items), state in zip(streams, states):
            axis = axes[phase]
            up, down = at_step(place, axis, 1), at_step(place, axis, 3)
            state["first"], state["second"] = [], []
            for first_half in (0, 1):
                for region, halves in items:
                    for target, half, way in ((up, first_half, 0), (down, 1 - first_half, 1)):
                        if halves[half] is None:
                            continue
                        ref = region(state["sel"], halves[half])
                        group = "first" if first_half == 0 else "second"
                        state[group].append((net.put(ref, ref, target), way, region, halves[half]))
            if last and with_core:
                for region, halves in items:
                    for half in halves:
                        if half is not None:
                            ref = region(state["sel"], half)
                            state["core"].append(net.put(ref, ref, other_core(place)))
        for (axes, items), state in zip(streams, states):
            axis = axes[phase]
            up, down = at_step(place, axis, 1), at_step(place, axis, 3)
            state["onward"] = []
            for copy, way, region, half in state["first"]:
                copy.wait_recv()
                origin, target = (down, up) if way == 0 else (up, down)
                ref = region({**state["sel"], axis: origin[axis]}, half)
                state["onward"].append((net.put(ref, ref, target), region, half))
                if last and with_core:
                    state["core"].append(net.put(ref, ref, other_core(place)))
        for (axes, items), state in zip(streams, states):
            axis = axes[phase]
            up, down = at_step(place, axis, 1), at_step(place, axis, 3)
            for copy, way, region, half in state["second"]:
                copy.wait_recv()
                if last and with_core:
                    origin = down if way == 0 else up
                    ref = region({**state["sel"], axis: origin[axis]}, half)
                    state["core"].append(net.put(ref, ref, other_core(place)))
        for (axes, items), state in zip(streams, states):
            axis = axes[phase]
            across = at_step(place, axis, 2)
            for copy, region, half in state["onward"]:
                copy.wait_recv()
                if last and with_core:
                    ref = region({**state["sel"], axis: across[axis]}, half)
                    state["core"].append(net.put(ref, ref, other_core(place)))
            state["sel"] = {**state["sel"], axis: None}
    for state in states:
        for copy in state["core"]:
            copy.wait_recv()


def pick(index):
    return slice(None) if index is None else index


def lanes_of(sel):
    if sel["y"] is None:
        return pl.ds(pl.multiple_of(sel["c"] * 512, 512), 512)
    return pl.ds(pl.multiple_of((sel["c"] * 4 + sel["y"]) * 128, 128), 128)


def halved(low, high):
    cut = low + (high - low) // 32 * 16
    return ((low, cut - low), (cut, high - cut))


def neighbours(place, axes=("x", "y", "z"), core=True):
    found = [at_step(place, axis, step) for axis in axes for step in (1, 3)]
    return found + ([other_core(place)] if core else [])


def weights_kernel(gi, go, gg, gd, meta, wi, wo, wg, wd, info, send, recv, local):
    place = my_place()
    greet(neighbours(place))

    def in_wi(sel, rows):
        return wi.at[pick(sel["z"]), pick(sel["x"]), pl.ds(*rows), lanes_of(sel)]

    def in_wo(sel, rows):
        z, x = sel["z"], sel["x"]
        xh, xl = (None, None) if x is None else (lax.div(x, 2), lax.rem(x, 2))
        return wo.at[pick(xh), pick(z), pick(xl), pl.ds(*rows), lanes_of(sel)]

    def in_wg(half):
        def region(sel, rows):
            z, x = sel["z"], sel["x"]
            zh, zl = (None, None) if z is None else (lax.div(z, 2), lax.rem(z, 2))
            return wg.at[pick(zh), half, pick(zl), pick(x), pl.ds(*rows), lanes_of(sel)]

        return region

    def in_wd(sel, rows):
        z, x = sel["z"], sel["x"]
        xh, xl = (None, None) if x is None else (lax.div(x, 2), lax.rem(x, 2))
        return wd.at[pick(xl), pick(z), pick(xh), pl.ds(*rows), lanes_of(sel)]

    def in_info(sel, rows):
        return info.at[pick(sel["z"]), pick(sel["x"]), pick(sel["y"]), sel["c"], :, :]

    owns = [
        (gi, in_wi(place, (0, RI))),
        (go, in_wo(place, (0, RO))),
        (gg.at[pl.ds(0, 160)], in_wg(0)(place, (0, 160))),
        (gg.at[pl.ds(160, 160)], in_wg(1)(place, (0, 160))),
        (gd, in_wd(place, (0, RD))),
        (meta, in_info(place, None)),
    ]
    copies = [pltpu.make_async_copy(src, dst, local.at[k]) for k, (src, dst) in enumerate(owns)]
    for copy in copies:
        copy.start()
    for copy in copies:
        copy.wait()
    streams = [
        (("x", "z", "y"), [(in_wg(0), halved(0, 160)), (in_wo, halved(0, 64))]),
        (("z", "y", "x"), [(in_wg(1), halved(0, 160)), (in_wi, halved(0, 64))]),
        (
            ("y", "x", "z"),
            [(in_wd, halved(0, 160)), (in_wi, halved(64, 112)), (in_info, ((0, 8), None))],
        ),
    ]
    net = Net(send, recv)
    gather_streams(net, place, streams, True)
    net.finish()


def gather_weights(gi, go, gg, gd, meta):
    shapes = [
        jax.ShapeDtypeStruct((4, 4, RI, DP), BF16),
        jax.ShapeDtypeStruct((2, 4, 2, RO, DP), BF16),
        jax.ShapeDtypeStruct((2, 2, 2, 4, 160, DP), BF16),
        jax.ShapeDtypeStruct((2, 4, 2, 160, DP), BF16),
        jax.ShapeDtypeStruct((4, 4, 4, 2, 8, 128), jnp.int32),
    ]
    count = 176
    return pl.pallas_call(
        weights_kernel,
        out_shape=shapes,
        in_specs=[ANY] * 5,
        out_specs=[ANY] * 5,
        scratch_shapes=[
            pltpu.SemaphoreType.DMA((count,)),
            pltpu.SemaphoreType.DMA((count,)),
            pltpu.SemaphoreType.DMA((6,)),
        ],
        compiler_params=pltpu.CompilerParams(collective_id=0, has_side_effects=True),
        name="gather_weights",
    )(gi, go, gg, gd, meta)


LANE_PARTS = ((0, 384), (384, 384), (768, 256))
ORDERS = (("x", "z", "y"), ("z", "y", "x"), ("y", "x", "z"))


def rows_kernel(own, rows, send, recv, local):
    place = my_place()
    greet(neighbours(place))

    def in_rows(lanes):
        def region(sel, part):
            return rows.at[
                pick(sel["z"]), pick(sel["x"]), pick(sel["y"]), sel["c"], pl.ds(*part), pl.ds(*lanes)
            ]

        return region

    copy = pltpu.make_async_copy(
        own, rows.at[place["z"], place["x"], place["y"], place["c"]], local
    )
    copy.start()
    copy.wait()
    streams = [
        (axes, [(in_rows(lanes), ((0, 16), (16, 16)))]) for axes, lanes in zip(ORDERS, LANE_PARTS)
    ]
    net = Net(send, recv)
    gather_streams(net, place, streams, True)
    net.finish()


def gather_rows(own):
    count = 90
    return pl.pallas_call(
        rows_kernel,
        out_shape=jax.ShapeDtypeStruct((4, 4, 4, 2, 32, DP), BF16),
        in_specs=[ANY],
        out_specs=ANY,
        scratch_shapes=[
            pltpu.SemaphoreType.DMA((count,)),
            pltpu.SemaphoreType.DMA((count,)),
            pltpu.SemaphoreType.DMA,
        ],
        compiler_params=pltpu.CompilerParams(collective_id=1, has_side_effects=True),
        name="gather_rows",
    )(own)


HOPS = (("c", 2), ("x", 4), ("y", 4), ("z", 4))


def small_kernel(combine, last, own, out, held, slots, send, recv):
    place = my_place()
    peers = [other_core(place)] + [
        at_step(place, axis, step) for axis, _ in HOPS[1:] for step in (1, 2, 3)
    ]
    greet(peers)
    held[0] = own[...]
    net = Net(send, recv)
    for hop, (axis, size) in enumerate(HOPS):
        targets = (
            [other_core(place)]
            if axis == "c"
            else [at_step(place, axis, step) for step in (1, 2, 3)]
        )
        copies = [net.put(held.at[hop], slots.at[hop, place[axis]], target) for target in targets]
        slots[hop, place[axis]] = held[hop]
        for copy in copies:
            copy.wait_recv()
        total = slots[hop, 0]
        for index in range(1, size):
            total = combine(total, slots[hop, index])
        held[hop + 1] = total
    out[...] = last(held[len(HOPS)])
    net.finish()


def small_all(value, combine, last, out_shape, collective_id, name):
    shape = value.shape
    count = 10
    return pl.pallas_call(
        functools.partial(small_kernel, combine, last),
        out_shape=jax.ShapeDtypeStruct(out_shape, F32),
        in_specs=[VMEM],
        out_specs=VMEM,
        scratch_shapes=[
            pltpu.VMEM((len(HOPS) + 1,) + shape, F32),
            pltpu.VMEM((len(HOPS), 4) + shape, F32),
            pltpu.SemaphoreType.DMA((count,)),
            pltpu.SemaphoreType.DMA((count,)),
        ],
        compiler_params=pltpu.CompilerParams(collective_id=collective_id, has_side_effects=True),
        name=name,
    )(value)


def combine_stats(one, two):
    highest = jnp.maximum(one[0], two[0])
    total = one[1] * jnp.exp(one[0] - highest) + two[1] * jnp.exp(two[0] - highest)
    return jnp.stack([highest, total])


def log_of_stats(stats):
    return stats[0] + jnp.log(stats[1])


def add_up(dst, index, parts):
    total = parts[0][...].astype(F32)
    for part in parts[1:]:
        total = total + part[...].astype(F32)
    dst[index] = total.astype(dst.dtype)


def scatter_sum(net, place, orders, sources, works, outs):
    def block(ref, sel, rows):
        return ref.at[pick(sel["z"]), pick(sel["x"]), pick(sel["y"]), pl.ds(*rows)]

    jobs = []
    for order, source, work, out in zip(orders, sources, works, outs):
        rows = source.shape[3] // 2
        jobs.append(
            {
                "order": order,
                "source": source,
                "work": work,
                "out": out,
                "halves": ((0, rows), (rows, rows)),
                "steps": [
                    [at_step(place, axis, step) for step in range(4)] for axis in order
                ],
            }
        )

    def everywhere():
        return {"z": None, "x": None, "y": None}

    def first_view(job, one, two, half):
        a, b, _ = job["order"]
        sel = {**everywhere(), a: one, b: two}
        return block(job["source"], sel, job["halves"][half])

    sequence = (2, 1, 3, 0)
    for sub, far in enumerate(sequence):
        for job in jobs:
            a, b, _ = job["order"]
            own = job["steps"][0]
            two = job["steps"][1][far][b]
            got = job["work"]["got1"]
            job.setdefault("c1", []).append(
                {
                    "ra": net.put(first_view(job, own[2][a], two, 0), got.at[sub, 0], own[1]),
                    "rb": net.put(first_view(job, own[2][a], two, 1), got.at[sub, 1], own[3]),
                }
            )
    for sub, far in enumerate(sequence):
        for job in jobs:
            a, b, _ = job["order"]
            own = job["steps"][0]
            two = job["steps"][1][far][b]
            got = job["work"]["got1"]
            copies = job["c1"][sub]
            copies["p1"] = net.put(first_view(job, own[1][a], two, 1), got.at[sub, 2], own[1])
            copies["m0"] = net.put(first_view(job, own[3][a], two, 0), got.at[sub, 3], own[3])
    for sub, far in enumerate(sequence):
        for job in jobs:
            a, b, _ = job["order"]
            own = job["steps"][0]
            two = job["steps"][1][far][b]
            got, mid = job["work"]["got1"], job["work"]["mid1"]
            copies = job["c1"][sub]
            copies["ra"].wait_recv()
            add_up(mid, (sub, 0), [first_view(job, own[1][a], two, 0), got.at[sub, 0]])
            copies["p0"] = net.put(mid.at[sub, 0], got.at[sub, 4], own[1])
            copies["rb"].wait_recv()
            add_up(mid, (sub, 1), [first_view(job, own[3][a], two, 1), got.at[sub, 1]])
            copies["m1"] = net.put(mid.at[sub, 1], got.at[sub, 5], own[3])
    def second_view(job, two, half):
        return job["work"]["acc1"].at[two, :, pl.ds(*job["halves"][half])]

    for sub, far in enumerate(sequence):
        for job in jobs:
            a, b, _ = job["order"]
            own = job["steps"][0]
            next_own = job["steps"][1]
            two = next_own[far][b]
            got = job["work"]["got1"]
            copies = job["c1"][sub]
            for name in ("p1", "m0", "p0", "m1"):
                copies[name].wait_recv()
            acc = job["work"]["acc1"]
            for half, (one, other) in enumerate(((4, 3), (2, 5))):
                add_up(
                    acc,
                    (two, slice(None), pl.ds(*job["halves"][half])),
                    [first_view(job, own[0][a], two, half), got.at[sub, one], got.at[sub, other]],
                )
            got2 = job["work"]["got2"]
            if far == 2:
                job["c2"] = {
                    "ra": net.put(second_view(job, two, 0), got2.at[0], next_own[1]),
                    "rb": net.put(second_view(job, two, 1), got2.at[1], next_own[3]),
                }
            if far == 1:
                job["c2"]["p1"] = net.put(second_view(job, two, 1), got2.at[2], next_own[1])
            if far == 3:
                job["c2"]["m0"] = net.put(second_view(job, two, 0), got2.at[3], next_own[3])
    for job in jobs:
        b = job["order"][1]
        own = job["steps"][1]
        got, mid, copies = job["work"]["got2"], job["work"]["mid2"], job["c2"]
        copies["ra"].wait_recv()
        add_up(mid, 0, [second_view(job, own[1][b], 0), got.at[0]])
        copies["p0"] = net.put(mid.at[0], got.at[4], own[1])
        copies["rb"].wait_recv()
        add_up(mid, 1, [second_view(job, own[3][b], 1), got.at[1]])
        copies["m1"] = net.put(mid.at[1], got.at[5], own[3])

    def third_view(job, three, half):
        return job["work"]["acc2"].at[three, pl.ds(*job["halves"][half])]

    for job in jobs:
        b = job["order"][1]
        own = job["steps"][1]
        got, acc, copies = job["work"]["got2"], job["work"]["acc2"], job["c2"]
        for name in ("p1", "m0", "p0", "m1"):
            copies[name].wait_recv()
        for half, (one, other) in enumerate(((4, 3), (2, 5))):
            add_up(
                acc,
                (slice(None), pl.ds(*job["halves"][half])),
                [second_view(job, own[0][b], half), got.at[one], got.at[other]],
            )
        third = job["order"][2]
        own = job["steps"][2]
        got = job["work"]["got3"]
        job["c3"] = {
            "ra": net.put(third_view(job, own[2][third], 0), got.at[0], own[1]),
            "rb": net.put(third_view(job, own[2][third], 1), got.at[1], own[3]),
            "p1": net.put(third_view(job, own[1][third], 1), got.at[2], own[1]),
            "m0": net.put(third_view(job, own[3][third], 0), got.at[3], own[3]),
        }
    for job in jobs:
        third = job["order"][2]
        own = job["steps"][2]
        got, mid, copies = job["work"]["got3"], job["work"]["mid3"], job["c3"]
        copies["ra"].wait_recv()
        add_up(mid, 0, [third_view(job, own[1][third], 0), got.at[0]])
        copies["p0"] = net.put(mid.at[0], got.at[4], own[1])
        copies["rb"].wait_recv()
        add_up(mid, 1, [third_view(job, own[3][third], 1), got.at[1]])
        copies["m1"] = net.put(mid.at[1], got.at[5], own[3])
    for job in jobs:
        third = job["order"][2]
        own = job["steps"][2]
        got, copies = job["work"]["got3"], job["c3"]
        for name in ("p1", "m0", "p0", "m1"):
            copies[name].wait_recv()
        for half, (one, other) in enumerate(((4, 3), (2, 5))):
            add_up(
                job["out"],
                (pl.ds(*job["halves"][half]),),
                [third_view(job, own[0][third], half), got.at[one], got.at[other]],
            )


WORK_NAMES = ("got1", "mid1", "acc1", "got2", "mid2", "acc2", "got3", "mid3")


def work_shapes(rows, lanes, first, later):
    half = rows // 2
    return [
        pltpu.VMEM((4, 6, 4, half, lanes), first),
        pltpu.VMEM((4, 2, 4, half, lanes), first),
        pltpu.VMEM((4, 4, rows, lanes), later),
        pltpu.VMEM((6, 4, half, lanes), later),
        pltpu.VMEM((2, 4, half, lanes), later),
        pltpu.VMEM((4, rows, lanes), later),
        pltpu.VMEM((6, half, lanes), later),
        pltpu.VMEM((2, half, lanes), later),
    ]


SUM_COPIES = 3 * (24 + 6 + 6)


def grads_kernel(di, do, dg, dd, out, *scratch):
    held = scratch[0:3]
    works = [dict(zip(WORK_NAMES, scratch[3 + 8 * k : 11 + 8 * k])) for k in range(3)]
    send, recv, local = scratch[27:]
    place = my_place()
    moves = []
    for y in range(4):
        lanes = pl.ds(y * 128, 128)
        for z in range(4):
            for half in range(2):
                moves.append(
                    (
                        dg.at[z // 2, half, z % 2, :, :, lanes],
                        held[half].at[z, :, y, pl.ds(0, 160)],
                    )
                )
        for x in range(4):
            moves.append((dd.at[x % 2, :, x // 2, :, lanes], held[2].at[:, x, y, pl.ds(0, 160)]))
            moves.append((do.at[x // 2, :, x % 2, :, lanes], held[0].at[:, x, y, pl.ds(160, 64)]))
        for z in range(4):
            moves.append(
                (di.at[z, :, pl.ds(0, 64), lanes], held[1].at[z, :, y, pl.ds(160, 64)])
            )
            moves.append(
                (di.at[z, :, pl.ds(64, 48), lanes], held[2].at[z, :, y, pl.ds(160, 48)])
            )
    copies = [pltpu.make_async_copy(src, dst, local.at[k]) for k, (src, dst) in enumerate(moves)]
    for copy in copies:
        copy.start()
    held[2][:, :, :, 208:224, :] = jnp.zeros((4, 4, 4, 16, 128), held[2].dtype)
    greet(neighbours(place, core=False))
    for copy in copies:
        copy.wait()
    net = Net(send, recv)
    scatter_sum(net, place, ORDERS, held, works, [out.at[k] for k in range(3)])
    net.finish()


def scatter_grads(di, do, dg, dd, first, later):
    rows, lanes = 224, 128
    scratch = [pltpu.VMEM((4, 4, 4, rows, lanes), first)] * 3
    for _ in range(3):
        scratch += work_shapes(rows, lanes, first, later)
    scratch += [
        pltpu.SemaphoreType.DMA((SUM_COPIES,)),
        pltpu.SemaphoreType.DMA((SUM_COPIES,)),
        pltpu.SemaphoreType.DMA((96,)),
    ]
    return pl.pallas_call(
        grads_kernel,
        out_shape=jax.ShapeDtypeStruct((3, rows, lanes), F32),
        in_specs=[ANY] * 4,
        out_specs=VMEM,
        scratch_shapes=scratch,
        compiler_params=pltpu.CompilerParams(
            collective_id=2, has_side_effects=True, vmem_limit_bytes=56 << 20
        ),
        name="scatter_grads",
    )(di, do, dg, dd)


def row_sums_kernel(part, out, *scratch):
    held = scratch[0:3]
    works = [dict(zip(WORK_NAMES, scratch[3 + 8 * k : 11 + 8 * k])) for k in range(3)]
    send, recv, local = scratch[27:]
    place = my_place()
    copies = [
        pltpu.make_async_copy(part.at[:, :, :, :, pl.ds(*lanes)], held[k], local.at[k])
        for k, lanes in enumerate(LANE_PARTS)
    ]
    for copy in copies:
        copy.start()
    greet(neighbours(place, core=False))
    for copy in copies:
        copy.wait()
    net = Net(send, recv)
    outs = [out.at[:, pl.ds(*lanes)] for lanes in LANE_PARTS]
    scatter_sum(net, place, ORDERS, held, works, outs)
    net.finish()


def scatter_rows(part, first, later):
    scratch = [pltpu.VMEM((4, 4, 4, 32, lanes), first) for _, lanes in LANE_PARTS]
    for _, lanes in LANE_PARTS:
        scratch += work_shapes(32, lanes, first, later)
    scratch += [
        pltpu.SemaphoreType.DMA((SUM_COPIES,)),
        pltpu.SemaphoreType.DMA((SUM_COPIES,)),
        pltpu.SemaphoreType.DMA((3,)),
    ]
    return pl.pallas_call(
        row_sums_kernel,
        out_shape=jax.ShapeDtypeStruct((32, DP), F32),
        in_specs=[ANY],
        out_specs=VMEM,
        scratch_shapes=scratch,
        compiler_params=pltpu.CompilerParams(
            collective_id=3, has_side_effects=True, vmem_limit_bytes=56 << 20
        ),
        name="scatter_rows",
    )(part)


def pad_features(values):
    lead = values.shape[:-1]
    blocks = values.reshape(lead + (4, 2, 2, 60))
    blocks = jnp.moveaxis(blocks, -3, -4)
    blocks = jnp.pad(blocks, [(0, 0)] * (len(lead) + 3) + [(0, 4)])
    return blocks.reshape(lead + (DP,))


def feature_table():
    feature = lax.broadcasted_iota(jnp.int32, (D, DP), 0)
    place = lax.broadcasted_iota(jnp.int32, (D, DP), 1)
    wide, rest = feature // 120, feature % 120
    where = ((wide % 2) * 4 + wide // 2) * 128 + (rest // 60) * 64 + rest % 60
    return (where == place).astype(BF16)


def column_table():
    column = lax.broadcasted_iota(jnp.int32, (QKV, 16 * RI), 0)
    place = lax.broadcasted_iota(jnp.int32, (QKV, 16 * RI), 1)
    return ((column // 100) * RI + column % 100 == place).astype(BF16)


def to_shard(matrix, rows):
    columns = matrix.shape[1]
    turned = matrix.T.reshape(columns, 2, 60)
    turned = jnp.pad(turned, ((0, rows - columns), (0, 0), (0, 4)))
    return turned.reshape(rows, 128)


def from_shard(shard, columns):
    return shard[:columns].reshape(columns, 2, 64)[:, :, :60].reshape(columns, 120).T


def dot(left, right, left_axis, right_axis, precision=None):
    return lax.dot_general(
        left,
        right,
        (((left_axis,), (right_axis,)), ((), ())),
        preferred_element_type=F32,
        precision=precision,
    )


def rms_norm(values, gain_row):
    mean = jnp.sum(values * values, axis=-1, keepdims=True) * (1.0 / D)
    return values * lax.rsqrt(mean + NORM_EPS) * gain_row


def rotate(values, places):
    half_width = HD // 2
    frequency = ROPE_THETA ** (-2.0 * jnp.arange(half_width).astype(F32) / HD)
    angles = places.astype(F32)[:, None] * frequency[None, :]
    cosine = jnp.concatenate([jnp.cos(angles), jnp.cos(angles)], axis=-1)[:, None, :]
    sine_part = jnp.concatenate([jnp.sin(angles), jnp.sin(angles)], axis=-1)[:, None, :]
    turned = jnp.concatenate([-values[..., half_width:], values[..., :half_width]], axis=-1)
    return values * cosine + turned * sine_part


def gated(gate_up):
    return gate_up[:, :FF] * jax.nn.sigmoid(gate_up[:, :FF]) * gate_up[:, FF:]


def adam_update(weight, first_moment, second_moment, gradient, step_rate, decay_rate):
    first_new = BETA_ONE * first_moment + (1.0 - BETA_ONE) * gradient
    second_new = BETA_TWO * second_moment + (1.0 - BETA_TWO) * gradient * gradient
    update = (
        first_new
        / (1.0 - BETA_ONE**STEP)
        / (jnp.sqrt(second_new / (1.0 - BETA_TWO**STEP)) + ADAM_EPS)
    )
    return (first_new, second_new, weight * (1.0 - step_rate * decay_rate) - step_rate * update)


def partner(value):
    return lax.ppermute(value, "wide", [(k, k ^ 1) for k in range(8)])


def body(
    token_ids,
    target_ids,
    prefix_lengths,
    loss_positions,
    w_input,
    w_output,
    w_gate_up,
    w_down,
    norm_gains,
    embed_table,
    moment_input,
    moment_output,
    moment_gate_up,
    moment_down,
    table_first,
    table_second,
    gains_first,
    gains_second,
):
    wide = lax.axis_index("wide")
    narrow = lax.axis_index("narrow")
    core = wide % 2
    masters = (w_input[0], w_output[0], w_gate_up[0], w_down[0])
    moments = (moment_input[0], moment_output[0], moment_gate_up[0], moment_down[0])
    group_size = H // KVH
    kv_width = KVH * HD
    scale_factor = HD ** (-0.5)
    features = feature_table()
    columns = column_table()
    gains = pad_features(norm_gains)
    own_places = wide * ROWS + jnp.arange(ROWS)
    key_places = jnp.arange(SEQ)
    tokens = token_ids[:, 0]
    targets = target_ids[:, 0]
    prefixes = prefix_lengths[:, 0]
    positions = loss_positions[:, 0]

    own_positions = lax.dynamic_slice_in_dim(positions, wide * PICK, PICK, axis=1)
    own_targets = jnp.take_along_axis(targets, own_positions, axis=1).reshape(MB * PICK)
    own_counted = (own_positions >= prefixes[:, None]).astype(jnp.int32).reshape(MB * PICK)
    meta = jnp.pad(jnp.stack([own_targets, own_counted]), ((0, 6), (0, 128 - MB * PICK)))

    table_low = dot(embed_table.astype(BF16), features, 1, 0).astype(BF16)
    slab = lax.all_gather(table_low, "narrow", axis=0, tiled=True)
    table_other = partner(table_low)

    shards = [
        to_shard(master.astype(BF16), rows) for master, rows in zip(masters, (RI, RO, RG, RD))
    ]
    wi, wo, wg, wd, info = gather_weights(*shards, meta)
    wi = wi.reshape(16, RI, DP)[:, :100].reshape(QKV, DP)
    wo = wo.reshape(DP, DP)
    wg = wg.reshape(2 * FF, DP)
    wd = wd.reshape(FF, DP)
    info = info.reshape(128, 8, 128)
    all_targets = info[:, 0, : MB * PICK].reshape(4096)
    all_counted = info[:, 1, : MB * PICK].reshape(4096).astype(F32)

    slab_rows = slab.shape[0]
    ordered = tokens.reshape(MB, 8, ROWS).swapaxes(0, 1).reshape(2048)
    local_ids = ordered - wide * slab_rows
    inside = (local_ids >= 0) & (local_ids < slab_rows)
    safe_ids = jnp.clip(local_ids, 0, slab_rows - 1)
    looked_up = jnp.where(inside[:, None], slab[safe_ids], jnp.zeros((), BF16))
    x0 = lax.psum_scatter(looked_up, "wide", scatter_dimension=0, tiled=True).astype(F32)

    a = rms_norm(x0, gains[0]).astype(BF16)
    projected = dot(a, wi, 1, 1)
    places_all = jnp.concatenate([own_places, own_places])
    rows_count = MB * ROWS
    query = rotate(projected[:, : H * HD].reshape(rows_count, H, HD), places_all).astype(BF16)
    key_own = rotate(
        projected[:, H * HD : H * HD + kv_width].reshape(rows_count, KVH, HD), places_all
    ).astype(BF16)
    value_own = projected[:, H * HD + kv_width :].astype(BF16)
    kv_own = jnp.concatenate([key_own.reshape(rows_count, kv_width), value_own], axis=1)
    kv_all = lax.all_gather(kv_own, "wide", axis=0, tiled=False)
    kv_all = kv_all.reshape(8, MB, ROWS, 2 * kv_width)

    def allowed_of(batch):
        return (key_places[None, :] <= own_places[:, None]) | (
            key_places[None, :] < prefixes[batch]
        )

    kept = []
    mixed_parts = []
    for batch in range(MB):
        q = query.reshape(MB, ROWS, KVH, group_size, HD)[batch]
        k = kv_all[:, batch, :, :kv_width].reshape(SEQ, KVH, HD)
        v = kv_all[:, batch, :, kv_width:].reshape(SEQ, KVH, HD)
        scores = jnp.einsum("qkgd,tkd->kgqt", q, k, preferred_element_type=F32) * scale_factor
        scores = jnp.where(allowed_of(batch), scores, NEGATIVE)
        highest = jnp.max(scores, axis=-1, keepdims=True)
        exp_part = jnp.exp(scores - highest)
        exp_total = jnp.sum(exp_part, axis=-1, keepdims=True)
        log_total = highest + jnp.log(exp_total)
        probs = (exp_part / exp_total).astype(BF16)
        mixed = jnp.einsum("kgqt,tkd->qkgd", probs, v, preferred_element_type=F32)
        mixed_parts.append(mixed.reshape(ROWS, H * HD).astype(BF16))
        kept.append((q, k, v, log_total))
    o_pad = dot(jnp.concatenate(mixed_parts), features, 1, 0).astype(BF16)
    x1 = x0 + dot(o_pad, wo, 1, 1)

    b = rms_norm(x1, gains[1]).astype(BF16)
    gate_up = dot(b, wg, 1, 1)
    activated = gated(gate_up).astype(BF16)
    x2 = x1 + dot(activated, wd, 1, 0)

    final = rms_norm(x2, gains[2]).astype(BF16)
    own_offsets = (own_positions - wide * ROWS + jnp.arange(MB)[:, None] * ROWS).reshape(-1)
    all_rows = gather_rows(final[own_offsets]).reshape(4096, DP)
    logits = dot(all_rows, table_low, 1, 1)
    vocab_start = (wide * 16 + narrow) * 384
    hit = jnp.arange(384)[None, :] == (all_targets - vocab_start)[:, None]
    highest = jnp.max(logits, axis=-1)
    exp_total = jnp.sum(jnp.exp(logits - highest[:, None]), axis=-1)
    stats = jnp.stack([highest.reshape(32, 128), exp_total.reshape(32, 128)])
    log_total = small_all(stats, combine_stats, log_of_stats, (32, 128), 4, "row_totals")
    log_total = log_total.reshape(4096)
    hit_sum = jnp.sum(jnp.where(hit, logits, 0.0) * all_counted[:, None])
    logit_sum = jnp.sum(logits * all_counted[:, None])
    token_count = jnp.sum(all_counted)
    loss_known = jnp.sum(all_counted * (log_total + ZLOSS_WEIGHT * log_total * log_total))
    d_logits = (
        all_counted[:, None]
        * (
            (1.0 + 2.0 * ZLOSS_WEIGHT * log_total)[:, None] * jnp.exp(logits - log_total[:, None])
            - (1.0 - SMOOTH) * hit.astype(F32)
            - SMOOTH / V
        )
    ).astype(BF16)
    table_grad_rows = dot(d_logits, all_rows, 0, 0)
    d_by_core = d_logits.reshape(64, 2, 32, 384)
    d_mine = lax.dynamic_index_in_dim(d_by_core, core, 1, keepdims=False).reshape(2048, 384)
    d_theirs = lax.dynamic_index_in_dim(d_by_core, 1 - core, 1, keepdims=False).reshape(2048, 384)
    d_theirs = partner(d_theirs)
    row_part = dot(d_mine, table_low, 1, 0) + dot(d_theirs, table_other, 1, 0)
    d_rows = scatter_rows(row_part.reshape(4, 4, 4, 32, DP), F32, F32)

    d_final = jnp.zeros((rows_count, DP), F32).at[own_offsets].add(d_rows)
    d_x2, d_gain_final = jax.vjp(rms_norm, x2, gains[2])[1](d_final)
    d_branch = d_x2.astype(BF16)
    d_activated = dot(d_branch, wd, 1, 1)
    d_gate_up = jax.vjp(gated, gate_up)[1](d_activated)[0].astype(BF16)
    d_b = dot(d_gate_up, wg, 1, 0)
    d_x1_part, d_gain_mlp = jax.vjp(rms_norm, x1, gains[1])[1](d_b)
    d_x1 = d_x2 + d_x1_part
    d_out = d_x1.astype(BF16)
    d_mixed_pad = dot(d_out, wo, 1, 0).astype(BF16)
    d_mixed = dot(d_mixed_pad, features, 1, 1).astype(BF16)
    d_queries, d_kv = [], []
    for batch in range(MB):
        q, k, v, log_sum = kept[batch]
        d_m = d_mixed.reshape(MB, ROWS, KVH, group_size, HD)[batch]
        scores = jnp.einsum("qkgd,tkd->kgqt", q, k, preferred_element_type=F32) * scale_factor
        scores = jnp.where(allowed_of(batch), scores, NEGATIVE)
        probs = jnp.exp(scores - log_sum)
        d_probs = jnp.einsum("qkgd,tkd->kgqt", d_m, v, preferred_element_type=F32)
        d_scores = (
            probs * (d_probs - jnp.sum(probs * d_probs, axis=-1, keepdims=True))
        ).astype(BF16)
        d_q = jnp.einsum("kgqt,tkd->qkgd", d_scores, k, preferred_element_type=F32) * scale_factor
        d_k = jnp.einsum("kgqt,qkgd->tkd", d_scores, q, preferred_element_type=F32) * scale_factor
        d_v = jnp.einsum(
            "kgqt,qkgd->tkd", probs.astype(BF16), d_m, preferred_element_type=F32
        )
        d_queries.append(d_q.reshape(ROWS, H, HD))
        d_kv.append(
            jnp.concatenate(
                [d_k.reshape(8, ROWS, kv_width), d_v.reshape(8, ROWS, kv_width)], axis=2
            )
        )
    d_kv_all = jnp.stack(d_kv, axis=1).reshape(8 * rows_count, 2 * kv_width)
    d_kv_own = lax.psum_scatter(d_kv_all, "wide", scatter_dimension=0, tiled=True)

    def unrotate(gradient, heads):
        primal = jnp.zeros((rows_count, heads, HD), F32)
        return jax.vjp(lambda values: rotate(values, places_all), primal)[1](gradient)[0]

    d_projected = jnp.concatenate(
        [
            unrotate(jnp.concatenate(d_queries), H).reshape(rows_count, H * HD),
            unrotate(d_kv_own[:, :kv_width].reshape(rows_count, KVH, HD), KVH).reshape(
                rows_count, kv_width
            ),
            d_kv_own[:, kv_width:],
        ],
        axis=1,
    ).astype(BF16)
    d_a = dot(d_projected, wi, 1, 0)
    d_x0_part, d_gain_attn = jax.vjp(rms_norm, x0, gains[0])[1](d_a)
    d_x0 = (d_x1 + d_x0_part).astype(BF16)

    def half_pair(value):
        mine = lax.dynamic_slice_in_dim(value, core * 512, 512, axis=1)
        theirs = lax.dynamic_slice_in_dim(value, (1 - core) * 512, 512, axis=1)
        return jnp.concatenate([mine, partner(theirs)])

    def both(value):
        return jnp.concatenate([value, partner(value)])

    d_projected_pad = dot(d_projected, columns, 1, 0).astype(BF16)
    grad_wd = dot(both(activated), half_pair(d_branch), 0, 0).astype(BF16)
    grad_wg = dot(both(d_gate_up), half_pair(b), 0, 0).astype(BF16)
    grad_wo = dot(both(d_out), half_pair(o_pad), 0, 0).astype(BF16)
    grad_wi = dot(both(d_projected_pad), half_pair(a), 0, 0).astype(BF16)
    summed_grads = scatter_grads(
        grad_wi.reshape(4, 4, RI, 512),
        grad_wo.reshape(2, 4, 2, RO, 512),
        grad_wg.reshape(2, 2, 2, 4, 160, 512),
        grad_wd.reshape(2, 4, 2, 160, 512),
        BF16,
        F32,
    )
    grad_shards = (
        jnp.concatenate([summed_grads[1, 160:224], summed_grads[2, 160:208]]),
        summed_grads[0, 160:224],
        jnp.concatenate([summed_grads[0, :160], summed_grads[1, :160]]),
        summed_grads[2, :160],
    )

    d_embed = lax.all_gather(d_x0, "wide", axis=0, tiled=True)
    onehot = (
        lax.broadcasted_iota(jnp.int32, (slab_rows, 2048), 0) == local_ids[None, :]
    ).astype(BF16)
    table_grad = lax.psum_scatter(
        dot(onehot, d_embed, 1, 0), "narrow", scatter_dimension=0, tiled=True
    )
    table_grad = dot(table_grad + table_grad_rows, features, 1, 1, HIGHEST)

    squares = sum(jnp.sum(shard * shard) for shard in grad_shards) + jnp.sum(
        table_grad * table_grad
    )
    gain_grads = jnp.stack([d_gain_attn, d_gain_mlp, d_gain_final]).reshape(24, 128)
    scalars = jnp.pad(jnp.stack([squares, hit_sum, logit_sum]), (0, 125))
    packed = jnp.pad(jnp.concatenate([gain_grads, scalars[None]]), ((0, 7), (0, 0)))
    summed = small_all(packed, jnp.add, lambda v: v, (32, 128), 5, "global_sums")
    gain_grad = dot(summed[:24].reshape(3, DP), features, 1, 1, HIGHEST)
    loss_total = loss_known - (1.0 - SMOOTH) * summed[24, 1] - SMOOTH / V * summed[24, 2]
    grad_norm = jnp.sqrt(summed[24, 0] + jnp.sum(gain_grad * gain_grad)) / token_count
    factor = jnp.minimum(1.0, CLIP_NORM / grad_norm) / token_count

    new_shards = [
        MOMENTUM * to_shard(moment, rows) + factor * grad
        for moment, rows, grad in zip(moments, (RI, RO, RG, RD), grad_shards)
    ]
    pieces = jnp.stack(
        [
            jnp.pad(part, ((0, 160 - part.shape[0]), (0, 0)))
            for shard in new_shards
            for part in jnp.split(shard, 2)
        ]
    )
    pieces = lax.all_to_all(pieces, "wide", split_axis=0, concat_axis=0)
    turned = pieces.reshape(4, 2, 160, 128).transpose(2, 1, 0, 3).reshape(160, DP)
    gram = dot(turned, turned, 0, 0, HIGHEST)
    gram = lax.psum(gram + partner(gram), "narrow")
    norm = jnp.sqrt(jnp.trace(gram)) + 1e-07
    current = turned / norm
    gram = gram / norm / norm
    identity = jnp.eye(DP, dtype=F32)
    for ns_step in range(ITERS):
        if ns_step < ITERS - 1:
            square = dot(gram, gram, 1, 0, HIGH)
            step_matrix = NS_A * identity + NS_B * gram + NS_C * square
            current = dot(current, step_matrix, 1, 0, HIGH)
            gram = dot(dot(step_matrix, gram, 1, 0, HIGH), step_matrix, 1, 0, HIGH)
        else:
            applied = dot(current, gram, 1, 0, HIGH)
            current = NS_A * current + NS_B * applied + NS_C * dot(applied, gram, 1, 0, HIGH)
    pieces = current.reshape(160, 2, 4, 128).transpose(2, 1, 0, 3).reshape(8, 160, 128)
    pieces = lax.all_to_all(pieces, "wide", split_axis=0, concat_axis=0)
    new_moments, new_weights = [], []
    for kind, rows in enumerate((RI, RO, RG, RD)):
        count = masters[kind].shape[1]
        ortho = jnp.concatenate([pieces[2 * kind, : rows // 2], pieces[2 * kind + 1, : rows // 2]])
        new_moments.append(from_shard(new_shards[kind], count)[None])
        new_weights.append(
            (
                masters[kind] * (1.0 - MUON_RATE * WEIGHT_DECAY)
                - MUON_RATE * 0.2 * math.sqrt(count * 16) * from_shard(ortho, count)
            )[None]
        )
    table_m, table_v, table_new = adam_update(
        embed_table, table_first, table_second, factor * table_grad, TABLE_RATE, WEIGHT_DECAY
    )
    gains_m, gains_v, gains_new = adam_update(
        norm_gains, gains_first, gains_second, factor * gain_grad, GAIN_RATE, 0.0
    )
    return (
        loss_total,
        token_count,
        grad_norm,
        *new_moments,
        *new_weights,
        *[weight.astype(BF16) for weight in new_weights],
        table_m,
        table_v,
        table_new,
        table_new.astype(BF16),
        gains_m,
        gains_v,
        gains_new,
    )


def solution(mesh):
    whole = P()
    by_sequence = P(None, "narrow", None)
    matrix = P(None, "wide", "narrow")
    table = P(("wide", "narrow"), None)
    return jax.shard_map(
        body,
        mesh=mesh,
        in_specs=(
            (by_sequence, by_sequence, P(None, "narrow"), by_sequence)
            + (matrix,) * 4
            + (whole, table)
            + (matrix,) * 4
            + (table, table, whole, whole)
        ),
        out_specs=(whole,) * 3 + (matrix,) * 12 + (table,) * 4 + (whole,) * 3,
        check_vma=False,
    )
```

time: 2800 us -> 1170 us (0.42)
  waiting for transfers between devices: 1350 us -> 329 us
  blocking collectives: 677 us -> 15.7 us
  Pallas kernels: 0 us -> 301 us
  local copies, waits for them, and re-layouts: 292 us -> 136 us
  other arithmetic: 129 us -> 79.4 us
  matrix products: 286 us -> 258 us
    all_gather x45 -> x0, blocking collectives: 612 us -> none  [the longest x10 155 us: columns_of(): lax.all_gather(matrices[3], 'wide', axis=1, tiled=True)]
    unnamed x48 -> x7, waiting for transfers between devices: 525 us -> 0.11 us
    psum x5 -> x1, waiting for transfers between devices: 407 us -> 96.3 us  [body(): gram = lax.psum(gram + partner(gram), 'narrow')]
    pallas_call x0 -> x6, Pallas kernels: none -> 301 us  [the longest x1 113 us: scatter_grads(): pl.pallas_call(grads_kernel, out_shape=jax.ShapeDtypeStruct((3, rows, lan...]
    reduce_scatter x7 -> x3, waiting for transfers between devices: 247 us -> 64.7 us  [the longest x1 33.4 us: body(): lax.psum_scatter(dot(onehot, d_embed, 1, 0), 'narrow', scatter_dimension=...]
    add x20 -> x2, local copies, waits for them, and re-layouts: 97.2 us -> 0.15 us  [body(): own_positions - wide * ROWS + jnp.arange(MB)[:, None] * ROWS]
    psum x1 -> x0, blocking collectives: 65 us -> none  [body(): lax.psum((grad_squares, cross_terms, moment_squares, table_squares, gain_...]
    unnamed x523 -> x242, local copies, waits for them, and re-layouts: 68 us -> 25.2 us
  transfers between devices with their start and end apart: 39 -> 19, of which waited for: 21 -> 8; matrix products, arithmetic and copies ran while one was open for 19% -> 7% of each run, Pallas kernels for 0% -> 16%
where the time goes in v1:
time: 1170 us; the launch traced here: 1160 us
  waiting for transfers between devices  329 us (28%)
  Pallas kernels  301 us (26%)
  matrix products  258 us (22%)
  local copies, waits for them, and re-layouts  136 us (12%)
  other arithmetic  79.4 us (7%)
  between operations  28.5 us (2%)
  blocking collectives  15.7 us (1%)
  starting transfers between devices  13.1 us (1%)
    dot_general x41, matrix products, dot(): lax.dot_general(left, right, (((left_axis,), (right_axis,)), ((), ())), p...  227 us
    pallas_call x1, Pallas kernels, scatter_grads(): pl.pallas_call(grads_kernel, out_shape=jax.ShapeDtypeStruct((3, rows, lan...  113 us
    all_gather x1, waiting for transfers between devices, body(): slab = lax.all_gather(table_low, 'narrow', axis=0, tiled=True)  102 us
    psum x1, waiting for transfers between devices, body(): gram = lax.psum(gram + partner(gram), 'narrow')  96.3 us
    pallas_call x1, Pallas kernels, gather_weights(): pl.pallas_call(weights_kernel, out_shape=shapes, in_specs=[ANY] * 5, out_...  73 us
    pallas_call x1, Pallas kernels, scatter_rows(): pl.pallas_call(row_sums_kernel, out_shape=jax.ShapeDtypeStruct((32, DP),...  44.5 us
    pallas_call x1, Pallas kernels, gather_rows(): pl.pallas_call(rows_kernel, out_shape=jax.ShapeDtypeStruct((4, 4, 4, 2, 3...  40.7 us
    all_gather x1, waiting for transfers between devices, body(): d_embed = lax.all_gather(d_x0, 'wide', axis=0, tiled=True)  34.7 us
  transfers between devices with their start and end apart: 19, of which 8 were waited for; matrix products, arithmetic and copies ran while one was open for 7% of the time, Pallas kernels for 16%

profile of v1, /device:TPU:1, one launch (start us, length us, event | category | flops | bytes accessed | tf_op | source)
XLA Modules:
  0.0 1160.4 jit_solution(9422969254237501591)
XLA Ops:
  12.8 101.6 %all-gather.5.cloned.1.call-done = bf16[6144,1024]{0,1:T(8,128)(2,1)} async-done(((bf16[384,1024]{0,1:T(8,128)(2,1)}), bf16[6144,1024]{0,1:T(8,128)(2,1)}) %all-gather.5.cloned.1.call-update) | async-done | bytes 12582928 | tf_op jit(solution)/shard_map/all_gather | solution.py:772
  114.4 16.6 %copy.123 = bf16[6144,1024]{1,0:T(8,128)(2,1)} copy(bf16[6144,1024]{0,1:T(8,128)(2,1)} %all-gather.5.cloned.1.call-done) | data formatting | bytes 25165824 | tf_op jit(solution)/shard_map/all_gather | solution.py:772
  131.1 17.1 %gather_fusion = bf16[2048,1024]{1,0:T(8,128)(2,1)} fusion(bf16[6144,1024]{1,0:T(8,128)(2,1)} %copy.123, s32[2048]{0:T(1024)S(1)} %broadcast_clamp_fusion), kind=kCustom, calls=%fused_computation | custom fusion | bytes 8396800 | tf_op jit(solution)/shard_map/gather | solution.py:792
  159.5 73.0 %gather_weights.1 = (bf16[4,4,112,1024]{3,2,1,0:T(8,128)(2,1)}, bf16[2,4,2,64,1024]{4,3,2,1,0:T(8,128)(2,1)}, bf16[2,2,2,4,160,1024]{5,4,3,2,1,0:T(8,128)(2,1)},...) custom-call(bf16[112,128]{1,0:T(8,128)(2,1)} %copy.117.gi, bf16[64,128]{1,0:T(8,128)(2,1)} %reshape.696.go, ...), custom_call_target="tpu_custom_call" | custom-call | tf_op jit(solution)/shard_map/gather_weights/pallas_call | solution.py:250
  249.4 23.6 %all-gather.9.cloned.1.call-done = bf16[2048,640]{0,1:T(8,128)(2,1)} async-done(((bf16[256,640]{0,1:T(8,128)(2,1)}), bf16[2048,640]{0,1:T(8,128)(2,1)}) %all-gather.9.cloned.1.call-update) | async-done | bytes 2621456 | tf_op jit(solution)/shard_map/all_gather | solution.py:805
  277.3 15.9 %slice_reduce_fusion.3 = (bf16[8,128,320]{1,0,2:T(8,128)(2,1)}, bf16[8,128,320]{1,0,2:T(8,128)(2,1)}, bf16[8,128,320]{1,0,2:T(8,128)(2,1)}, bf16[8,128,320]{1,0,2:T(8,128)(2,1)}) fusion(bf16[8,2,128,640]{2,1,0,3:T(2,128)(2,1)S(1)} %reshape.706), kind=kLoop, calls=%fused_computation.199 | loop fusion | bytes 5242880 | tf_op jit(solution)/shard_map/slice | solution.py:818
  325.1 40.7 %gather_rows.1 = bf16[4,4,4,2,32,1024]{5,4,3,2,1,0:T(8,128)(2,1)} custom-call(bf16[32,1024]{1,0:T(8,128)(2,1)} %gather_fusion.1), custom_call_target="tpu_custom_call" | custom-call | tf_op jit(solution)/shard_map/gather_rows/pallas_call | solution.py:296
  365.9 7.1 fusion.305
  381.5 14.2 %row_totals.1 = f32[32,128]{1,0:T(8,128)} custom-call(f32[2,32,128]{2,1,0:T(8,128)} %pad_maximum_fusion.15.own), custom_call_target="tpu_custom_call" | custom-call | tf_op jit(solution)/shard_map/row_totals/pallas_call | solution.py:343
  396.4 7.7 multiply_convert_fusion
  417.1 44.5 %scatter_rows.1 = f32[32,1024]{1,0:T(8,128)} custom-call(f32[4,4,4,32,1024]{4,3,2,1,0:T(8,128)} %bitcast.446), custom_call_target="tpu_custom_call" | custom-call | tf_op jit(solution)/shard_map/scatter_rows/pallas_call | solution.py:638
  485.9 7.9 fusion.6
  506.3 7.2 fusion.8
  519.7 7.1 fusion.5
  544.7 31.2 %reduce-scatter.6.cloned.1.call-done = f32[256,640]{1,0:T(8,128)} async-done(((f32[2048,640]{1,0:T(8,128)}), f32[256,640]{1,0:T(8,128)}) %reduce-scatter.6.cloned.1.call-update) | async-done | bytes 655376 | tf_op jit(solution)/shard_map/reduce_scatter | solution.py:902
  589.7 34.7 %all-gather.7.cloned.1.call-done = bf16[2048,1024]{1,0:T(8,128)(2,1)} async-done(((bf16[256,1024]{1,0:T(8,128)(2,1)}), bf16[2048,1024]{1,0:T(8,128)(2,1)}) %all-gather.7.cloned.1.call-update) | async-done | bytes 4194320 | tf_op jit(solution)/shard_map/all_gather | solution.py:950
  624.4 30.9 %fusion = f32[6144,1024]{1,0:T(8,128)} fusion(bf16[2048,1024]{1,0:T(8,128)(2,1)} %all-gather.7.cloned.1.call-done, s32[2048]{0:T(1024)S(1)} %bitcast.532), kind=kOutput, calls=%fused_computation.5 | convolution fusion | flops 25782386688 | bytes 29368320 | tf_op jit(solution)/shard_map/dot_general | solution.py:685
  691.3 7.5 convolution_convert_fusion
  702.5 112.8 %scatter_grads.1 = f32[3,224,128]{2,1,0:T(8,128)} custom-call(bf16[4,4,112,512]{3,2,1,0:T(8,128)(2,1)} %bitcast.485, bf16[2,4,2,64,512]{4,3,2,1,0:T(8,128)(2,1)} %bitcast.491, bf16[2,2,2,4,160,512]{5,4,3,2,1,0:T(8,128)(2,1)} %bitcast.458, bf16[2,4,2,160,512]{4,3,2,1,0:T(8,128)(2,1)} %bitcast.478), custom_call_target="tpu_custom_call" | custom-call | tf_op jit(solution)/shard_map/scatter_grads/pallas_call | solution.py:596
  822.8 33.4 %reduce-scatter.8.cloned.1.call-done = f32[384,1024]{1,0:T(8,128)} async-done(((f32[6144,1024]{1,0:T(8,128)}), f32[384,1024]{1,0:T(8,128)}) %reduce-scatter.8.cloned.1.call-update) | async-done | bytes 1572880 | tf_op jit(solution)/shard_map/reduce_scatter | solution.py:954
  856.3 7.9 multiply_reduce_fusion.2
  866.8 15.7 %global_sums.1 = f32[32,128]{1,0:T(8,128)} custom-call(f32[32,128]{1,0:T(8,128)} %select_maximum_fusion.own), custom_call_target="tpu_custom_call" | custom-call | tf_op jit(solution)/shard_map/global_sums/pallas_call | solution.py:343
  890.7 15.7 %all_to_all.10 = f32[8,160,128]{2,1,0:T(8,128)S(1)} all-to-all(f32[8,160,128]{2,1,0:T(8,128)S(1)} %bitcast_dynamic-update-slice_fusion), channel_id=1, replica_groups=mesh['wide'=8,'narrow'=16] {'wide'}, dimensions={0} | all-to-all | bytes 1310720 | tf_op jit(solution)/shard_map/all_to_all | solution.py:982
  925.0 96.3 %all-reduce.26.cloned.1.call-done = f32[1024,1024]{1,0:T(8,128)} async-done(((f32[1024,1024]{1,0:T(8,128)}), f32[1024,1024]{1,0:T(8,128)}) %all-reduce.26.cloned.1.call-update) | async-done | bytes 4194320 | tf_op jit(solution)/shard_map/psum | solution.py:985
  1025.0 10.8 fusion.280
  1049.6 7.3 fusion.311
  1056.9 7.5 fusion.67
  1075.1 7.2 fusion.312
  1082.4 7.0 fusion.61
  1098.4 7.4 fusion.313
  1105.9 7.0 fusion.55
  1114.8 7.1 fusion.53
  (542 shorter events, 300.2 us)
Async XLA Ops:
  7.2 107.2 %all-gather.5.cloned.1.call-start = ((), (), s32[]{:S(2)}) async-start(), calls=%async_computation.5 | async-start | bytes 13369344 | tf_op jit(solution)/shard_map/all_gather | solution.py:772
  7.3 470.0 %copy-start.94 = (pred[960]{0:T(1024)(128)(4,1)}, pred[960]{0:T(1024)(128)(4,1)S(1)}, u32[]{:S(2)}) copy-start(pred[960]{0:T(1024)(128)(4,1)S(1)} %get-tuple-element.193) | copy-start | bytes 2884
  7.3 470.0 %copy-start.96 = (pred[960]{0:T(1024)(128)(4,1)}, pred[960]{0:T(1024)(128)(4,1)S(1)}, u32[]{:S(2)}) copy-start(pred[960]{0:T(1024)(128)(4,1)S(1)} %get-tuple-element.194) | copy-start | bytes 2884
  7.3 469.9 %copy-start.85 = (s32[960]{0:T(1024)}, s32[960]{0:T(1024)S(1)}, u32[]{:S(2)}) copy-start(s32[960]{0:T(1024)S(1)} %get-tuple-element.197) | copy-start | bytes 11524
  7.3 469.9 %copy-start.87 = (s32[960]{0:T(1024)}, s32[960]{0:T(1024)S(1)}, u32[]{:S(2)}) copy-start(s32[960]{0:T(1024)S(1)} %get-tuple-element.198) | copy-start | bytes 11524
  7.3 469.9 %copy-start.89 = (s32[960]{0:T(1024)}, s32[960]{0:T(1024)S(1)}, u32[]{:S(2)}) copy-start(s32[960]{0:T(1024)S(1)} %get-tuple-element.195) | copy-start | bytes 11524
  7.3 469.9 %copy-start.91 = (s32[960]{0:T(1024)}, s32[960]{0:T(1024)S(1)}, u32[]{:S(2)}) copy-start(s32[960]{0:T(1024)S(1)} %get-tuple-element.196) | copy-start | bytes 11524
  12.1 225.4 %reduce-scatter.4.cloned.1.call-start = ((), (), s32[]{:S(2)}) async-start(), calls=%async_computation.6 | async-start | bytes 4718592 | tf_op jit(solution)/shard_map/reduce_scatter | solution.py:793
  152.1 121.0 %all-gather.9.cloned.1.call-start = ((), (), s32[]{:S(2)}) async-start(), calls=%async_computation.11 | async-start | bytes 2949120 | tf_op jit(solution)/shard_map/all_gather | solution.py:805
  244.3 331.6 %reduce-scatter.6.cloned.1.call-start = ((), (), s32[]{:S(2)}) async-start(), calls=%async_computation.7 | async-start | bytes 5898240 | tf_op jit(solution)/shard_map/reduce_scatter | solution.py:902
  404.6 6.8 collective-permute-start
  407.2 4.2 collective-permute-start.1
  538.3 86.2 %all-gather.7.cloned.1.call-start = ((), (), s32[]{:S(2)}) async-start(), calls=%async_computation.8 | async-start | bytes 4718592 | tf_op jit(solution)/shard_map/all_gather | solution.py:950
  589.7 266.6 %reduce-scatter.8.cloned.1.call-start = ((), (), s32[]{:S(2)}) async-start(), calls=%async_computation.9 | async-start | bytes 26738688 | tf_op jit(solution)/shard_map/reduce_scatter | solution.py:954
  655.3 366.0 %all-reduce.26.cloned.1.call-start = ((), (), s32[]{:S(2)}) async-start(), calls=%async_computation.10 | async-start | bytes 8388608 | tf_op jit(solution)/shard_map/psum | solution.py:985
  666.7 17.2 %collective-permute-start.8 = (bf16[256,2560]{1,0:T(8,128)(2,1)}, bf16[256,2560]{1,0:T(8,128)(2,1)}, u32[]{:S(2)}, u32[]{:S(2)}) collective-permute-start(bf16[256,2560]{1,0:T(8,128)(2,1)} %copy-done.40), channel_id=1, source_target_pairs={{0,16},{16,0},{32,48},{48,32},{64,80},{80,64},{96,112},{112,96},{1... | collective-permute-start | bytes 3932168 | tf_op jit(solution)/shard_map/ppermute | solution.py:725
  667.0 24.2 %collective-permute-start.6 = (bf16[256,5120]{1,0:T(8,128)(2,1)}, bf16[256,5120]{1,0:T(8,128)(2,1)}, u32[]{:S(2)}, u32[]{:S(2)}) collective-permute-start(bf16[256,5120]{1,0:T(8,128)(2,1)} %copy-done.28), channel_id=1, source_target_pairs={{0,16},{16,0},{32,48},{48,32},{64,80},{80,64},{96,112},{112,96},{1... | collective-permute-start | bytes 7864328 | tf_op jit(solution)/shard_map/ppermute | solution.py:725
  675.4 13.6 %collective-permute-start.5 = (bf16[256,512]{1,0:T(8,128)(2,1)S(1)}, bf16[256,512]{1,0:T(8,128)(2,1)S(1)}, u32[]{:S(2)}, u32[]{:S(2)}) collective-permute-start(bf16[256,512]{1,0:T(8,128)(2,1)S(1)} %get-tuple-element.131), channel_id=1, source_target_pairs={{0,16},{16,0},{32,48},{48,32},{64,80},{80,64},{96,112},{112,96},{1... | collective-permute-start | bytes 786440 | tf_op jit(solution)/shard_map/ppermute | solution.py:725
  678.2 11.3 collective-permute-start.4
  679.5 4.8 collective-permute-start.9
  684.0 7.3 collective-permute-start.7
  684.3 14.5 %collective-permute-start.2 = (bf16[256,1792]{1,0:T(8,128)(2,1)S(1)}, bf16[256,1792]{1,0:T(8,128)(2,1)}, u32[]{:S(2)}, u32[]{:S(2)}) collective-permute-start(bf16[256,1792]{1,0:T(8,128)(2,1)S(1)} %fusion.81), channel_id=1, source_target_pairs={{0,16},{16,0},{32,48},{48,32},{64,80},{80,64},{96,112},{112,96},{1... | collective-permute-start | bytes 2752520 | tf_op jit(solution)/shard_map/ppermute | solution.py:725
  689.0 9.8 collective-permute-start.3
  702.4 153.8 %copy-start.38 = (f32[384,1024]{1,0:T(8,128)S(1)}, f32[384,1024]{1,0:T(8,128)}, u32[]{:S(2)}) copy-start(f32[384,1024]{1,0:T(8,128)} %fusion.309) | copy-start | bytes 4718596
  702.4 153.8 %copy-start.86 = (s32[960]{0:T(1024)S(1)}, s32[960]{0:T(1024)}, u32[]{:S(2)}) copy-start(s32[960]{0:T(1024)} %copy-done.85) | copy-start | bytes 11524
  702.4 153.8 %copy-start.88 = (s32[960]{0:T(1024)S(1)}, s32[960]{0:T(1024)}, u32[]{:S(2)}) copy-start(s32[960]{0:T(1024)} %copy-done.87) | copy-start | bytes 11524
  702.4 153.8 %copy-start.90 = (s32[960]{0:T(1024)S(1)}, s32[960]{0:T(1024)}, u32[]{:S(2)}) copy-start(s32[960]{0:T(1024)} %copy-done.89) | copy-start | bytes 11524
  702.5 153.8 %copy-start.92 = (s32[960]{0:T(1024)S(1)}, s32[960]{0:T(1024)}, u32[]{:S(2)}) copy-start(s32[960]{0:T(1024)} %copy-done.91) | copy-start | bytes 11524
  702.5 153.8 %copy-start.95 = (pred[960]{0:T(1024)(128)(4,1)S(1)}, pred[960]{0:T(1024)(128)(4,1)}, u32[]{:S(2)}) copy-start(pred[960]{0:T(1024)(128)(4,1)} %copy-done.94) | copy-start | bytes 2884
  702.5 153.8 %copy-start.97 = (pred[960]{0:T(1024)(128)(4,1)S(1)}, pred[960]{0:T(1024)(128)(4,1)}, u32[]{:S(2)}) copy-start(pred[960]{0:T(1024)(128)(4,1)} %copy-done.96) | copy-start | bytes 2884
  910.8 7.7 collective-permute-start.10
  1126.7 17.4 %all-to-all-start.1 = ((f32[8,160,128]{2,1,0:T(8,128)}), f32[8,160,128]{2,1,0:T(8,128)S(1)}, u32[]{:S(2)}, u32[]{:S(2)}) async-start(f32[8,160,128]{2,1,0:T(8,128)} %bitcast.133), calls=%async_computation.4 | async-start | bytes 1310720 | tf_op jit(solution)/shard_map/all_to_all | solution.py:1000
  (95 other events, 786.6 us)
Sparse Core Ops, SparseCore 0:
  12.2 102.1 all-gather.4
  152.2 46.2 reduce-scatter.3
  244.4 28.6 all-gather.8
  538.4 37.4 reduce-scatter.5
  589.8 34.5 all-gather.6
  655.5 200.7 reduce-scatter.7
  921.7 99.6 all-reduce.25

commit v2 on v1

--- a/solution.py
+++ b/solution.py
@@ -258,6 +258,7 @@
             pltpu.SemaphoreType.DMA((6,)),
         ],
         compiler_params=pltpu.CompilerParams(collective_id=0, has_side_effects=True),
+        cost_estimate=pl.CostEstimate(flops=0, bytes_accessed=400_000_000, transcendentals=0),
         name="gather_weights",
     )(gi, go, gg, gd, meta)
 
@@ -366,163 +367,161 @@
     return stats[0] + jnp.log(stats[1])
 
 
-def add_up(dst, index, parts):
+def add_up(dst, parts):
+    if len(dst.shape) == 3:
+
+        @pl.loop(0, dst.shape[0])
+        def _(k):
+            total = parts[0][k].astype(F32)
+            for part in parts[1:]:
+                total = total + part[k].astype(F32)
+            dst[k] = total.astype(dst.dtype)
+
+        return
     total = parts[0][...].astype(F32)
     for part in parts[1:]:
         total = total + part[...].astype(F32)
-    dst[index] = total.astype(dst.dtype)
+    dst[...] = total.astype(dst.dtype)
+
+
+class Ring:
+    def __init__(self, net, place, axis, source, got, mid, result):
+        self.net, self.source, self.got, self.mid, self.result = net, source, got, mid, result
+        steps = [at_step(place, axis, step) for step in range(4)]
+        self.own, self.up, self.across, self.down = [step[axis] for step in steps]
+        self.to_up, self.to_down = steps[1], steps[3]
+
+    def send_across(self):
+        self.far_up = self.net.put(self.source(self.across, 0), self.got(0), self.to_up)
+        self.far_down = self.net.put(self.source(self.across, 1), self.got(1), self.to_down)
+
+    def send_up(self):
+        self.near_up = self.net.put(self.source(self.up, 1), self.got(2), self.to_up)
+
+    def send_down(self):
+        self.near_down = self.net.put(self.source(self.down, 0), self.got(3), self.to_down)
+
+    def send_all(self):
+        self.send_across()
+        self.send_up()
+        self.send_down()
+
+    def pass_on(self):
+        self.far_up.wait_recv()
+        add_up(self.mid(0), [self.source(self.up, 0), self.got(0)])
+        self.on_up = self.net.put(self.mid(0), self.got(4), self.to_up)
+        self.far_down.wait_recv()
+        add_up(self.mid(1), [self.source(self.down, 1), self.got(1)])
+        self.on_down = self.net.put(self.mid(1), self.got(5), self.to_down)
+
+    def close(self):
+        for copy in (self.near_up, self.near_down, self.on_up, self.on_down):
+            copy.wait_recv()
+        add_up(self.result(0), [self.source(self.own, 0), self.got(4), self.got(3)])
+        add_up(self.result(1), [self.source(self.own, 1), self.got(2), self.got(5)])
+
+
+FAR_FIRST = (2, 1, 3, 0)
+
+
+def start_scatter(net, place, orders, sources, works, outs):
+    streams = []
+    for order, source, work, out in zip(orders, sources, works, outs):
+        rows = out.shape[0] // 2
+        halves = (pl.ds(0, rows), pl.ds(rows, rows))
+        deep = len(order) == 3
+        stream = {"first": {}, "rest": []}
+
+        def block(one, two, half, order=order, source=source, halves=halves, deep=deep):
+            sel = {"z": None, "x": None, "y": None, order[0]: one, order[1]: two}
+            lead = ("z", "x", "y") if deep else ("z", "x")
+            return source.at[tuple(pick(sel[axis]) for axis in lead) + (halves[half],)]
+
+        for sub, far in enumerate(FAR_FIRST):
+            two = at_step(place, order[1], far)[order[1]]
+            acc = work["acc1"]
+
+            def result(half, two=two, acc=acc, halves=halves, deep=deep):
+                return acc.at[(two,) + ((slice(None),) if deep else ()) + (halves[half],)]
+
+            stream["first"][far] = Ring(
+                net,
+                place,
+                order[0],
+                lambda one, half, two=two, block=block: block(one, two, half),
+                lambda k, sub=sub, work=work: work["got1"].at[sub, k],
+                lambda k, sub=sub, work=work: work["mid1"].at[sub, k],
+                result,
+            )
+        if deep:
+            stream["rest"].append(
+                Ring(
+                    net,
+                    place,
+                    order[1],
+                    lambda two, half, work=work, halves=halves: work["acc1"].at[
+                        two, :, halves[half]
+                    ],
+                    lambda k, work=work: work["got2"].at[k],
+                    lambda k, work=work: work["mid2"].at[k],
+                    lambda half, work=work, halves=halves: work["acc2"].at[:, halves[half]],
+                )
+            )
+        final, number = ("acc2", "3") if deep else ("acc1", "2")
+        stream["rest"].append(
+            Ring(
+                net,
+                place,
+                order[-1],
+                lambda k, half, work=work, halves=halves, final=final: work[final].at[
+                    k, halves[half]
+                ],
+                lambda k, work=work, number=number: work["got" + number].at[k],
+                lambda k, work=work, number=number: work["mid" + number].at[k],
+                lambda half, out=out, halves=halves: out.at[halves[half]],
+            )
+        )
+        streams.append(stream)
+    return streams
+
+
+def send_first(streams):
+    for far in FAR_FIRST:
+        for stream in streams:
+            stream["first"][far].send_across()
+    for far in FAR_FIRST:
+        for stream in streams:
+            stream["first"][far].send_up()
+            stream["first"][far].send_down()
+
+
+def finish_scatter(streams):
+    for far in FAR_FIRST:
+        for stream in streams:
+            stream["first"][far].pass_on()
+    for far in FAR_FIRST:
+        for stream in streams:
+            stream["first"][far].close()
+            following = stream["rest"][0]
+            if far == 2:
+                following.send_across()
+            if far == 1:
+                following.send_up()
+            if far == 3:
+                following.send_down()
+    for number in range(len(streams[0]["rest"])):
+        for stream in streams:
+            stream["rest"][number].pass_on()
+        for stream in streams:
+            stream["rest"][number].close()
+            if number + 1 < len(stream["rest"]):
+                stream["rest"][number + 1].send_all()
 
 
 def scatter_sum(net, place, orders, sources, works, outs):
-    def block(ref, sel, rows):
-        return ref.at[pick(sel["z"]), pick(sel["x"]), pick(sel["y"]), pl.ds(*rows)]
-
-    jobs = []
-    for order, source, work, out in zip(orders, sources, works, outs):
-        rows = source.shape[3] // 2
-        jobs.append(
-            {
-                "order": order,
-                "source": source,
-                "work": work,
-                "out": out,
-                "halves": ((0, rows), (rows, rows)),
-                "steps": [
-                    [at_step(place, axis, step) for step in range(4)] for axis in order
-                ],
-            }
-        )
-
-    def everywhere():
-        return {"z": None, "x": None, "y": None}
-
-    def first_view(job, one, two, half):
-        a, b, _ = job["order"]
-        sel = {**everywhere(), a: one, b: two}
-        return block(job["source"], sel, job["halves"][half])
-
-    sequence = (2, 1, 3, 0)
-    for sub, far in enumerate(sequence):
-        for job in jobs:
-            a, b, _ = job["order"]
-            own = job["steps"][0]
-            two = job["steps"][1][far][b]
-            got = job["work"]["got1"]
-            job.setdefault("c1", []).append(
-                {
-                    "ra": net.put(first_view(job, own[2][a], two, 0), got.at[sub, 0], own[1]),
-                    "rb": net.put(first_view(job, own[2][a], two, 1), got.at[sub, 1], own[3]),
-                }
-            )
-    for sub, far in enumerate(sequence):
-        for job in jobs:
-            a, b, _ = job["order"]
-            own = job["steps"][0]
-            two = job["steps"][1][far][b]
-            got = job["work"]["got1"]
-            copies = job["c1"][sub]
-            copies["p1"] = net.put(first_view(job, own[1][a], two, 1), got.at[sub, 2], own[1])
-            copies["m0"] = net.put(first_view(job, own[3][a], two, 0), got.at[sub, 3], own[3])
-    for sub, far in enumerate(sequence):
-        for job in jobs:
-            a, b, _ = job["order"]
-            own = job["steps"][0]
-            two = job["steps"][1][far][b]
-            got, mid = job["work"]["got1"], job["work"]["mid1"]
-            copies = job["c1"][sub]
-            copies["ra"].wait_recv()
-            add_up(mid, (sub, 0), [first_view(job, own[1][a], two, 0), got.at[sub, 0]])
-            copies["p0"] = net.put(mid.at[sub, 0], got.at[sub, 4], own[1])
-            copies["rb"].wait_recv()
-            add_up(mid, (sub, 1), [first_view(job, own[3][a], two, 1), got.at[sub, 1]])
-            copies["m1"] = net.put(mid.at[sub, 1], got.at[sub, 5], own[3])
-    def second_view(job, two, half):
-        return job["work"]["acc1"].at[two, :, pl.ds(*job["halves"][half])]
-
-    for sub, far in enumerate(sequence):
-        for job in jobs:
-            a, b, _ = job["order"]
-            own = job["steps"][0]
-            next_own = job["steps"][1]
-            two = next_own[far][b]
-            got = job["work"]["got1"]
-            copies = job["c1"][sub]
-            for name in ("p1", "m0", "p0", "m1"):
-                copies[name].wait_recv()
-            acc = job["work"]["acc1"]
-            for half, (one, other) in enumerate(((4, 3), (2, 5))):
-                add_up(
-                    acc,
-                    (two, slice(None), pl.ds(*job["halves"][half])),
-                    [first_view(job, own[0][a], two, half), got.at[sub, one], got.at[sub, other]],
-                )
-            got2 = job["work"]["got2"]
-            if far == 2:
-                job["c2"] = {
-                    "ra": net.put(second_view(job, two, 0), got2.at[0], next_own[1]),
-                    "rb": net.put(second_view(job, two, 1), got2.at[1], next_own[3]),
-                }
-            if far == 1:
-                job["c2"]["p1"] = net.put(second_view(job, two, 1), got2.at[2], next_own[1])
-            if far == 3:
-                job["c2"]["m0"] = net.put(second_view(job, two, 0), got2.at[3], next_own[3])
-    for job in jobs:
-        b = job["order"][1]
-        own = job["steps"][1]
-        got, mid, copies = job["work"]["got2"], job["work"]["mid2"], job["c2"]
-        copies["ra"].wait_recv()
-        add_up(mid, 0, [second_view(job, own[1][b], 0), got.at[0]])
-        copies["p0"] = net.put(mid.at[0], got.at[4], own[1])
-        copies["rb"].wait_recv()
-        add_up(mid, 1, [second_view(job, own[3][b], 1), got.at[1]])
-        copies["m1"] = net.put(mid.at[1], got.at[5], own[3])
-
-    def third_view(job, three, half):
-        return job["work"]["acc2"].at[three, pl.ds(*job["halves"][half])]
-
-    for job in jobs:
-        b = job["order"][1]
-        own = job["steps"][1]
-        got, acc, copies = job["work"]["got2"], job["work"]["acc2"], job["c2"]
-        for name in ("p1", "m0", "p0", "m1"):
-            copies[name].wait_recv()
-        for half, (one, other) in enumerate(((4, 3), (2, 5))):
-            add_up(
-                acc,
-                (slice(None), pl.ds(*job["halves"][half])),
-                [second_view(job, own[0][b], half), got.at[one], got.at[other]],
-            )
-        third = job["order"][2]
-        own = job["steps"][2]
-        got = job["work"]["got3"]
-        job["c3"] = {
-            "ra": net.put(third_view(job, own[2][third], 0), got.at[0], own[1]),
-            "rb": net.put(third_view(job, own[2][third], 1), got.at[1], own[3]),
-            "p1": net.put(third_view(job, own[1][third], 1), got.at[2], own[1]),
-            "m0": net.put(third_view(job, own[3][third], 0), got.at[3], own[3]),
-        }
-    for job in jobs:
-        third = job["order"][2]
-        own = job["steps"][2]
-        got, mid, copies = job["work"]["got3"], job["work"]["mid3"], job["c3"]
-        copies["ra"].wait_recv()
-        add_up(mid, 0, [third_view(job, own[1][third], 0), got.at[0]])
-        copies["p0"] = net.put(mid.at[0], got.at[4], own[1])
-        copies["rb"].wait_recv()
-        add_up(mid, 1, [third_view(job, own[3][third], 1), got.at[1]])
-        copies["m1"] = net.put(mid.at[1], got.at[5], own[3])
-    for job in jobs:
-        third = job["order"][2]
-        own = job["steps"][2]
-        got, copies = job["work"]["got3"], job["c3"]
-        for name in ("p1", "m0", "p0", "m1"):
-            copies[name].wait_recv()
-        for half, (one, other) in enumerate(((4, 3), (2, 5))):
-            add_up(
-                job["out"],
-                (pl.ds(*job["halves"][half]),),
-                [third_view(job, own[0][third], half), got.at[one], got.at[other]],
-            )
+    streams = start_scatter(net, place, orders, sources, works, outs)
+    send_first(streams)
+    finish_scatter(streams)
 
 
 WORK_NAMES = ("got1", "mid1", "acc1", "got2", "mid2", "acc2", "got3", "mid3")
@@ -542,7 +541,22 @@
     ]
 
 
+SHALLOW_NAMES = ("got1", "mid1", "acc1", "got2", "mid2")
+
+
+def shallow_shapes(rows, lanes, first, later):
+    half = rows // 2
+    return [
+        pltpu.VMEM((4, 6, half, lanes), first),
+        pltpu.VMEM((4, 2, half, lanes), first),
+        pltpu.VMEM((4, rows, lanes), later),
+        pltpu.VMEM((6, half, lanes), later),
+        pltpu.VMEM((2, half, lanes), later),
+    ]
+
+
 SUM_COPIES = 3 * (24 + 6 + 6)
+SHALLOW_COPIES = 2 * (24 + 6)
 
 
 def grads_kernel(di, do, dg, dd, out, *scratch):
@@ -646,6 +660,178 @@
         ),
         name="scatter_rows",
     )(part)
+
+
+def embed_grad_kernel(dx, ids, out, rows, table, chosen, *scratch):
+    works = [dict(zip(SHALLOW_NAMES, scratch[5 * k : 5 * k + 5])) for k in range(2)]
+    send, recv, local = scratch[10:]
+    place = my_place()
+    greet(neighbours(place))
+    copy = pltpu.make_async_copy(dx, rows.at[place["y"], place["c"]], local)
+    copy.start()
+    copy.wait()
+
+    def in_rows(sel, part):
+        return rows.at[pick(sel["y"]), sel["c"], pl.ds(*part)]
+
+    net = Net(send, recv)
+    gather_streams(net, place, [(("y",), [(in_rows, ((0, 128), (128, 128)))])], True)
+    base = (place["y"] * 2 + place["c"]) * 16
+
+    def parts(count, place_of):
+        @pl.loop(0, count)
+        def _(k):
+            z, x = place_of(k)
+            start = (base + z * 4 + x) * 384
+
+            @pl.loop(0, 24)
+            def _(r):
+                row = pl.multiple_of(r * 16, 16)
+                number = lax.broadcasted_iota(jnp.int32, (16, 2048), 0) + (start + row)
+                chosen[pl.ds(row, 16), :] = (number == ids[...]).astype(F32).astype(BF16)
+
+            @pl.loop(0, 4)
+            def _(l):
+                lanes = pl.ds(pl.multiple_of(l * 256, 256), 256)
+                total = jnp.zeros((384, 256), F32)
+                for w in range(8):
+                    total = total + jnp.dot(
+                        chosen[:, pl.ds(w * 256, 256)],
+                        rows[w // 2, w % 2, :, lanes],
+                        preferred_element_type=F32,
+                    )
+                table[z, x, :, lanes] = total.astype(BF16)
+
+    def further(axis, step):
+        return lax.rem(place[axis] + step, 4)
+
+    sources = [table.at[:, :, pl.ds(0, 192)], table.at[:, :, pl.ds(192, 192)]]
+    outs = [out.at[pl.ds(0, 192)], out.at[pl.ds(192, 192)]]
+    streams = start_scatter(net, place, (("x", "z"), ("z", "x")), sources, works, outs)
+    by_x, by_z = streams[0]["first"], streams[1]["first"]
+    parts(4, lambda k: (further("z", 2), further("x", k + 2)))
+    for step in FAR_FIRST:
+        by_z[step].send_across()
+    by_x[2].send_across()
+    parts(3, lambda k: (further("z", k + 3), further("x", 2)))
+    for step in (1, 3, 0):
+        by_x[step].send_across()
+    by_x[2].send_up()
+    by_x[2].send_down()
+    by_z[2].send_up()
+    by_z[2].send_down()
+    parts(9, lambda k: (further("z", lax.div(k, 3) + 3), further("x", lax.rem(k, 3) + 3)))
+    for step in (1, 3, 0):
+        by_x[step].send_up()
+        by_x[step].send_down()
+        by_z[step].send_up()
+        by_z[step].send_down()
+    finish_scatter(streams)
+    net.finish()
+
+
+def embed_grad(dx, ids):
+    count = SHALLOW_COPIES + 16
+    scratch = [
+        pltpu.VMEM((4, 2, 256, DP), BF16),
+        pltpu.VMEM((4, 4, 384, DP), BF16),
+        pltpu.VMEM((384, 2048), BF16),
+    ]
+    for _ in range(2):
+        scratch += shallow_shapes(192, DP, BF16, BF16)
+    scratch += [
+        pltpu.SemaphoreType.DMA((count,)),
+        pltpu.SemaphoreType.DMA((count,)),
+        pltpu.SemaphoreType.DMA,
+    ]
+    return pl.pallas_call(
+        embed_grad_kernel,
+        out_shape=jax.ShapeDtypeStruct((384, DP), F32),
+        in_specs=[ANY, VMEM],
+        out_specs=VMEM,
+        scratch_shapes=scratch,
+        compiler_params=pltpu.CompilerParams(
+            collective_id=6, has_side_effects=True, vmem_limit_bytes=56 << 20
+        ),
+        name="embed_grad",
+    )(dx, ids)
+
+
+def gram_kernel(pieces, turned, gram, part, *scratch):
+    works = [dict(zip(SHALLOW_NAMES, scratch[5 * k : 5 * k + 5])) for k in range(2)]
+    send, recv, local = scratch[10:]
+    place = my_place()
+    wides = [
+        {**at_step(place, "y", step), "c": core}
+        for step in (2, 1, 3, 0)
+        for core in (place["c"], 1 - place["c"])
+    ][:-2] + [other_core(place)]
+    greet(wides + neighbours(place, ("x", "z"), False))
+    net = Net(send, recv)
+
+    def lanes_from(who):
+        return pl.ds(pl.multiple_of((who["c"] * 4 + who["y"]) * 128, 128), 128)
+
+    arrivals = [net.put(pieces.at[who["y"]], turned.at[:, lanes_from(place)], who) for who in wides]
+    copy = pltpu.make_async_copy(pieces.at[place["y"]], turned.at[:, lanes_from(place)], local)
+    copy.start()
+    copy.wait()
+    for arrival in arrivals:
+        arrival.wait_recv()
+    @pl.loop(0, 4)
+    def _(k):
+        rows = pl.ds(pl.multiple_of(place["c"] * 512 + k * 128, 128), 128)
+        left = turned[:, rows].T
+        for l in range(2):
+            lanes = pl.ds(l * 512, 512)
+            product = jnp.dot(left, turned[:, lanes], precision=HIGHEST, preferred_element_type=F32)
+            for m in range(4):
+                part[k, m, :, lanes] = product[m * 32 : m * 32 + 32]
+
+    orders = (("x", "z"), ("z", "x"))
+    lanes = (pl.ds(0, 512), pl.ds(512, 512))
+    sources = [part.at[:, :, :, lane] for lane in lanes]
+    mine = gram.at[place["c"], place["z"], place["x"]]
+    outs = [mine.at[:, lane] for lane in lanes]
+    scatter_sum(net, place, orders, sources, works, outs)
+
+    def in_gram(lane):
+        def region(sel, rows):
+            return gram.at[sel["c"], pick(sel["z"]), pick(sel["x"]), pl.ds(*rows), lane]
+
+        return region
+
+    streams = [
+        (order[::-1], [(in_gram(lane), ((0, 16), (16, 16)))]) for order, lane in zip(orders, lanes)
+    ]
+    gather_streams(net, place, streams, True)
+    net.finish()
+
+
+def gram_of(pieces):
+    count = 7 + SHALLOW_COPIES + 44
+    scratch = [pltpu.VMEM((4, 4, 32, DP), F32)]
+    for _ in range(2):
+        scratch += shallow_shapes(32, 512, F32, F32)
+    scratch += [
+        pltpu.SemaphoreType.DMA((count,)),
+        pltpu.SemaphoreType.DMA((count,)),
+        pltpu.SemaphoreType.DMA,
+    ]
+    return pl.pallas_call(
+        gram_kernel,
+        out_shape=[
+            jax.ShapeDtypeStruct((320, DP), F32),
+            jax.ShapeDtypeStruct((2, 4, 4, 32, DP), F32),
+        ],
+        in_specs=[VMEM],
+        out_specs=[VMEM, VMEM],
+        scratch_shapes=scratch,
+        compiler_params=pltpu.CompilerParams(
+            collective_id=7, has_side_effects=True, vmem_limit_bytes=40 << 20
+        ),
+        name="gram_sums",
+    )(pieces)
 
 
 def pad_features(values):
@@ -776,6 +962,7 @@
         to_shard(master.astype(BF16), rows) for master, rows in zip(masters, (RI, RO, RG, RD))
     ]
     wi, wo, wg, wd, info = gather_weights(*shards, meta)
+    slab, wi = lax.optimization_barrier((slab, wi))
     wi = wi.reshape(16, RI, DP)[:, :100].reshape(QKV, DP)
     wo = wo.reshape(DP, DP)
     wg = wg.reshape(2 * FF, DP)
@@ -863,7 +1050,7 @@
     d_theirs = lax.dynamic_index_in_dim(d_by_core, 1 - core, 1, keepdims=False).reshape(2048, 384)
     d_theirs = partner(d_theirs)
     row_part = dot(d_mine, table_low, 1, 0) + dot(d_theirs, table_other, 1, 0)
-    d_rows = scatter_rows(row_part.reshape(4, 4, 4, 32, DP), F32, F32)
+    d_rows = scatter_rows(row_part.astype(BF16).reshape(4, 4, 4, 32, DP), BF16, F32)
 
     d_final = jnp.zeros((rows_count, DP), F32).at[own_offsets].add(d_rows)
     d_x2, d_gain_final = jax.vjp(rms_norm, x2, gains[2])[1](d_final)
@@ -947,13 +1134,7 @@
         summed_grads[2, :160],
     )
 
-    d_embed = lax.all_gather(d_x0, "wide", axis=0, tiled=True)
-    onehot = (
-        lax.broadcasted_iota(jnp.int32, (slab_rows, 2048), 0) == local_ids[None, :]
-    ).astype(BF16)
-    table_grad = lax.psum_scatter(
-        dot(onehot, d_embed, 1, 0), "narrow", scatter_dimension=0, tiled=True
-    )
+    table_grad = embed_grad(d_x0, ordered[None, :])
     table_grad = dot(table_grad + table_grad_rows, features, 1, 1, HIGHEST)
 
     squares = sum(jnp.sum(shard * shard) for shard in grad_shards) + jnp.sum(
@@ -972,17 +1153,10 @@
         MOMENTUM * to_shard(moment, rows) + factor * grad
         for moment, rows, grad in zip(moments, (RI, RO, RG, RD), grad_shards)
     ]
-    pieces = jnp.stack(
-        [
-            jnp.pad(part, ((0, 160 - part.shape[0]), (0, 0)))
-            for shard in new_shards
-            for part in jnp.split(shard, 2)
-        ]
-    )
-    pieces = lax.all_to_all(pieces, "wide", split_axis=0, concat_axis=0)
-    turned = pieces.reshape(4, 2, 160, 128).transpose(2, 1, 0, 3).reshape(160, DP)
-    gram = dot(turned, turned, 0, 0, HIGHEST)
-    gram = lax.psum(gram + partner(gram), "narrow")
+    pieces = jnp.stack([jnp.pad(s, ((0, 320 - s.shape[0]), (0, 0))) for s in new_shards])
+    turned, gram = gram_of(pieces)
+    gram = gram.reshape(DP, DP)
+    turned = lax.dynamic_slice_in_dim(turned, core * 160, 160)
     norm = jnp.sqrt(jnp.trace(gram)) + 1e-07
     current = turned / norm
     gram = gram / norm / norm
@@ -998,10 +1172,11 @@
             current = NS_A * current + NS_B * applied + NS_C * dot(applied, gram, 1, 0, HIGH)
     pieces = current.reshape(160, 2, 4, 128).transpose(2, 1, 0, 3).reshape(8, 160, 128)
     pieces = lax.all_to_all(pieces, "wide", split_axis=0, concat_axis=0)
+    pieces = pieces.reshape(4, 320, 128)
     new_moments, new_weights = [], []
     for kind, rows in enumerate((RI, RO, RG, RD)):
         count = masters[kind].shape[1]
-        ortho = jnp.concatenate([pieces[2 * kind, : rows // 2], pieces[2 * kind + 1, : rows // 2]])
+        ortho = pieces[kind, :rows]
         new_moments.append(from_shard(new_shards[kind], count)[None])
         new_weights.append(
             (

time: 1170 us -> 1020 us (0.87)
  waiting for transfers between devices: 329 us -> 85.6 us
  Pallas kernels: 301 us -> 427 us
  matrix products: 258 us -> 221 us
  blocking collectives: 15.7 us -> 0 us
  local copies, waits for them, and re-layouts: 136 us -> 149 us
    pallas_call x0 -> x2, Pallas kernels: none -> 177 us  [the longest x1 115 us: embed_grad(): pl.pallas_call(embed_grad_kernel, out_shape=jax.ShapeDtypeStruct((384, DP...]
    psum x1 -> x0, waiting for transfers between devices: 96.3 us -> none  [body(): gram = lax.psum(gram + partner(gram), 'narrow')]
    all_gather x1, waiting for transfers between devices: 102 us -> 31.1 us  [body(): slab = lax.all_gather(table_low, 'narrow', axis=0, tiled=True)]
    pallas_call x1, Pallas kernels: 113 us -> 61.3 us  [scatter_grads(): pl.pallas_call(grads_kernel, out_shape=jax.ShapeDtypeStruct((3, rows, lan...]
    dot_general x41 -> x39, matrix products: 227 us -> 189 us  [dot(): lax.dot_general(left, right, (((left_axis,), (right_axis,)), ((), ())), p...]
    all_gather x1 -> x0, waiting for transfers between devices: 34.7 us -> none  [body(): d_embed = lax.all_gather(d_x0, 'wide', axis=0, tiled=True)]
    reduce_scatter x1 -> x0, waiting for transfers between devices: 33.4 us -> none  [body(): lax.psum_scatter(dot(onehot, d_embed, 1, 0), 'narrow', scatter_dimension=...]
    reduce_scatter x1, waiting for transfers between devices: 31.2 us -> 0.01 us  [body(): lax.psum_scatter(d_kv_all, 'wide', scatter_dimension=0, tiled=True)]
  transfers between devices with their start and end apart: 19 -> 15, of which waited for: 8 -> 4; matrix products, arithmetic and copies ran while one was open for 7% -> 10% of each run, Pallas kernels for 16% -> 20%
where the time goes in v2:
time: 1020 us; the launch traced here: 1010 us
  Pallas kernels  427 us (42%)
  matrix products  221 us (22%)
  local copies, waits for them, and re-layouts  149 us (15%)
  waiting for transfers between devices  85.6 us (8%)
  other arithmetic  84.4 us (8%)
  between operations  28.3 us (3%)
  starting transfers between devices  13.8 us (1%)
    dot_general x39, matrix products, dot(): lax.dot_general(left, right, (((left_axis,), (right_axis,)), ((), ())), p...  189 us
    pallas_call x1, Pallas kernels, embed_grad(): pl.pallas_call(embed_grad_kernel, out_shape=jax.ShapeDtypeStruct((384, DP...  115 us
    pallas_call x1, Pallas kernels, gather_weights(): pl.pallas_call(weights_kernel, out_shape=shapes, in_specs=[ANY] * 5, out_...  89.3 us
    pallas_call x1, Pallas kernels, scatter_grads(): pl.pallas_call(grads_kernel, out_shape=jax.ShapeDtypeStruct((3, rows, lan...  61.3 us
    pallas_call x1, Pallas kernels, gram_of(): pl.pallas_call(gram_kernel, out_shape=[jax.ShapeDtypeStruct((320, DP), F3...  61.2 us
    pallas_call x1, Pallas kernels, gather_rows(): pl.pallas_call(rows_kernel, out_shape=jax.ShapeDtypeStruct((4, 4, 4, 2, 3...  40.7 us
    unnamed x281, local copies, waits for them, and re-layouts  33.6 us
    all_gather x1, waiting for transfers between devices, body(): slab = lax.all_gather(table_low, 'narrow', axis=0, tiled=True)  31.1 us
  transfers between devices with their start and end apart: 15, of which 4 were waited for; matrix products, arithmetic and copies ran while one was open for 10% of the time, Pallas kernels for 20%

profile of v2, /device:TPU:1, one launch (start us, length us, event | category | flops | bytes accessed | tf_op | source)
XLA Modules:
  0.0 1009.6 jit_solution(4627559879366445380)
XLA Ops:
  19.1 89.3 %gather_weights.1 = (bf16[4,4,112,1024]{3,2,1,0:T(8,128)(2,1)}, bf16[2,4,2,64,1024]{4,3,2,1,0:T(8,128)(2,1)}, bf16[2,2,2,4,160,1024]{5,4,3,2,1,0:T(8,128)(2,1)},...) custom-call(bf16[112,128]{1,0:T(8,128)(2,1)} %copy.113.gi, bf16[64,128]{1,0:T(8,128)(2,1)} %reshape.730.go, ...), custom_call_target="tpu_custom_call" | custom-call | bytes 400000000 | tf_op jit(solution)/shard_map/gather_weights/pallas_call | solution.py:250
  108.4 31.1 %all-gather.4.cloned.1.call-done = bf16[6144,1024]{0,1:T(8,128)(2,1)} async-done(((bf16[384,1024]{0,1:T(8,128)(2,1)}), bf16[6144,1024]{0,1:T(8,128)(2,1)}) %all-gather.4.cloned.1.call-update) | async-done | bytes 12582928 | tf_op jit(solution)/shard_map/all_gather | solution.py:958
  139.5 16.6 %copy.118 = bf16[6144,1024]{1,0:T(8,128)(2,1)} copy(bf16[6144,1024]{0,1:T(8,128)(2,1)} %all-gather.4.cloned.1.call-done) | data formatting | bytes 25165824 | tf_op jit(solution)/shard_map/optimization_barrier | solution.py:965
  156.1 17.1 %gather_fusion = bf16[2048,1024]{1,0:T(8,128)(2,1)} fusion(bf16[6144,1024]{1,0:T(8,128)(2,1)} %copy.118, s32[2048]{0:T(1024)S(1)} %broadcast_clamp_fusion), kind=kCustom, calls=%fused_computation | custom fusion | bytes 8396800 | tf_op jit(solution)/shard_map/gather | solution.py:979
  184.2 26.7 %reduce-scatter.3.cloned.1.call-done = bf16[256,1024]{1,0:T(8,128)(2,1)} async-done(((bf16[2048,1024]{1,0:T(8,128)(2,1)}), bf16[256,1024]{1,0:T(8,128)(2,1)}) %reduce-scatter.3.cloned.1.call-update) | async-done | bytes 524304 | tf_op jit(solution)/shard_map/reduce_scatter | solution.py:980
  223.6 27.0 %all-gather.6.cloned.1.call-done = bf16[2048,640]{0,1:T(8,128)(2,1)} async-done(((bf16[256,640]{0,1:T(8,128)(2,1)}), bf16[2048,640]{0,1:T(8,128)(2,1)}) %all-gather.6.cloned.1.call-update) | async-done | bytes 2621456 | tf_op jit(solution)/shard_map/all_gather | solution.py:992
  254.8 15.9 %slice_reduce_fusion.3 = (bf16[8,128,320]{1,0,2:T(8,128)(2,1)}, bf16[8,128,320]{1,0,2:T(8,128)(2,1)}, bf16[8,128,320]{1,0,2:T(8,128)(2,1)}, bf16[8,128,320]{1,0,2:T(8,128)(2,1)}) fusion(bf16[8,2,128,640]{2,1,0,3:T(2,128)(2,1)S(1)} %reshape.740), kind=kLoop, calls=%fused_computation.197 | loop fusion | bytes 5242880 | tf_op jit(solution)/shard_map/slice | solution.py:1005
  306.7 40.7 %gather_rows.1 = bf16[4,4,4,2,32,1024]{5,4,3,2,1,0:T(8,128)(2,1)} custom-call(bf16[32,1024]{1,0:T(8,128)(2,1)} %gather_fusion.1), custom_call_target="tpu_custom_call" | custom-call | tf_op jit(solution)/shard_map/gather_rows/pallas_call | solution.py:297
  347.5 7.1 fusion.300
  363.1 14.2 %row_totals.1 = f32[32,128]{1,0:T(8,128)} custom-call(f32[2,32,128]{2,1,0:T(8,128)} %pad_maximum_fusion.11.own), custom_call_target="tpu_custom_call" | custom-call | tf_op jit(solution)/shard_map/row_totals/pallas_call | solution.py:344
  378.0 7.7 multiply_convert_fusion
  397.4 30.7 %scatter_rows.1 = f32[32,1024]{1,0:T(8,128)} custom-call(bf16[4,4,4,32,1024]{4,3,2,1,0:T(8,128)(2,1)} %bitcast.429), custom_call_target="tpu_custom_call" | custom-call | tf_op jit(solution)/shard_map/scatter_rows/pallas_call | solution.py:652
  442.3 7.5 multiply_reduce_fusion.4
  463.0 7.9 fusion.4
  486.6 7.2 fusion.6
  500.2 7.1 fusion.3
  539.5 7.0 fusion.304
  564.3 7.0 convolution_convert_fusion
  588.0 115.4 %embed_grad.1 = f32[384,1024]{1,0:T(8,128)} custom-call(bf16[256,1024]{1,0:T(8,128)(2,1)} %fusion.145.dx, s32[1,2048]{1,0:T(1,128)} %bitcast.511), custom_call_target="tpu_custom_call" | custom-call | tf_op jit(solution)/shard_map/embed_grad/pallas_call | solution.py:747
  703.5 7.5 multiply_reduce_fusion.2
  714.4 61.3 %scatter_grads.1 = f32[3,224,128]{2,1,0:T(8,128)} custom-call(bf16[4,4,112,512]{3,2,1,0:T(8,128)(2,1)} %bitcast.466, bf16[2,4,2,64,512]{4,3,2,1,0:T(8,128)(2,1)} %bitcast.474, bf16[2,2,2,4,160,512]{5,4,3,2,1,0:T(8,128)(2,1)} %bitcast.437, bf16[2,4,2,160,512]{4,3,2,1,0:T(8,128)(2,1)} %bitcast.459), custom_call_target="tpu_custom_call" | custom-call | tf_op jit(solution)/shard_map/scatter_grads/pallas_call | solution.py:610
  786.0 14.5 %global_sums.1 = f32[32,128]{1,0:T(8,128)} custom-call(f32[32,128]{1,0:T(8,128)} %select_maximum_fusion.own), custom_call_target="tpu_custom_call" | custom-call | tf_op jit(solution)/shard_map/global_sums/pallas_call | solution.py:344
  811.1 61.2 %gram_sums.1 = (f32[320,1024]{1,0:T(8,128)S(1)}, f32[2,4,4,32,1024]{4,3,2,1,0:T(8,128)S(1)}) custom-call(f32[4,320,128]{2,1,0:T(8,128)S(1)} %pad_maximum_fusion.3.pieces), custom_call_target="tpu_custom_call" | custom-call | tf_op jit(solution)/shard_map/gram_sums/pallas_call | solution.py:821
  879.9 7.0 fusion.305
  886.9 7.2 fusion.71
  901.1 7.3 fusion.306
  908.3 7.0 fusion.65
  926.6 7.2 fusion.307
  933.8 7.0 fusion.59
  949.9 7.4 fusion.308
  957.3 7.0 fusion.53
  966.3 7.1 fusion.51
  (562 shorter events, 289.2 us)
Async XLA Ops:
  7.2 132.3 %all-gather.4.cloned.1.call-start = ((), (), s32[]{:S(2)}) async-start(), calls=%async_computation.3 | async-start | bytes 13369344 | tf_op jit(solution)/shard_map/all_gather | solution.py:958
  12.3 198.5 %reduce-scatter.3.cloned.1.call-start = ((), (), s32[]{:S(2)}) async-start(), calls=%async_computation.4 | async-start | bytes 4718592 | tf_op jit(solution)/shard_map/reduce_scatter | solution.py:980
  177.1 73.5 %all-gather.6.cloned.1.call-start = ((), (), s32[]{:S(2)}) async-start(), calls=%async_computation.6 | async-start | bytes 2949120 | tf_op jit(solution)/shard_map/all_gather | solution.py:992
  178.6 34.1 %copy-start.81 = (f32[1024]{0:T(1024)}, f32[1024]{0:T(1024)S(1)}, u32[]{:S(2)}) copy-start(f32[1024]{0:T(1024)S(1)} %mul.921) | copy-start | bytes 12292
  179.3 43.9 %copy-start.39 = (f32[256,64]{0,1:T(8,128)}, f32[256,64]{0,1:T(8,128)S(1)}, u32[]{:S(2)}) copy-start(f32[256,64]{0,1:T(8,128)S(1)} %get-tuple-element.193) | copy-start | bytes 196612
  179.3 43.9 %copy-start.41 = (f32[256,64]{0,1:T(8,128)}, f32[256,64]{0,1:T(8,128)S(1)}, u32[]{:S(2)}) copy-start(f32[256,64]{0,1:T(8,128)S(1)} %get-tuple-element.194) | copy-start | bytes 196612
  218.7 352.7 %reduce-scatter.5.cloned.1.call-start = ((), (), s32[]{:S(2)}) async-start(), calls=%async_computation.5 | async-start | bytes 5898240 | tf_op jit(solution)/shard_map/reduce_scatter | solution.py:1089
  219.1 85.3 %copy-start.73 = (f32[1024]{0:T(1024)}, f32[1024]{0:T(1024)S(1)}, u32[]{:S(2)}) copy-start(f32[1024]{0:T(1024)S(1)} %mul.955) | copy-start | bytes 12292
  219.2 73.3 %copy-start.83 = (f32[1024]{0:T(1024)}, f32[1024]{0:T(1024)S(1)}, u32[]{:S(2)}) copy-start(f32[1024]{0:T(1024)S(1)} %mul.946) | copy-start | bytes 12292
  223.6 53.6 %copy-start.23 = (bf16[128,15,64]{0,2,1:T(8,128)(2,1)}, bf16[128,15,64]{0,2,1:T(8,128)(2,1)S(1)}, u32[]{:S(2)}) copy-start(bf16[128,15,64]{0,2,1:T(8,128)(2,1)S(1)} %get-tuple-element.137) | copy-start | bytes 737284
  306.7 40.7 %copy-start.25 = (bf16[1024,384]{1,0:T(8,128)(2,1)S(1)}, bf16[1024,384]{1,0:T(8,128)(2,1)}, u32[]{:S(2)}) copy-start(bf16[1024,384]{1,0:T(8,128)(2,1)} %convolution_convert_fusion.4) | copy-start | bytes 2359300
  386.2 6.8 collective-permute-start
  388.8 4.2 collective-permute-start.1
  397.4 32.9 %copy-start.74 = (f32[1024]{0:T(1024)S(1)}, f32[1024]{0:T(1024)}, u32[]{:S(2)}) copy-start(f32[1024]{0:T(1024)} %copy-done.73) | copy-start | bytes 12292
  535.2 175.9 %collective-permute-start.3 = (bf16[256,512]{1,0:T(8,128)(2,1)}, bf16[256,512]{1,0:T(8,128)(2,1)}, u32[]{:S(2)}, u32[]{:S(2)}) collective-permute-start(bf16[256,512]{1,0:T(8,128)(2,1)} %get-tuple-element.131), channel_id=1, source_target_pairs={{0,16},{16,0},{32,48},{48,32},{64,80},{80,64},{96,112},{112,96},{1... | collective-permute-start | bytes 786440 | tf_op jit(solution)/shard_map/ppermute | solution.py:911
  538.9 18.2 %collective-permute-start.8 = (bf16[256,2560]{1,0:T(8,128)(2,1)}, bf16[256,2560]{1,0:T(8,128)(2,1)}, u32[]{:S(2)}, u32[]{:S(2)}) collective-permute-start(bf16[256,2560]{1,0:T(8,128)(2,1)} %copy-done.45), channel_id=1, source_target_pairs={{0,16},{16,0},{32,48},{48,32},{64,80},{80,64},{96,112},{112,96},{1... | collective-permute-start | bytes 3932168 | tf_op jit(solution)/shard_map/ppermute | solution.py:911
  539.0 25.3 %collective-permute-start.6 = (bf16[256,5120]{1,0:T(8,128)(2,1)}, bf16[256,5120]{1,0:T(8,128)(2,1)}, u32[]{:S(2)}, u32[]{:S(2)}) collective-permute-start(bf16[256,5120]{1,0:T(8,128)(2,1)} %copy-done.31), channel_id=1, source_target_pairs={{0,16},{16,0},{32,48},{48,32},{64,80},{80,64},{96,112},{112,96},{1... | collective-permute-start | bytes 7864328 | tf_op jit(solution)/shard_map/ppermute | solution.py:911
  550.3 12.3 %collective-permute-start.4 = (bf16[256,1024]{1,0:T(8,128)(2,1)}, bf16[256,1024]{1,0:T(8,128)(2,1)S(1)}, u32[]{:S(2)}, u32[]{:S(2)}) collective-permute-start(bf16[256,1024]{1,0:T(8,128)(2,1)} %get-tuple-element.112), channel_id=1, source_target_pairs={{0,16},{16,0},{32,48},{48,32},{64,80},{80,64},{96,112},{112,96},{1... | collective-permute-start | bytes 1572872 | tf_op jit(solution)/shard_map/ppermute | solution.py:911
  551.7 5.7 collective-permute-start.9
  557.1 5.5 collective-permute-start.5
  557.5 6.9 collective-permute-start.7
  586.4 117.0 %copy-start.43 = (f32[384,1024]{1,0:T(8,128)S(1)}, f32[384,1024]{1,0:T(8,128)}, u32[]{:S(2)}) copy-start(f32[384,1024]{1,0:T(8,128)} %fusion.304) | copy-start | bytes 4718596
  586.4 117.0 %copy-start.101 = (s32[960]{0:T(1024)S(1)}, s32[960]{0:T(1024)}, u32[]{:S(2)}) copy-start(s32[960]{0:T(1024)} %copy-done.99) | copy-start | bytes 11524
  586.4 117.0 %copy-start.104 = (s32[960]{0:T(1024)S(1)}, s32[960]{0:T(1024)}, u32[]{:S(2)}) copy-start(s32[960]{0:T(1024)} %copy-done.102) | copy-start | bytes 11524
  586.4 117.0 %copy-start.107 = (s32[960]{0:T(1024)S(1)}, s32[960]{0:T(1024)}, u32[]{:S(2)}) copy-start(s32[960]{0:T(1024)} %copy-done.105) | copy-start | bytes 11524
  586.4 117.0 %copy-start.110 = (s32[960]{0:T(1024)S(1)}, s32[960]{0:T(1024)}, u32[]{:S(2)}) copy-start(s32[960]{0:T(1024)} %copy-done.108) | copy-start | bytes 11524
  586.4 117.0 %copy-start.117 = (pred[960]{0:T(1024)(128)(4,1)S(1)}, pred[960]{0:T(1024)(128)(4,1)}, u32[]{:S(2)}) copy-start(pred[960]{0:T(1024)(128)(4,1)} %copy-done.115) | copy-start | bytes 2884
  586.4 117.0 %copy-start.120 = (pred[960]{0:T(1024)(128)(4,1)S(1)}, pred[960]{0:T(1024)(128)(4,1)}, u32[]{:S(2)}) copy-start(pred[960]{0:T(1024)(128)(4,1)} %copy-done.118) | copy-start | bytes 2884
  586.4 124.6 %collective-permute-start.2 = (bf16[256,1792]{1,0:T(8,128)(2,1)S(1)}, bf16[256,1792]{1,0:T(8,128)(2,1)S(1)}, u32[]{:S(2)}, u32[]{:S(2)}) collective-permute-start(bf16[256,1792]{1,0:T(8,128)(2,1)S(1)} %fusion.79), channel_id=1, source_target_pairs={{0,16},{16,0},{32,48},{48,32},{64,80},{80,64},{96,112},{112,96},{1... | collective-permute-start | bytes 2752520 | tf_op jit(solution)/shard_map/ppermute | solution.py:911
  807.0 67.4 %copy-start.78 = (s32[2,4,4,32]{3,2,1,0:T(4,128)S(1)}, s32[2,4,4,32]{3,2,1,0:T(4,128)}, u32[]{:S(2)}) copy-start(s32[2,4,4,32]{3,2,1,0:T(4,128)} %multiply_add_fusion.4) | copy-start | bytes 12292
  809.9 69.9 %copy-start.61 = (f32[64,128]{1,0:T(8,128)}, f32[64,128]{1,0:T(8,128)S(1)}, u32[]{:S(2)}) copy-start(f32[64,128]{1,0:T(8,128)S(1)} %bitcast_add_fusion.2) | copy-start | bytes 98308
  978.2 15.6 %all-to-all-start = ((f32[8,160,128]{2,1,0:T(8,128)}), f32[8,160,128]{2,1,0:T(8,128)S(1)}, u32[]{:S(2)}, u32[]{:S(2)}) async-start(f32[8,160,128]{2,1,0:T(8,128)} %bitcast.123), calls=%async_computation.2 | async-start | bytes 1310720 | tf_op jit(solution)/shard_map/all_to_all | solution.py:1174
  (114 other events, 562.3 us)
Sparse Core Ops, SparseCore 0:
  12.4 127.0 all-gather.3
  177.2 33.6 reduce-scatter.2
  218.8 31.7 all-gather.5
  519.8 39.6 reduce-scatter.4

commit v3 on v2

--- a/solution.py
+++ b/solution.py
@@ -107,61 +107,71 @@
             copy.wait_send()
 
 
+class Spread:
+    def __init__(self, net, place, axes, items, with_core):
+        self.net, self.place, self.axes, self.items = net, place, axes, items
+        self.with_core = with_core
+        self.sel = dict(place)
+        self.phase = 0
+        self.core = []
+
+    def to_core(self, region, sel, half):
+        if self.with_core and self.phase == len(self.axes) - 1:
+            ref = region(sel, half)
+            self.core.append(self.net.put(ref, ref, other_core(self.place)))
+
+    def begin(self):
+        self.axis = self.axes[self.phase]
+        self.up, self.across, self.down = [at_step(self.place, self.axis, k) for k in (1, 2, 3)]
+        self.first, self.second, self.onward = [], [], []
+        for group, first_half in ((self.first, 0), (self.second, 1)):
+            for region, halves in self.items:
+                for target, origin, half in (
+                    (self.up, self.down, first_half),
+                    (self.down, self.up, 1 - first_half),
+                ):
+                    if halves[half] is not None:
+                        ref = region(self.sel, halves[half])
+                        copy = self.net.put(ref, ref, target)
+                        group.append((copy, origin, target, region, halves[half]))
+        for region, halves in self.items:
+            for half in halves:
+                if half is not None:
+                    self.to_core(region, self.sel, half)
+
+    def relay(self):
+        for copy, origin, target, region, half in self.first:
+            copy.wait_recv()
+            sel = {**self.sel, self.axis: origin[self.axis]}
+            ref = region(sel, half)
+            self.onward.append((self.net.put(ref, ref, target), region, half))
+            self.to_core(region, sel, half)
+
+    def near(self):
+        for copy, origin, _, region, half in self.second:
+            copy.wait_recv()
+            self.to_core(region, {**self.sel, self.axis: origin[self.axis]}, half)
+
+    def far(self):
+        for copy, region, half in self.onward:
+            copy.wait_recv()
+            self.to_core(region, {**self.sel, self.axis: self.across[self.axis]}, half)
+        self.sel[self.axis] = None
+        self.phase += 1
+
+    def end(self):
+        for copy in self.core:
+            copy.wait_recv()
+
+
 def gather_streams(net, place, streams, with_core):
-    states = [{"sel": dict(place), "core": []} for _ in streams]
-    phases = max(len(axes) for axes, _ in streams)
-    for phase in range(phases):
-        last = phase == phases - 1
-        for (axes, items), state in zip(streams, states):
-            axis = axes[phase]
-            up, down = at_step(place, axis, 1), at_step(place, axis, 3)
-            state["first"], state["second"] = [], []
-            for first_half in (0, 1):
-                for region, halves in items:
-                    for target, half, way in ((up, first_half, 0), (down, 1 - first_half, 1)):
-                        if halves[half] is None:
-                            continue
-                        ref = region(state["sel"], halves[half])
-                        group = "first" if first_half == 0 else "second"
-                        state[group].append((net.put(ref, ref, target), way, region, halves[half]))
-            if last and with_core:
-                for region, halves in items:
-                    for half in halves:
-                        if half is not None:
-                            ref = region(state["sel"], half)
-                            state["core"].append(net.put(ref, ref, other_core(place)))
-        for (axes, items), state in zip(streams, states):
-            axis = axes[phase]
-            up, down = at_step(place, axis, 1), at_step(place, axis, 3)
-            state["onward"] = []
-            for copy, way, region, half in state["first"]:
-                copy.wait_recv()
-                origin, target = (down, up) if way == 0 else (up, down)
-                ref = region({**state["sel"], axis: origin[axis]}, half)
-                state["onward"].append((net.put(ref, ref, target), region, half))
-                if last and with_core:
-                    state["core"].append(net.put(ref, ref, other_core(place)))
-        for (axes, items), state in zip(streams, states):
-            axis = axes[phase]
-            up, down = at_step(place, axis, 1), at_step(place, axis, 3)
-            for copy, way, region, half in state["second"]:
-                copy.wait_recv()
-                if last and with_core:
-                    origin = down if way == 0 else up
-                    ref = region({**state["sel"], axis: origin[axis]}, half)
-                    state["core"].append(net.put(ref, ref, other_core(place)))
-        for (axes, items), state in zip(streams, states):
-            axis = axes[phase]
-            across = at_step(place, axis, 2)
-            for copy, region, half in state["onward"]:
-                copy.wait_recv()
-                if last and with_core:
-                    ref = region({**state["sel"], axis: across[axis]}, half)
-                    state["core"].append(net.put(ref, ref, other_core(place)))
-            state["sel"] = {**state["sel"], axis: None}
-    for state in states:
-        for copy in state["core"]:
-            copy.wait_recv()
+    spreads = [Spread(net, place, axes, items, with_core) for axes, items in streams]
+    for _ in range(len(streams[0][0])):
+        for step in ("begin", "relay", "near", "far"):
+            for spread in spreads:
+                getattr(spread, step)()
+    for spread in spreads:
+        spread.end()
 
 
 def pick(index):
@@ -184,9 +194,11 @@
     return found + ([other_core(place)] if core else [])
 
 
-def weights_kernel(gi, go, gg, gd, meta, wi, wo, wg, wd, info, send, recv, local):
+def fetch_kernel(
+    gi, go, gg, gd, meta, table, ids, marks, wi, wo, wg, wd, info, x0, *scratch
+):
+    slab_x, slab_z, total, chosen, packed, theirs, got, send, recv, local = scratch
     place = my_place()
-    greet(neighbours(place))
 
     def in_wi(sel, rows):
         return wi.at[pick(sel["z"]), pick(sel["x"]), pl.ds(*rows), lanes_of(sel)]
@@ -219,48 +231,152 @@
         (gg.at[pl.ds(160, 160)], in_wg(1)(place, (0, 160))),
         (gd, in_wd(place, (0, RD))),
         (meta, in_info(place, None)),
+        (table.at[pl.ds(0, 192)], slab_x.at[place["z"], place["x"]]),
+        (table.at[pl.ds(192, 192)], slab_z.at[place["x"], place["z"]]),
     ]
     copies = [pltpu.make_async_copy(src, dst, local.at[k]) for k, (src, dst) in enumerate(owns)]
     for copy in copies:
         copy.start()
     for copy in copies:
         copy.wait()
-    streams = [
-        (("x", "z", "y"), [(in_wg(0), halved(0, 160)), (in_wo, halved(0, 64))]),
-        (("z", "y", "x"), [(in_wg(1), halved(0, 160)), (in_wi, halved(0, 64))]),
-        (
-            ("y", "x", "z"),
-            [(in_wd, halved(0, 160)), (in_wi, halved(64, 112)), (in_info, ((0, 8), None))],
+    greet(neighbours(place))
+    net = Net(send, recv)
+    rows = ((0, 96), (96, 96))
+    tables = [
+        Spread(
+            net,
+            place,
+            ("x", "z"),
+            [(lambda sel, part: slab_x.at[pick(sel["z"]), pick(sel["x"]), pl.ds(*part)], rows)],
+            False,
         ),
-    ]
-    net = Net(send, recv)
-    gather_streams(net, place, streams, True)
+        Spread(
+            net,
+            place,
+            ("z", "x"),
+            [(lambda sel, part: slab_z.at[pick(sel["x"]), pick(sel["z"]), pl.ds(*part)], rows)],
+            False,
+        ),
+    ]
+    weights = [
+        Spread(net, place, axes, items, True)
+        for axes, items in (
+            (("x", "z", "y"), [(in_wg(0), halved(0, 160)), (in_wo, halved(0, 64))]),
+            (("z", "x", "y"), [(in_wg(1), halved(0, 160)), (in_wi, halved(0, 64))]),
+            (
+                ("y", "z", "x"),
+                [(in_wd, halved(0, 160)), (in_wi, halved(64, 112)), (in_info, ((0, 8), None))],
+            ),
+        )
+    ]
+
+    def each(spreads, *steps):
+        for step in steps:
+            for spread in spreads:
+                getattr(spread, step)()
+
+    base = (place["y"] * 2 + place["c"]) * (16 * 384)
+
+    def look_up(slab, index, kind, start, initial):
+        @pl.loop(0, 16)
+        def _(r):
+            part = pl.ds(pl.multiple_of(r * 128, 128), 128)
+            wanted = ids[part, :] - start
+            chosen[part, :] = (marks[kind : kind + 1, :] == wanted).astype(F32).astype(BF16)
+
+        @pl.loop(0, 8)
+        def _(k):
+            part = pl.ds(pl.multiple_of(lax.div(k, 4) * 1024, 1024), 1024)
+            lanes = pl.ds(pl.multiple_of(lax.rem(k, 4) * 256, 256), 256)
+            block = slab[index, :, :, lanes].reshape(768, 256)
+            found = jnp.dot(chosen[part, :], block, preferred_element_type=F32)
+            total[part, lanes] = found if initial else total[part, lanes] + found
+
+    def by_x(step, initial=False):
+        z = lax.rem(place["z"] + step, 4)
+        look_up(slab_x, z, 0, base + z * (4 * 384), initial)
+
+    def by_z(step):
+        x = lax.rem(place["x"] + step, 4)
+        look_up(slab_z, x, 1, base + x * 384 + 192, False)
+
+    each(tables, "begin")
+    each(weights, "begin")
+    each(tables, "relay")
+    each(weights, "relay")
+    each(tables, "near", "far", "begin")
+    each(weights, "near", "far", "begin")
+    by_x(0, True)
+    by_z(0)
+    each(tables, "relay")
+    each(weights, "relay", "near", "far", "begin")
+    each(tables, "near")
+    by_x(1)
+    by_x(3)
+    each(weights, "relay")
+    by_z(1)
+    by_z(3)
+    each(tables, "far")
+    by_x(2)
+    each(weights, "near")
+    by_z(2)
+    for y in range(4):
+        for c in range(2):
+            packed[c, y] = total[(y * 2 + c) * 256 : (y * 2 + c + 1) * 256, :].astype(BF16)
+    swap = net.put(packed.at[1 - place["c"]], theirs, other_core(place))
+    swap.wait_recv()
+    mine = packed.at[place["c"]]
+    for y in range(4):
+        add_up(theirs.at[y], [mine.at[y], theirs.at[y]])
+    halves = (pl.ds(0, 128), pl.ds(128, 128))
+    ring = Ring(
+        net,
+        place,
+        "y",
+        lambda k, half: theirs.at[k, halves[half]],
+        lambda k: got.at[k],
+        lambda half: x0.at[halves[half]],
+    )
+    ring.send_all()
+    each(weights, "far")
+    ring.pass_on()
+    ring.close()
+    each(weights, "end")
     net.finish()
 
 
-def gather_weights(gi, go, gg, gd, meta):
+def fetch(gi, go, gg, gd, meta, table, ids, marks):
     shapes = [
         jax.ShapeDtypeStruct((4, 4, RI, DP), BF16),
         jax.ShapeDtypeStruct((2, 4, 2, RO, DP), BF16),
         jax.ShapeDtypeStruct((2, 2, 2, 4, 160, DP), BF16),
         jax.ShapeDtypeStruct((2, 4, 2, 160, DP), BF16),
         jax.ShapeDtypeStruct((4, 4, 4, 2, 8, 128), jnp.int32),
-    ]
-    count = 176
+        jax.ShapeDtypeStruct((256, DP), BF16),
+    ]
+    count = 210
     return pl.pallas_call(
-        weights_kernel,
+        fetch_kernel,
         out_shape=shapes,
-        in_specs=[ANY] * 5,
-        out_specs=[ANY] * 5,
+        in_specs=[ANY] * 6 + [VMEM] * 2,
+        out_specs=[ANY] * 5 + [VMEM],
         scratch_shapes=[
+            pltpu.VMEM((4, 4, 192, DP), BF16),
+            pltpu.VMEM((4, 4, 192, DP), BF16),
+            pltpu.VMEM((2048, DP), F32),
+            pltpu.VMEM((2048, 768), BF16),
+            pltpu.VMEM((2, 4, 256, DP), BF16),
+            pltpu.VMEM((4, 256, DP), BF16),
+            pltpu.VMEM((6, 128, DP), BF16),
             pltpu.SemaphoreType.DMA((count,)),
             pltpu.SemaphoreType.DMA((count,)),
-            pltpu.SemaphoreType.DMA((6,)),
+            pltpu.SemaphoreType.DMA((8,)),
         ],
-        compiler_params=pltpu.CompilerParams(collective_id=0, has_side_effects=True),
-        cost_estimate=pl.CostEstimate(flops=0, bytes_accessed=400_000_000, transcendentals=0),
-        name="gather_weights",
-    )(gi, go, gg, gd, meta)
+        compiler_params=pltpu.CompilerParams(
+            collective_id=0, has_side_effects=True, vmem_limit_bytes=56 << 20
+        ),
+        name="fetch",
+    )(gi, go, gg, gd, meta, table, ids, marks)
 
 
 LANE_PARTS = ((0, 384), (384, 384), (768, 256))
@@ -297,14 +413,16 @@
     return pl.pallas_call(
         rows_kernel,
         out_shape=jax.ShapeDtypeStruct((4, 4, 4, 2, 32, DP), BF16),
-        in_specs=[ANY],
-        out_specs=ANY,
+        in_specs=[VMEM],
+        out_specs=VMEM,
         scratch_shapes=[
             pltpu.SemaphoreType.DMA((count,)),
             pltpu.SemaphoreType.DMA((count,)),
             pltpu.SemaphoreType.DMA,
         ],
-        compiler_params=pltpu.CompilerParams(collective_id=1, has_side_effects=True),
+        compiler_params=pltpu.CompilerParams(
+            collective_id=1, has_side_effects=True, vmem_limit_bytes=24 << 20
+        ),
         name="gather_rows",
     )(own)
 
@@ -385,8 +503,8 @@
 
 
 class Ring:
-    def __init__(self, net, place, axis, source, got, mid, result):
-        self.net, self.source, self.got, self.mid, self.result = net, source, got, mid, result
+    def __init__(self, net, place, axis, source, got, result):
+        self.net, self.source, self.got, self.result = net, source, got, result
         steps = [at_step(place, axis, step) for step in range(4)]
         self.own, self.up, self.across, self.down = [step[axis] for step in steps]
         self.to_up, self.to_down = steps[1], steps[3]
@@ -408,11 +526,11 @@
 
     def pass_on(self):
         self.far_up.wait_recv()
-        add_up(self.mid(0), [self.source(self.up, 0), self.got(0)])
-        self.on_up = self.net.put(self.mid(0), self.got(4), self.to_up)
+        add_up(self.got(0), [self.source(self.up, 0), self.got(0)])
+        self.on_up = self.net.put(self.got(0), self.got(4), self.to_up)
         self.far_down.wait_recv()
-        add_up(self.mid(1), [self.source(self.down, 1), self.got(1)])
-        self.on_down = self.net.put(self.mid(1), self.got(5), self.to_down)
+        add_up(self.got(1), [self.source(self.down, 1), self.got(1)])
+        self.on_down = self.net.put(self.got(1), self.got(5), self.to_down)
 
     def close(self):
         for copy in (self.near_up, self.near_down, self.on_up, self.on_down):
@@ -424,65 +542,45 @@
 FAR_FIRST = (2, 1, 3, 0)
 
 
-def start_scatter(net, place, orders, sources, works, outs):
-    streams = []
-    for order, source, work, out in zip(orders, sources, works, outs):
-        rows = out.shape[0] // 2
-        halves = (pl.ds(0, rows), pl.ds(rows, rows))
-        deep = len(order) == 3
-        stream = {"first": {}, "rest": []}
-
-        def block(one, two, half, order=order, source=source, halves=halves, deep=deep):
-            sel = {"z": None, "x": None, "y": None, order[0]: one, order[1]: two}
-            lead = ("z", "x", "y") if deep else ("z", "x")
-            return source.at[tuple(pick(sel[axis]) for axis in lead) + (halves[half],)]
-
-        for sub, far in enumerate(FAR_FIRST):
-            two = at_step(place, order[1], far)[order[1]]
-            acc = work["acc1"]
-
-            def result(half, two=two, acc=acc, halves=halves, deep=deep):
-                return acc.at[(two,) + ((slice(None),) if deep else ()) + (halves[half],)]
-
-            stream["first"][far] = Ring(
-                net,
-                place,
-                order[0],
-                lambda one, half, two=two, block=block: block(one, two, half),
-                lambda k, sub=sub, work=work: work["got1"].at[sub, k],
-                lambda k, sub=sub, work=work: work["mid1"].at[sub, k],
-                result,
-            )
-        if deep:
-            stream["rest"].append(
-                Ring(
-                    net,
-                    place,
-                    order[1],
-                    lambda two, half, work=work, halves=halves: work["acc1"].at[
-                        two, :, halves[half]
-                    ],
-                    lambda k, work=work: work["got2"].at[k],
-                    lambda k, work=work: work["mid2"].at[k],
-                    lambda half, work=work, halves=halves: work["acc2"].at[:, halves[half]],
-                )
-            )
-        final, number = ("acc2", "3") if deep else ("acc1", "2")
+def start_scatter(net, place, order, source, gots, out, acc=None):
+    rows = out.shape[0] // 2
+    halves = (pl.ds(0, rows), pl.ds(rows, rows))
+    lead = ("z", "x", "y")[: len(order)]
+
+    def block(sel, half):
+        return source.at[tuple(pick(sel.get(axis)) for axis in lead) + (halves[half],)]
+
+    def summed(sel, half):
+        if acc is None:
+            return block({order[0]: place[order[0]], **sel}, half)
+        return acc.at[tuple(pick(sel.get(axis)) for axis in order[1:]) + (halves[half],)]
+
+    stream = {"first": {}, "rest": []}
+    one, two = order[:2]
+    for sub, far in enumerate(FAR_FIRST):
+        at_two = at_step(place, two, far)[two]
+        stream["first"][far] = Ring(
+            net,
+            place,
+            one,
+            lambda k, half, at_two=at_two: block({one: k, two: at_two}, half),
+            lambda k, sub=sub: gots[0].at[sub, k],
+            lambda half, at_two=at_two: summed({two: at_two}, half),
+        )
+    for number in range(1, len(order)):
+        done = {axis: place[axis] for axis in order[1:number]}
+
+        def part(k, half, done=done, axis=order[number]):
+            return summed({**done, axis: k}, half)
+
+        if number + 1 < len(order):
+            result = lambda half, part=part, axis=order[number]: part(place[axis], half)
+        else:
+            result = lambda half: out.at[halves[half]]
         stream["rest"].append(
-            Ring(
-                net,
-                place,
-                order[-1],
-                lambda k, half, work=work, halves=halves, final=final: work[final].at[
-                    k, halves[half]
-                ],
-                lambda k, work=work, number=number: work["got" + number].at[k],
-                lambda k, work=work, number=number: work["mid" + number].at[k],
-                lambda half, out=out, halves=halves: out.at[halves[half]],
-            )
+            Ring(net, place, order[number], part, lambda k, n=number: gots[n].at[k], result)
         )
-        streams.append(stream)
-    return streams
+    return stream
 
 
 def send_first(streams):
@@ -495,10 +593,11 @@
             stream["first"][far].send_down()
 
 
-def finish_scatter(streams):
-    for far in FAR_FIRST:
-        for stream in streams:
-            stream["first"][far].pass_on()
+def finish_scatter(streams, passed=False):
+    if not passed:
+        for far in FAR_FIRST:
+            for stream in streams:
+                stream["first"][far].pass_on()
     for far in FAR_FIRST:
         for stream in streams:
             stream["first"][far].close()
@@ -509,62 +608,94 @@
                 following.send_up()
             if far == 3:
                 following.send_down()
-    for number in range(len(streams[0]["rest"])):
-        for stream in streams:
-            stream["rest"][number].pass_on()
-        for stream in streams:
-            stream["rest"][number].close()
-            if number + 1 < len(stream["rest"]):
-                stream["rest"][number + 1].send_all()
-
-
-def scatter_sum(net, place, orders, sources, works, outs):
-    streams = start_scatter(net, place, orders, sources, works, outs)
+    for number in range(max(len(stream["rest"]) for stream in streams)):
+        active = [stream["rest"] for stream in streams if number < len(stream["rest"])]
+        for rest in active:
+            rest[number].pass_on()
+        for rest in active:
+            rest[number].close()
+            if number + 1 < len(rest):
+                rest[number + 1].send_all()
+
+
+def got_shapes(depth, rows, lanes, first, later):
+    half = rows // 2
+    return [
+        pltpu.VMEM(
+            ((4, 6) if number == 0 else (6,)) + (4,) * (depth - max(number, 1) - 1) + (half, lanes),
+            later if number else first,
+        )
+        for number in range(depth)
+    ]
+
+
+def row_sums_kernel(part, out, *scratch):
+    held = scratch[0:3]
+    accs = scratch[12:15]
+    send, recv, local = scratch[15:]
+    place = my_place()
+    copies = [
+        pltpu.make_async_copy(part.at[:, :, :, :, pl.ds(*lanes)], held[k], local.at[k])
+        for k, lanes in enumerate(LANE_PARTS)
+    ]
+    for copy in copies:
+        copy.start()
+    greet(neighbours(place, core=False))
+    for copy in copies:
+        copy.wait()
+    net = Net(send, recv)
+    streams = [
+        start_scatter(
+            net,
+            place,
+            order,
+            held[k],
+            scratch[3 + 3 * k : 6 + 3 * k],
+            out.at[:, pl.ds(*lanes)],
+            accs[k],
+        )
+        for k, (order, lanes) in enumerate(zip(ORDERS, LANE_PARTS))
+    ]
     send_first(streams)
     finish_scatter(streams)
-
-
-WORK_NAMES = ("got1", "mid1", "acc1", "got2", "mid2", "acc2", "got3", "mid3")
-
-
-def work_shapes(rows, lanes, first, later):
-    half = rows // 2
-    return [
-        pltpu.VMEM((4, 6, 4, half, lanes), first),
-        pltpu.VMEM((4, 2, 4, half, lanes), first),
-        pltpu.VMEM((4, 4, rows, lanes), later),
-        pltpu.VMEM((6, 4, half, lanes), later),
-        pltpu.VMEM((2, 4, half, lanes), later),
-        pltpu.VMEM((4, rows, lanes), later),
-        pltpu.VMEM((6, half, lanes), later),
-        pltpu.VMEM((2, half, lanes), later),
-    ]
-
-
-SHALLOW_NAMES = ("got1", "mid1", "acc1", "got2", "mid2")
-
-
-def shallow_shapes(rows, lanes, first, later):
-    half = rows // 2
-    return [
-        pltpu.VMEM((4, 6, half, lanes), first),
-        pltpu.VMEM((4, 2, half, lanes), first),
-        pltpu.VMEM((4, rows, lanes), later),
-        pltpu.VMEM((6, half, lanes), later),
-        pltpu.VMEM((2, half, lanes), later),
-    ]
-
-
-SUM_COPIES = 3 * (24 + 6 + 6)
-SHALLOW_COPIES = 2 * (24 + 6)
-
-
-def grads_kernel(di, do, dg, dd, out, *scratch):
-    held = scratch[0:3]
-    works = [dict(zip(WORK_NAMES, scratch[3 + 8 * k : 11 + 8 * k])) for k in range(3)]
-    send, recv, local = scratch[27:]
+    net.finish()
+
+
+def scatter_rows(part):
+    scratch = [pltpu.VMEM((4, 4, 4, 32, lanes), part.dtype) for _, lanes in LANE_PARTS]
+    for _, lanes in LANE_PARTS:
+        scratch += got_shapes(3, 32, lanes, part.dtype, F32)
+    scratch += [pltpu.VMEM((4, 4, 32, lanes), F32) for _, lanes in LANE_PARTS]
+    scratch += [
+        pltpu.SemaphoreType.DMA((108,)),
+        pltpu.SemaphoreType.DMA((108,)),
+        pltpu.SemaphoreType.DMA((3,)),
+    ]
+    return pl.pallas_call(
+        row_sums_kernel,
+        out_shape=jax.ShapeDtypeStruct((32, DP), F32),
+        in_specs=[ANY],
+        out_specs=VMEM,
+        scratch_shapes=scratch,
+        compiler_params=pltpu.CompilerParams(
+            collective_id=3, has_side_effects=True, vmem_limit_bytes=40 << 20
+        ),
+        name="scatter_rows",
+    )(part)
+
+
+GRAD_ORDERS = (("y", "x", "z"), ("y", "z", "x"), ("x", "z", "y"))
+
+
+def grads_kernel(dx, ids, di, do, dg, dd, out, weights_out, *scratch):
+    rows, table, chosen = scratch[:3]
+    held = scratch[3:6]
+    gots = scratch[6:10]
+    weight_gots = scratch[10:19]
+    accs = scratch[19:22]
+    send, recv, local = scratch[22:]
     place = my_place()
-    moves = []
+    moves = [(dx, rows.at[place["y"], place["c"]])]
     for y in range(4):
         lanes = pl.ds(y * 128, 128)
         for z in range(4):
@@ -579,103 +710,35 @@
             moves.append((dd.at[x % 2, :, x // 2, :, lanes], held[2].at[:, x, y, pl.ds(0, 160)]))
             moves.append((do.at[x // 2, :, x % 2, :, lanes], held[0].at[:, x, y, pl.ds(160, 64)]))
         for z in range(4):
-            moves.append(
-                (di.at[z, :, pl.ds(0, 64), lanes], held[1].at[z, :, y, pl.ds(160, 64)])
-            )
-            moves.append(
-                (di.at[z, :, pl.ds(64, 48), lanes], held[2].at[z, :, y, pl.ds(160, 48)])
-            )
+            moves.append((di.at[z, :, pl.ds(0, 64), lanes], held[1].at[z, :, y, pl.ds(160, 64)]))
+            moves.append((di.at[z, :, pl.ds(64, 48), lanes], held[2].at[z, :, y, pl.ds(160, 48)]))
     copies = [pltpu.make_async_copy(src, dst, local.at[k]) for k, (src, dst) in enumerate(moves)]
     for copy in copies:
         copy.start()
-    held[2][:, :, :, 208:224, :] = jnp.zeros((4, 4, 4, 16, 128), held[2].dtype)
-    greet(neighbours(place, core=False))
-    for copy in copies:
-        copy.wait()
-    net = Net(send, recv)
-    scatter_sum(net, place, ORDERS, held, works, [out.at[k] for k in range(3)])
-    net.finish()
-
-
-def scatter_grads(di, do, dg, dd, first, later):
-    rows, lanes = 224, 128
-    scratch = [pltpu.VMEM((4, 4, 4, rows, lanes), first)] * 3
-    for _ in range(3):
-        scratch += work_shapes(rows, lanes, first, later)
-    scratch += [
-        pltpu.SemaphoreType.DMA((SUM_COPIES,)),
-        pltpu.SemaphoreType.DMA((SUM_COPIES,)),
-        pltpu.SemaphoreType.DMA((96,)),
-    ]
-    return pl.pallas_call(
-        grads_kernel,
-        out_shape=jax.ShapeDtypeStruct((3, rows, lanes), F32),
-        in_specs=[ANY] * 4,
-        out_specs=VMEM,
-        scratch_shapes=scratch,
-        compiler_params=pltpu.CompilerParams(
-            collective_id=2, has_side_effects=True, vmem_limit_bytes=56 << 20
-        ),
-        name="scatter_grads",
-    )(di, do, dg, dd)
-
-
-def row_sums_kernel(part, out, *scratch):
-    held = scratch[0:3]
-    works = [dict(zip(WORK_NAMES, scratch[3 + 8 * k : 11 + 8 * k])) for k in range(3)]
-    send, recv, local = scratch[27:]
-    place = my_place()
-    copies = [
-        pltpu.make_async_copy(part.at[:, :, :, :, pl.ds(*lanes)], held[k], local.at[k])
-        for k, lanes in enumerate(LANE_PARTS)
-    ]
-    for copy in copies:
-        copy.start()
-    greet(neighbours(place, core=False))
-    for copy in copies:
-        copy.wait()
-    net = Net(send, recv)
-    outs = [out.at[:, pl.ds(*lanes)] for lanes in LANE_PARTS]
-    scatter_sum(net, place, ORDERS, held, works, outs)
-    net.finish()
-
-
-def scatter_rows(part, first, later):
-    scratch = [pltpu.VMEM((4, 4, 4, 32, lanes), first) for _, lanes in LANE_PARTS]
-    for _, lanes in LANE_PARTS:
-        scratch += work_shapes(32, lanes, first, later)
-    scratch += [
-        pltpu.SemaphoreType.DMA((SUM_COPIES,)),
-        pltpu.SemaphoreType.DMA((SUM_COPIES,)),
-        pltpu.SemaphoreType.DMA((3,)),
-    ]
-    return pl.pallas_call(
-        row_sums_kernel,
-        out_shape=jax.ShapeDtypeStruct((32, DP), F32),
-        in_specs=[ANY],
-        out_specs=VMEM,
-        scratch_shapes=scratch,
-        compiler_params=pltpu.CompilerParams(
-            collective_id=3, has_side_effects=True, vmem_limit_bytes=56 << 20
-        ),
-        name="scatter_rows",
-    )(part)
-
-
-def embed_grad_kernel(dx, ids, out, rows, table, chosen, *scratch):
-    works = [dict(zip(SHALLOW_NAMES, scratch[5 * k : 5 * k + 5])) for k in range(2)]
-    send, recv, local = scratch[10:]
-    place = my_place()
+    held[2][:, :, :, 208:224, :] = jnp.zeros((4, 4, 4, 16, 128), BF16)
     greet(neighbours(place))
-    copy = pltpu.make_async_copy(dx, rows.at[place["y"], place["c"]], local)
-    copy.start()
-    copy.wait()
+    copies[0].wait()
 
     def in_rows(sel, part):
         return rows.at[pick(sel["y"]), sel["c"], pl.ds(*part)]
 
     net = Net(send, recv)
-    gather_streams(net, place, [(("y",), [(in_rows, ((0, 128), (128, 128)))])], True)
+    spread = Spread(net, place, ("y",), [(in_rows, ((0, 128), (128, 128)))], True)
+    spread.begin()
+    for copy in copies[1:]:
+        copy.wait()
+    weight_streams = [
+        start_scatter(
+            net, place, order, held[k], weight_gots[3 * k : 3 * k + 3], weights_out.at[k], accs[k]
+        )
+        for k, order in enumerate(GRAD_ORDERS)
+    ]
+    send_first(weight_streams[2:])
+    spread.relay()
+    spread.near()
+    spread.far()
+    send_first(weight_streams[:2])
+    spread.end()
     base = (place["y"] * 2 + place["c"]) * 16
 
     def parts(count, place_of):
@@ -705,9 +768,17 @@
     def further(axis, step):
         return lax.rem(place[axis] + step, 4)
 
-    sources = [table.at[:, :, pl.ds(0, 192)], table.at[:, :, pl.ds(192, 192)]]
-    outs = [out.at[pl.ds(0, 192)], out.at[pl.ds(192, 192)]]
-    streams = start_scatter(net, place, (("x", "z"), ("z", "x")), sources, works, outs)
+    streams = [
+        start_scatter(
+            net,
+            place,
+            order,
+            table.at[:, :, pl.ds(192 * k, 192)],
+            gots[2 * k : 2 * k + 2],
+            out.at[pl.ds(192 * k, 192)],
+        )
+        for k, order in enumerate((("x", "z"), ("z", "x")))
+    ]
     by_x, by_z = streams[0]["first"], streams[1]["first"]
     parts(4, lambda k: (further("z", 2), further("x", k + 2)))
     for step in FAR_FIRST:
@@ -720,46 +791,155 @@
     by_x[2].send_down()
     by_z[2].send_up()
     by_z[2].send_down()
+    for step in FAR_FIRST:
+        weight_streams[2]["first"][step].pass_on()
     parts(9, lambda k: (further("z", lax.div(k, 3) + 3), further("x", lax.rem(k, 3) + 3)))
     for step in (1, 3, 0):
         by_x[step].send_up()
         by_x[step].send_down()
         by_z[step].send_up()
         by_z[step].send_down()
-    finish_scatter(streams)
+    for step in FAR_FIRST:
+        for stream in streams + weight_streams[:2]:
+            stream["first"][step].pass_on()
+    finish_scatter(streams + weight_streams, passed=True)
     net.finish()
 
 
-def embed_grad(dx, ids):
-    count = SHALLOW_COPIES + 16
+def scatter_grads(dx, ids, di, do, dg, dd):
+    count = 3 * 36 + 2 * 30 + 16
     scratch = [
         pltpu.VMEM((4, 2, 256, DP), BF16),
         pltpu.VMEM((4, 4, 384, DP), BF16),
         pltpu.VMEM((384, 2048), BF16),
     ]
-    for _ in range(2):
-        scratch += shallow_shapes(192, DP, BF16, BF16)
+    scratch += [pltpu.VMEM((4, 4, 4, 224, 128), BF16)] * 3
+    scratch += got_shapes(2, 192, DP, BF16, BF16) * 2
+    scratch += got_shapes(3, 224, 128, BF16, F32) * 3
+    scratch += [pltpu.VMEM((4, 4, 224, 128), F32)] * 3
     scratch += [
         pltpu.SemaphoreType.DMA((count,)),
         pltpu.SemaphoreType.DMA((count,)),
-        pltpu.SemaphoreType.DMA,
+        pltpu.SemaphoreType.DMA((97,)),
     ]
     return pl.pallas_call(
-        embed_grad_kernel,
-        out_shape=jax.ShapeDtypeStruct((384, DP), F32),
-        in_specs=[ANY, VMEM],
-        out_specs=VMEM,
+        grads_kernel,
+        out_shape=[
+            jax.ShapeDtypeStruct((384, DP), F32),
+            jax.ShapeDtypeStruct((3, 224, 128), F32),
+        ],
+        in_specs=[ANY, VMEM] + [ANY] * 4,
+        out_specs=[VMEM, VMEM],
         scratch_shapes=scratch,
         compiler_params=pltpu.CompilerParams(
-            collective_id=6, has_side_effects=True, vmem_limit_bytes=56 << 20
+            collective_id=2, has_side_effects=True, vmem_limit_bytes=60 << 20
         ),
-        name="embed_grad",
-    )(dx, ids)
+        name="scatter_grads",
+    )(dx, ids, di, do, dg, dd)
+
+
+def lanes_of_wide(y, c):
+    return pl.ds(pl.multiple_of((y * 2 + c) * 128, 128), 128)
+
+
+def keys_kernel(own, out, send, recv, local):
+    place = my_place()
+    copy = pltpu.make_async_copy(own, out.at[:, :, lanes_of_wide(place["y"], place["c"])], local)
+    copy.start()
+    greet(neighbours(place, ("y",)))
+    copy.wait()
+
+    def region(sel, rows):
+        return out.at[:, pl.ds(*rows), lanes_of_wide(sel["y"], sel["c"])]
+
+    net = Net(send, recv)
+    gather_streams(net, place, [(("y",), [(region, ((0, 160), (160, 160)))])], True)
+    net.finish()
+
+
+def gather_keys(own):
+    return pl.pallas_call(
+        keys_kernel,
+        out_shape=jax.ShapeDtypeStruct((4, 320, SEQ), BF16),
+        in_specs=[VMEM],
+        out_specs=VMEM,
+        scratch_shapes=[
+            pltpu.SemaphoreType.DMA((14,)),
+            pltpu.SemaphoreType.DMA((14,)),
+            pltpu.SemaphoreType.DMA,
+        ],
+        compiler_params=pltpu.CompilerParams(
+            collective_id=6, has_side_effects=True, vmem_limit_bytes=16 << 20
+        ),
+        name="gather_keys",
+    )(own)
+
+
+def key_sums_kernel(*refs):
+    parts, out = refs[:4], refs[4]
+    theirs, held, got, send, recv = refs[5:]
+    place = my_place()
+    greet(neighbours(place, ("y",)))
+    net = Net(send, recv)
+    swaps = [
+        [
+            net.put(
+                part.at[:, lanes_of_wide(at_step(place, "y", step)["y"], 1 - place["c"])],
+                theirs.at[at_step(place, "y", step)["y"], k],
+                other_core(place),
+            )
+            for k, part in enumerate(parts)
+        ]
+        for step in FAR_FIRST
+    ]
+    ring = Ring(
+        net,
+        place,
+        "y",
+        lambda k, half: held.at[k, pl.ds(2 * half, 2)],
+        lambda k: got.at[k],
+        lambda half: out.at[pl.ds(2 * half, 2)],
+    )
+    for step, swap in zip(FAR_FIRST, swaps):
+        y = at_step(place, "y", step)["y"]
+        for k, part in enumerate(parts):
+            swap[k].wait_recv()
+            own = part[:, lanes_of_wide(y, place["c"])]
+            held[y, k] = (own + theirs[y, k]).astype(BF16)
+        if step == 2:
+            ring.send_across()
+        if step == 1:
+            ring.send_up()
+        if step == 3:
+            ring.send_down()
+    ring.pass_on()
+    ring.close()
+    net.finish()
+
+
+def sum_keys(parts):
+    return pl.pallas_call(
+        key_sums_kernel,
+        out_shape=jax.ShapeDtypeStruct((4, 320, 128), F32),
+        in_specs=[VMEM] * 4,
+        out_specs=VMEM,
+        scratch_shapes=[
+            pltpu.VMEM((4, 4, 320, 128), F32),
+            pltpu.VMEM((4, 4, 320, 128), BF16),
+            pltpu.VMEM((6, 2, 320, 128), BF16),
+            pltpu.SemaphoreType.DMA((22,)),
+            pltpu.SemaphoreType.DMA((22,)),
+        ],
+        compiler_params=pltpu.CompilerParams(
+            collective_id=8, has_side_effects=True, vmem_limit_bytes=32 << 20
+        ),
+        name="sum_keys",
+    )(*parts)
 
 
 def gram_kernel(pieces, turned, gram, part, *scratch):
-    works = [dict(zip(SHALLOW_NAMES, scratch[5 * k : 5 * k + 5])) for k in range(2)]
-    send, recv, local = scratch[10:]
+    gots = scratch[:4]
+    send, recv, local = scratch[4:]
     place = my_place()
     wides = [
         {**at_step(place, "y", step), "c": core}
@@ -790,10 +970,15 @@
 
     orders = (("x", "z"), ("z", "x"))
     lanes = (pl.ds(0, 512), pl.ds(512, 512))
-    sources = [part.at[:, :, :, lane] for lane in lanes]
     mine = gram.at[place["c"], place["z"], place["x"]]
-    outs = [mine.at[:, lane] for lane in lanes]
-    scatter_sum(net, place, orders, sources, works, outs)
+    streams = [
+        start_scatter(
+            net, place, order, part.at[:, :, :, lane], gots[2 * k : 2 * k + 2], mine.at[:, lane]
+        )
+        for k, (order, lane) in enumerate(zip(orders, lanes))
+    ]
+    send_first(streams)
+    finish_scatter(streams)
 
     def in_gram(lane):
         def region(sel, rows):
@@ -809,10 +994,9 @@
 
 
 def gram_of(pieces):
-    count = 7 + SHALLOW_COPIES + 44
+    count = 7 + 2 * 30 + 44
     scratch = [pltpu.VMEM((4, 4, 32, DP), F32)]
-    for _ in range(2):
-        scratch += shallow_shapes(32, 512, F32, F32)
+    scratch += got_shapes(2, 32, 512, F32, F32) * 2
     scratch += [
         pltpu.SemaphoreType.DMA((count,)),
         pltpu.SemaphoreType.DMA((count,)),
@@ -955,14 +1139,18 @@
     meta = jnp.pad(jnp.stack([own_targets, own_counted]), ((0, 6), (0, 128 - MB * PICK)))
 
     table_low = dot(embed_table.astype(BF16), features, 1, 0).astype(BF16)
-    slab = lax.all_gather(table_low, "narrow", axis=0, tiled=True)
     table_other = partner(table_low)
 
     shards = [
         to_shard(master.astype(BF16), rows) for master, rows in zip(masters, (RI, RO, RG, RD))
     ]
-    wi, wo, wg, wd, info = gather_weights(*shards, meta)
-    slab, wi = lax.optimization_barrier((slab, wi))
+    ordered = tokens.reshape(MB, 8, ROWS).swapaxes(0, 1).reshape(2048)
+    mark = jnp.arange(768)
+    marks = jnp.stack([mark // 192 * 384, mark // 192 * 1536]) + mark % 192
+    wi, wo, wg, wd, info, x0 = fetch(
+        *shards, meta, table_low, ordered[:, None], marks.astype(jnp.int32)
+    )
+    x0 = x0.astype(F32)
     wi = wi.reshape(16, RI, DP)[:, :100].reshape(QKV, DP)
     wo = wo.reshape(DP, DP)
     wg = wg.reshape(2 * FF, DP)
@@ -970,14 +1158,6 @@
     info = info.reshape(128, 8, 128)
     all_targets = info[:, 0, : MB * PICK].reshape(4096)
     all_counted = info[:, 1, : MB * PICK].reshape(4096).astype(F32)
-
-    slab_rows = slab.shape[0]
-    ordered = tokens.reshape(MB, 8, ROWS).swapaxes(0, 1).reshape(2048)
-    local_ids = ordered - wide * slab_rows
-    inside = (local_ids >= 0) & (local_ids < slab_rows)
-    safe_ids = jnp.clip(local_ids, 0, slab_rows - 1)
-    looked_up = jnp.where(inside[:, None], slab[safe_ids], jnp.zeros((), BF16))
-    x0 = lax.psum_scatter(looked_up, "wide", scatter_dimension=0, tiled=True).astype(F32)
 
     a = rms_norm(x0, gains[0]).astype(BF16)
     projected = dot(a, wi, 1, 1)
@@ -988,9 +1168,11 @@
         projected[:, H * HD : H * HD + kv_width].reshape(rows_count, KVH, HD), places_all
     ).astype(BF16)
     value_own = projected[:, H * HD + kv_width :].astype(BF16)
-    kv_own = jnp.concatenate([key_own.reshape(rows_count, kv_width), value_own], axis=1)
-    kv_all = lax.all_gather(kv_own, "wide", axis=0, tiled=False)
-    kv_all = kv_all.reshape(8, MB, ROWS, 2 * kv_width)
+    kv_own = [
+        part.reshape(MB, ROWS, kv_width).swapaxes(1, 2)
+        for part in (key_own.reshape(rows_count, kv_width), value_own)
+    ]
+    kv_all = gather_keys(jnp.concatenate(kv_own)).reshape(4, KVH, HD, SEQ)
 
     def allowed_of(batch):
         return (key_places[None, :] <= own_places[:, None]) | (
@@ -1001,16 +1183,15 @@
     mixed_parts = []
     for batch in range(MB):
         q = query.reshape(MB, ROWS, KVH, group_size, HD)[batch]
-        k = kv_all[:, batch, :, :kv_width].reshape(SEQ, KVH, HD)
-        v = kv_all[:, batch, :, kv_width:].reshape(SEQ, KVH, HD)
-        scores = jnp.einsum("qkgd,tkd->kgqt", q, k, preferred_element_type=F32) * scale_factor
+        k, v = kv_all[batch], kv_all[MB + batch]
+        scores = jnp.einsum("qkgd,kdt->kgqt", q, k, preferred_element_type=F32) * scale_factor
         scores = jnp.where(allowed_of(batch), scores, NEGATIVE)
         highest = jnp.max(scores, axis=-1, keepdims=True)
         exp_part = jnp.exp(scores - highest)
         exp_total = jnp.sum(exp_part, axis=-1, keepdims=True)
         log_total = highest + jnp.log(exp_total)
         probs = (exp_part / exp_total).astype(BF16)
-        mixed = jnp.einsum("kgqt,tkd->qkgd", probs, v, preferred_element_type=F32)
+        mixed = jnp.einsum("kgqt,kdt->qkgd", probs, v, preferred_element_type=F32)
         mixed_parts.append(mixed.reshape(ROWS, H * HD).astype(BF16))
         kept.append((q, k, v, log_total))
     o_pad = dot(jnp.concatenate(mixed_parts), features, 1, 0).astype(BF16)
@@ -1050,7 +1231,7 @@
     d_theirs = lax.dynamic_index_in_dim(d_by_core, 1 - core, 1, keepdims=False).reshape(2048, 384)
     d_theirs = partner(d_theirs)
     row_part = dot(d_mine, table_low, 1, 0) + dot(d_theirs, table_other, 1, 0)
-    d_rows = scatter_rows(row_part.astype(BF16).reshape(4, 4, 4, 32, DP), BF16, F32)
+    d_rows = scatter_rows(row_part.astype(BF16).reshape(4, 4, 4, 32, DP))
 
     d_final = jnp.zeros((rows_count, DP), F32).at[own_offsets].add(d_rows)
     d_x2, d_gain_final = jax.vjp(rms_norm, x2, gains[2])[1](d_final)
@@ -1067,26 +1248,22 @@
     for batch in range(MB):
         q, k, v, log_sum = kept[batch]
         d_m = d_mixed.reshape(MB, ROWS, KVH, group_size, HD)[batch]
-        scores = jnp.einsum("qkgd,tkd->kgqt", q, k, preferred_element_type=F32) * scale_factor
+        scores = jnp.einsum("qkgd,kdt->kgqt", q, k, preferred_element_type=F32) * scale_factor
         scores = jnp.where(allowed_of(batch), scores, NEGATIVE)
         probs = jnp.exp(scores - log_sum)
-        d_probs = jnp.einsum("qkgd,tkd->kgqt", d_m, v, preferred_element_type=F32)
+        d_probs = jnp.einsum("qkgd,kdt->kgqt", d_m, v, preferred_element_type=F32)
         d_scores = (
             probs * (d_probs - jnp.sum(probs * d_probs, axis=-1, keepdims=True))
         ).astype(BF16)
-        d_q = jnp.einsum("kgqt,tkd->qkgd", d_scores, k, preferred_element_type=F32) * scale_factor
-        d_k = jnp.einsum("kgqt,qkgd->tkd", d_scores, q, preferred_element_type=F32) * scale_factor
+        d_q = jnp.einsum("kgqt,kdt->qkgd", d_scores, k, preferred_element_type=F32) * scale_factor
+        d_k = jnp.einsum("kgqt,qkgd->kdt", d_scores, q, preferred_element_type=F32) * scale_factor
         d_v = jnp.einsum(
-            "kgqt,qkgd->tkd", probs.astype(BF16), d_m, preferred_element_type=F32
+            "kgqt,qkgd->kdt", probs.astype(BF16), d_m, preferred_element_type=F32
         )
         d_queries.append(d_q.reshape(ROWS, H, HD))
-        d_kv.append(
-            jnp.concatenate(
-                [d_k.reshape(8, ROWS, kv_width), d_v.reshape(8, ROWS, kv_width)], axis=2
-            )
-        )
-    d_kv_all = jnp.stack(d_kv, axis=1).reshape(8 * rows_count, 2 * kv_width)
-    d_kv_own = lax.psum_scatter(d_kv_all, "wide", scatter_dimension=0, tiled=True)
+        d_kv.append((d_k.reshape(kv_width, SEQ), d_v.reshape(kv_width, SEQ)))
+    d_kv_own = sum_keys([d_kv[0][0], d_kv[1][0], d_kv[0][1], d_kv[1][1]])
+    d_kv_own = d_kv_own.swapaxes(1, 2).reshape(2, rows_count, kv_width)
 
     def unrotate(gradient, heads):
         primal = jnp.zeros((rows_count, heads, HD), F32)
@@ -1095,10 +1272,10 @@
     d_projected = jnp.concatenate(
         [
             unrotate(jnp.concatenate(d_queries), H).reshape(rows_count, H * HD),
-            unrotate(d_kv_own[:, :kv_width].reshape(rows_count, KVH, HD), KVH).reshape(
+            unrotate(d_kv_own[0].reshape(rows_count, KVH, HD), KVH).reshape(
                 rows_count, kv_width
             ),
-            d_kv_own[:, kv_width:],
+            d_kv_own[1],
         ],
         axis=1,
     ).astype(BF16)
@@ -1119,13 +1296,13 @@
     grad_wg = dot(both(d_gate_up), half_pair(b), 0, 0).astype(BF16)
     grad_wo = dot(both(d_out), half_pair(o_pad), 0, 0).astype(BF16)
     grad_wi = dot(both(d_projected_pad), half_pair(a), 0, 0).astype(BF16)
-    summed_grads = scatter_grads(
+    table_grad, summed_grads = scatter_grads(
+        d_x0,
+        ordered[None, :],
         grad_wi.reshape(4, 4, RI, 512),
         grad_wo.reshape(2, 4, 2, RO, 512),
         grad_wg.reshape(2, 2, 2, 4, 160, 512),
         grad_wd.reshape(2, 4, 2, 160, 512),
-        BF16,
-        F32,
     )
     grad_shards = (
         jnp.concatenate([summed_grads[1, 160:224], summed_grads[2, 160:208]]),
@@ -1134,7 +1311,6 @@
         summed_grads[2, :160],
     )
 
-    table_grad = embed_grad(d_x0, ordered[None, :])
     table_grad = dot(table_grad + table_grad_rows, features, 1, 1, HIGHEST)
 
     squares = sum(jnp.sum(shard * shard) for shard in grad_shards) + jnp.sum(
@@ -1163,10 +1339,11 @@
     identity = jnp.eye(DP, dtype=F32)
     for ns_step in range(ITERS):
         if ns_step < ITERS - 1:
-            square = dot(gram, gram, 1, 0, HIGH)
+            fine = HIGHEST if ns_step == 0 else HIGH
+            square = dot(gram, gram, 1, 0, fine)
             step_matrix = NS_A * identity + NS_B * gram + NS_C * square
             current = dot(current, step_matrix, 1, 0, HIGH)
-            gram = dot(dot(step_matrix, gram, 1, 0, HIGH), step_matrix, 1, 0, HIGH)
+            gram = dot(dot(step_matrix, gram, 1, 0, fine), step_matrix, 1, 0, fine)
         else:
             applied = dot(current, gram, 1, 0, HIGH)
             current = NS_A * current + NS_B * applied + NS_C * dot(applied, gram, 1, 0, HIGH)

time: 1020 us -> 938 us (0.920)
  Pallas kernels: 427 us -> 523 us
  waiting for transfers between devices: 85.6 us -> 0.03 us
  local copies, waits for them, and re-layouts: 149 us -> 64.1 us
  matrix products: 221 us -> 245 us
  between operations: 28.3 us -> 15.2 us
  other arithmetic: 84.4 us -> 72.2 us
    pallas_call x3 -> x4, Pallas kernels: 266 us -> 368 us  [the longest x1 183 us: fetch(): pl.pallas_call(fetch_kernel, out_shape=shapes, in_specs=[ANY] * 6 + [VMEM...]
    all_gather x2 -> x0, waiting for transfers between devices: 58.1 us -> none  [the longest x1 31.1 us: body(): slab = lax.all_gather(table_low, 'narrow', axis=0, tiled=True)]
    reduce_scatter x2 -> x0, waiting for transfers between devices: 26.7 us -> none  [the longest x1 26.7 us: body(): lax.psum_scatter(looked_up, 'wide', scatter_dimension=0, tiled=True)]
    slice x7 -> x3, local copies, waits for them, and re-layouts: 23.2 us -> 0.61 us  [the longest x1 0.34 us: body(): k, v = (kv_all[batch], kv_all[MB + batch])]
    dot_general x39, matrix products: 189 us -> 211 us  [dot(): lax.dot_general(left, right, (((left_axis,), (right_axis,)), ((), ())), p...]
    gather x1 -> x0, local copies, waits for them, and re-layouts: 17.1 us -> none  [body(): looked_up = jnp.where(inside[:, None], slab[safe_ids], jnp.zeros((), BF16))]
    optimization_barrier x1 -> x0, local copies, waits for them, and re-layouts: 16.6 us -> none  [body(): slab, wi = lax.optimization_barrier((slab, wi))]
    reshape x5 -> x0, local copies, waits for them, and re-layouts: 16 us -> none  [the longest x2 5.88 us: body(): d_k.reshape(8, ROWS, kv_width)]
  transfers between devices with their start and end apart: 15 -> 11, of which waited for: 4 -> 0; matrix products, arithmetic and copies ran while one was open for 10% -> 22% of each run, Pallas kernels for 20% -> 31%
where the time goes in v3:
time: 938 us; the launch traced here: 934 us
  Pallas kernels  523 us (56%)
  matrix products  245 us (26%)
  other arithmetic  72.2 us (8%)
  local copies, waits for them, and re-layouts  64.1 us (7%)
  between operations  15.2 us (2%)
  starting transfers between devices  14.7 us (2%)
    dot_general x39, matrix products, dot(): lax.dot_general(left, right, (((left_axis,), (right_axis,)), ((), ())), p...  211 us
    pallas_call x1, Pallas kernels, fetch(): pl.pallas_call(fetch_kernel, out_shape=shapes, in_specs=[ANY] * 6 + [VMEM...  183 us
    pallas_call x1, Pallas kernels, scatter_grads(): pl.pallas_call(grads_kernel, out_shape=[jax.ShapeDtypeStruct((384, DP), F...  155 us
    pallas_call x1, Pallas kernels, gram_of(): pl.pallas_call(gram_kernel, out_shape=[jax.ShapeDtypeStruct((320, DP), F3...  61.4 us
    pallas_call x1, Pallas kernels, gather_rows(): pl.pallas_call(rows_kernel, out_shape=jax.ShapeDtypeStruct((4, 4, 4, 2, 3...  34 us
    pallas_call x1, Pallas kernels, scatter_rows(): pl.pallas_call(row_sums_kernel, out_shape=jax.ShapeDtypeStruct((32, DP),...  30.3 us
    pallas_call x2, Pallas kernels, small_all(): pl.pallas_call(functools.partial(small_kernel, combine, last), out_shape=...  28.5 us
    unnamed x296, local copies, waits for them, and re-layouts  23.2 us
  transfers between devices with their start and end apart: 11, of which 0 were waited for; matrix products, arithmetic and copies ran while one was open for 22% of the time, Pallas kernels for 31%

profile of v3, /device:TPU:1, one launch (start us, length us, event | category | flops | bytes accessed | tf_op | source)
XLA Modules:
  0.0 933.6 jit_solution(17486716184233879609)
XLA Ops:
  19.0 182.7 %fetch.1 = (bf16[4,4,112,1024]{3,2,1,0:T(8,128)(2,1)}, bf16[2,4,2,64,1024]{4,3,2,1,0:T(8,128)(2,1)}, bf16[2,2,2,4,160,1024]{5,4,3,2,1,0:T(8,128)(2,1)}, bf16[2,4...) custom-call(bf16[112,128]{1,0:T(8,128)(2,1)} %copy.58.gi, ...), custom_call_target="tpu_custom_call" | custom-call | tf_op jit(solution)/shard_map/fetch/pallas_call | solution.py:358
  215.2 14.4 %gather_keys.1 = bf16[4,320,1024]{2,1,0:T(8,128)(2,1)S(1)} custom-call(bf16[4,320,128]{2,1,0:T(8,128)(2,1)S(1)} %pad_maximum_fusion.5.own), custom_call_target="tpu_custom_call" | custom-call | tf_op jit(solution)/shard_map/gather_keys/pallas_call | solution.py:861
  244.8 6.0 fusion.299
  263.5 34.0 %gather_rows.1 = bf16[4,4,4,2,32,1024]{5,4,3,2,1,0:T(8,128)(2,1)S(1)} custom-call(bf16[32,1024]{1,0:T(8,128)(2,1)S(1)} %gather_fusion), custom_call_target="tpu_custom_call" | custom-call | tf_op jit(solution)/shard_map/gather_rows/pallas_call | solution.py:413
  297.5 6.3 fusion.297
  312.3 14.3 %row_totals.1 = f32[32,128]{1,0:T(8,128)} custom-call(f32[2,32,128]{2,1,0:T(8,128)} %pad_maximum_fusion.10.own), custom_call_target="tpu_custom_call" | custom-call | tf_op jit(solution)/shard_map/row_totals/pallas_call | solution.py:462
  327.3 7.7 multiply_convert_fusion
  360.1 7.4 fusion.301
  375.6 30.3 %scatter_rows.1 = f32[32,1024]{1,0:T(8,128)S(1)} custom-call(bf16[4,4,4,32,1024]{4,3,2,1,0:T(8,128)(2,1)S(1)} %bitcast.406), custom_call_target="tpu_custom_call" | custom-call | tf_op jit(solution)/shard_map/scatter_rows/pallas_call | solution.py:674
  408.2 6.6 fusion.151
  437.3 8.1 fusion.1
  445.4 7.3 fusion.3
  466.3 7.5 fusion.6
  476.8 16.8 %sum_keys.1 = f32[4,320,128]{2,1,0:T(8,128)S(1)} custom-call(f32[320,1024]{1,0:T(8,128)S(1)} %bitcast.408, f32[320,1024]{1,0:T(8,128)S(1)} %bitcast.407, f32[320,1024]{1,0:T(8,128)S(1)} %bitcast.410, f32[320,1024]{1,0:T(8,128)S(1)} %bitcast.409), custom_call_target="tpu_custom_call" | custom-call | tf_op jit(solution)/shard_map/sum_keys/pallas_call | solution.py:921
  515.9 7.8 convolution_convert_fusion
  523.7 154.5 %scatter_grads.1 = (f32[384,1024]{1,0:T(8,128)}, f32[3,224,128]{2,1,0:T(8,128)}) custom-call(bf16[256,1024]{1,0:T(8,128)(2,1)} %fusion.145.dx, s32[1,2048]{1,0:T(1,128)} %bitcast.490, bf16[4,4,112,512]{3,2,1,0:T(8,128)(2,1)} %bitcast.451, bf16[2,4,2,64,512]{4,3,2,1,0:T(8,128)(2,1)} %bitcast.458, bf16[2,2,2,4,160,512]{5,4,3,2,1,0:T(8,128)(2,1)} %bitcast.426, ...), custom_call_target="tpu_custom_call" | custom-call | tf_op jit(solution)/shard_map/scatter_grads/pallas_call | solution.py:825
  682.0 7.5 multiply_reduce_fusion.2
  696.0 14.3 %global_sums.1 = f32[32,128]{1,0:T(8,128)} custom-call(f32[32,128]{1,0:T(8,128)} %select_maximum_fusion.own), custom_call_target="tpu_custom_call" | custom-call | tf_op jit(solution)/shard_map/global_sums/pallas_call | solution.py:462
  720.2 61.4 %gram_sums.1 = (f32[320,1024]{1,0:T(8,128)S(1)}, f32[2,4,4,32,1024]{4,3,2,1,0:T(8,128)S(1)}) custom-call(f32[4,320,128]{2,1,0:T(8,128)S(1)} %pad_maximum_fusion.2.pieces), custom_call_target="tpu_custom_call" | custom-call | tf_op jit(solution)/shard_map/gram_sums/pallas_call | solution.py:1005
  789.1 14.1 %fusion.302 = f32[1024,1024]{1,0:T(8,128)S(1)} fusion(f32[1024,1024]{1,0:T(8,128)S(1)} %bitcast.431), kind=kOutput, calls=%fused_computation.499 | convolution fusion | flops 12884901888 | bytes 8388608 | tf_op jit(solution)/shard_map/dot_general | solution.py:1055
  803.3 14.2 %fusion.71 = f32[1024,1024]{1,0:T(8,128)S(1)} fusion(f32[1024,1024]{1,0:T(8,128)S(1)} %bitcast.432, f32[1024,1024]{1,0:T(8,128)S(1)} %fusion.302), kind=kOutput, calls=%fused_computation.104 | convolution fusion | flops 12891193344 | bytes 12582912 | tf_op jit(solution)/shard_map/dot_general | solution.py:1055
  817.4 14.2 %fusion.69 = f32[1024,1024]{1,0:T(8,128)S(1)} fusion(f32[1024,1024]{1,0:T(8,128)S(1)} %fusion.71, f32[1024,1024]{1,0:T(8,128)S(1)} %fusion.302, f32[1024,1024]{1,0:T(8,128)S(1)} %bitcast.433), kind=kOutput, calls=%fused_computation.103 | convolution fusion | flops 12891193344 | bytes 16777216 | tf_op jit(solution)/shard_map/dot_general | solution.py:1055
  831.6 7.0 fusion.303
  838.7 7.5 fusion.65
  850.0 7.1 fusion.63
  857.1 7.0 fusion.304
  864.1 7.3 fusion.59
  873.3 6.9 fusion.57
  880.2 7.4 fusion.305
  887.7 7.0 fusion.53
  896.8 6.9 fusion.51
  918.9 5.3 fusion.282
  (552 shorter events, 211.6 us)
Async XLA Ops:
  0.9 15.3 %copy-start.46 = (f32[1,120,320]{1,2,0:T(8,128)S(1)}, f32[1,120,320]{1,2,0:T(8,128)}, u32[]{:S(2)}) copy-start(f32[1,120,320]{1,2,0:T(8,128)} %param.24) | copy-start | bytes 460804
  5.6 366.0 %collective-permute-start.1 = (bf16[384,1024]{1,0:T(8,128)(2,1)}, bf16[384,1024]{1,0:T(8,128)(2,1)}, u32[]{:S(2)}, u32[]{:S(2)}) collective-permute-start(bf16[384,1024]{1,0:T(8,128)(2,1)} %bitcast.12.table), channel_id=1, source_target_pairs={{0,16},{16,0},{32,48},{48,32},{64,80},{80,64},{96,112},{112,96},{1... | collective-permute-start | bytes 2359304 | tf_op jit(solution)/shard_map/ppermute | solution.py:1095
  11.2 190.5 %copy-start.70 = (s32[2,8,128]{2,0,1:T(2,128)}, s32[2,8,128]{2,0,1:T(2,128)S(1)}, u32[]{:S(2)}) copy-start(s32[2,8,128]{2,0,1:T(2,128)S(1)} %copy.57) | copy-start | bytes 24580
  13.4 195.2 %copy-start.77 = (f32[1024]{0:T(1024)}, f32[1024]{0:T(1024)S(1)}, u32[]{:S(2)}) copy-start(f32[1024]{0:T(1024)S(1)} %mul.941) | copy-start | bytes 12292
  213.9 30.7 %copy-start.79 = (f32[1024]{0:T(1024)}, f32[1024]{0:T(1024)S(1)}, u32[]{:S(2)}) copy-start(f32[1024]{0:T(1024)S(1)} %mul.966) | copy-start | bytes 12292
  215.1 16.7 %copy-start.23 = (bf16[128,15,64]{0,2,1:T(8,128)(2,1)}, bf16[128,15,64]{0,2,1:T(8,128)(2,1)S(1)}, u32[]{:S(2)}) copy-start(bf16[128,15,64]{0,2,1:T(8,128)(2,1)S(1)} %get-tuple-element.119) | copy-start | bytes 737284
  215.1 21.2 %copy-start.21 = (bf16[128,15,64]{0,2,1:T(8,128)(2,1)}, bf16[128,15,64]{0,2,1:T(8,128)(2,1)S(1)}, u32[]{:S(2)}) copy-start(bf16[128,15,64]{0,2,1:T(8,128)(2,1)S(1)} %get-tuple-element.118) | copy-start | bytes 737284
  254.9 249.5 %collective-permute-start.8 = (bf16[256,2560]{1,0:T(8,128)(2,1)}, bf16[256,2560]{1,0:T(8,128)(2,1)}, u32[]{:S(2)}, u32[]{:S(2)}) collective-permute-start(bf16[256,2560]{1,0:T(8,128)(2,1)} %multiply_convert_fusion.1), channel_id=1, source_target_pairs={{0,16},{16,0},{32,48},{48,32},{64,80},{80,64},{96,112},{112,96},{1... | collective-permute-start | bytes 3932168 | tf_op jit(solution)/shard_map/ppermute | solution.py:1095
  261.7 35.7 %copy-start.100 = (f32[256]{0:T(256)}, f32[256]{0:T(256)S(1)}, u32[]{:S(2)}) copy-start(f32[256]{0:T(256)S(1)} %get-tuple-element.155) | copy-start | bytes 3076
  261.8 35.7 %copy-start.82 = (f32[256]{0:T(256)}, f32[256]{0:T(256)S(1)}, u32[]{:S(2)}) copy-start(f32[256]{0:T(256)S(1)} %fusion.215) | copy-start | bytes 3076
  335.0 14.5 %copy-start.54 = (f32[32,128]{1,0:T(8,128)S(1)}, f32[32,128]{1,0:T(8,128)}, u32[]{:S(2)}) copy-start(f32[32,128]{1,0:T(8,128)} %row_totals.1) | copy-start | bytes 49156
  335.0 16.8 %copy-start.74 = (f32[1,120,100]{1,0,2:T(1,128)S(1)}, f32[1,120,100]{1,0,2:T(1,128)}, u32[]{:S(2)}) copy-start(f32[1,120,100]{1,0,2:T(1,128)} %param.28) | copy-start | bytes 144004
  337.2 34.4 %collective-permute-start = (bf16[2048,384]{1,0:T(8,128)(2,1)}, bf16[2048,384]{1,0:T(8,128)(2,1)}, u32[]{:S(2)}, u32[]{:S(2)}) collective-permute-start(bf16[2048,384]{1,0:T(8,128)(2,1)} %bitcast.59), channel_id=1, source_target_pairs={{0,16},{16,0},{32,48},{48,32},{64,80},{80,64},{96,112},{112,96},{1... | collective-permute-start | bytes 4718600 | tf_op jit(solution)/shard_map/ppermute | solution.py:1095
  375.6 32.0 %copy-start.6 = (f32[256,1024]{1,0:T(8,128)S(1)}, f32[256,1024]{1,0:T(8,128)}, u32[]{:S(2)}) copy-start(f32[256,1024]{1,0:T(8,128)} %copy-done.5) | copy-start | bytes 3145732
  375.6 32.0 %copy-start.83 = (f32[256]{0:T(256)S(1)}, f32[256]{0:T(256)}, u32[]{:S(2)}) copy-start(f32[256]{0:T(256)} %copy-done.82) | copy-start | bytes 3076
  375.6 32.3 %copy-start.101 = (f32[256]{0:T(256)S(1)}, f32[256]{0:T(256)}, u32[]{:S(2)}) copy-start(f32[256]{0:T(256)} %copy-done.100) | copy-start | bytes 3076
  428.0 82.6 %collective-permute-start.4 = (bf16[256,1024]{1,0:T(8,128)(2,1)}, bf16[256,1024]{1,0:T(8,128)(2,1)}, u32[]{:S(2)}, u32[]{:S(2)}) collective-permute-start(bf16[256,1024]{1,0:T(8,128)(2,1)} %get-tuple-element.88), channel_id=1, source_target_pairs={{0,16},{16,0},{32,48},{48,32},{64,80},{80,64},{96,112},{112,96},{1... | collective-permute-start | bytes 1572872 | tf_op jit(solution)/shard_map/ppermute | solution.py:1095
  431.5 84.3 %collective-permute-start.6 = (bf16[256,5120]{1,0:T(8,128)(2,1)}, bf16[256,5120]{1,0:T(8,128)(2,1)}, u32[]{:S(2)}, u32[]{:S(2)}) collective-permute-start(bf16[256,5120]{1,0:T(8,128)(2,1)} %add_convert_fusion.1), channel_id=1, source_target_pairs={{0,16},{16,0},{32,48},{48,32},{64,80},{80,64},{96,112},{112,96},{1... | collective-permute-start | bytes 7864328 | tf_op jit(solution)/shard_map/ppermute | solution.py:1095
  476.1 18.8 %copy-start.40 = (f32[256,64]{0,1:T(8,128)S(1)}, f32[256,64]{0,1:T(8,128)}, u32[]{:S(2)}) copy-start(f32[256,64]{0,1:T(8,128)} %copy-done.39) | copy-start | bytes 196612
  476.1 28.4 %collective-permute-start.9 = (bf16[256,512]{1,0:T(8,128)(2,1)}, bf16[256,512]{1,0:T(8,128)(2,1)}, u32[]{:S(2)}, u32[]{:S(2)}) collective-permute-start(bf16[256,512]{1,0:T(8,128)(2,1)} %get-tuple-element.107), channel_id=1, source_target_pairs={{0,16},{16,0},{32,48},{48,32},{64,80},{80,64},{96,112},{112,96},{1... | collective-permute-start | bytes 786440 | tf_op jit(solution)/shard_map/ppermute | solution.py:1095
  476.8 18.2 %copy-start.18 = (f32[5,64,3,128]{3,1,2,0:T(8,128)S(1)}, f32[5,64,3,128]{3,1,2,0:T(8,128)}, u32[]{:S(2)}) copy-start(f32[5,64,3,128]{3,1,2,0:T(8,128)} %convolution_multiply_fusion.1) | copy-start | bytes 1474564
  502.6 10.9 %collective-permute-start.2 = (bf16[256,1792]{1,0:T(8,128)(2,1)S(1)}, bf16[256,1792]{1,0:T(8,128)(2,1)S(1)}, u32[]{:S(2)}, u32[]{:S(2)}) collective-permute-start(bf16[256,1792]{1,0:T(8,128)(2,1)S(1)} %fusion.79), channel_id=1, source_target_pairs={{0,16},{16,0},{32,48},{48,32},{64,80},{80,64},{96,112},{112,96},{1... | collective-permute-start | bytes 2752520 | tf_op jit(solution)/shard_map/ppermute | solution.py:1095
  504.5 9.0 collective-permute-start.3
  504.5 5.4 collective-permute-start.5
  509.9 5.9 collective-permute-start.7
  523.7 158.3 %copy-start.41 = (f32[384,1024]{1,0:T(8,128)S(1)}, f32[384,1024]{1,0:T(8,128)}, u32[]{:S(2)}) copy-start(f32[384,1024]{1,0:T(8,128)} %fusion.301) | copy-start | bytes 4718596
  523.7 158.3 %copy-start.111 = (s32[960]{0:T(1024)S(1)}, s32[960]{0:T(1024)}, u32[]{:S(2)}) copy-start(s32[960]{0:T(1024)} %copy-done.108) | copy-start | bytes 11524
  523.7 158.3 %copy-start.115 = (s32[960]{0:T(1024)S(1)}, s32[960]{0:T(1024)}, u32[]{:S(2)}) copy-start(s32[960]{0:T(1024)} %copy-done.112) | copy-start | bytes 11524
  523.7 158.3 %copy-start.122 = (pred[960]{0:T(1024)(128)(4,1)S(1)}, pred[960]{0:T(1024)(128)(4,1)}, u32[]{:S(2)}) copy-start(pred[960]{0:T(1024)(128)(4,1)} %copy-done.119) | copy-start | bytes 2884
  523.7 158.3 %copy-start.126 = (pred[960]{0:T(1024)(128)(4,1)S(1)}, pred[960]{0:T(1024)(128)(4,1)}, u32[]{:S(2)}) copy-start(pred[960]{0:T(1024)(128)(4,1)} %copy-done.123) | copy-start | bytes 2884
  715.9 67.7 %copy-start.71 = (s32[2,4,4,32]{3,2,1,0:T(4,128)S(1)}, s32[2,4,4,32]{3,2,1,0:T(4,128)}, u32[]{:S(2)}) copy-start(s32[2,4,4,32]{3,2,1,0:T(4,128)} %multiply_add_fusion.4) | copy-start | bytes 12292
  908.5 15.7 %all-to-all-start = ((f32[8,160,128]{2,1,0:T(8,128)}), f32[8,160,128]{2,1,0:T(8,128)S(1)}, u32[]{:S(2)}, u32[]{:S(2)}) async-start(f32[8,160,128]{2,1,0:T(8,128)} %bitcast.135), calls=%async_computation | async-start | bytes 1310720 | tf_op jit(solution)/shard_map/all_to_all | solution.py:1351
  (118 other events, 567.4 us)

commit v4 on v3

--- a/solution.py
+++ b/solution.py
@@ -195,9 +195,9 @@
 
 
 def fetch_kernel(
-    gi, go, gg, gd, meta, table, ids, marks, wi, wo, wg, wd, info, x0, *scratch
+    gi, go, gg, gd, meta, table, ids, wi, wo, wg, wd, info, x0, *scratch
 ):
-    slab_x, slab_z, total, chosen, packed, theirs, got, send, recv, local = scratch
+    slab, packed, theirs, got, send, recv, local = scratch
     place = my_place()
 
     def in_wi(sel, rows):
@@ -231,8 +231,8 @@
         (gg.at[pl.ds(160, 160)], in_wg(1)(place, (0, 160))),
         (gd, in_wd(place, (0, RD))),
         (meta, in_info(place, None)),
-        (table.at[pl.ds(0, 192)], slab_x.at[place["z"], place["x"]]),
-        (table.at[pl.ds(192, 192)], slab_z.at[place["x"], place["z"]]),
+        (table.at[pl.ds(0, 192)], slab.at[pl.ds((place["z"] * 4 + place["x"]) * 192, 192)]),
+        (table.at[pl.ds(192, 192)], slab.at[pl.ds((16 + place["x"] * 4 + place["z"]) * 192, 192)]),
     ]
     copies = [pltpu.make_async_copy(src, dst, local.at[k]) for k, (src, dst) in enumerate(owns)]
     for copy in copies:
@@ -241,22 +241,20 @@
         copy.wait()
     greet(neighbours(place))
     net = Net(send, recv)
-    rows = ((0, 96), (96, 96))
+    slab[pl.ds(6144, 8)] = jnp.zeros((8, 8, 128), BF16)
+
+    def in_slab(major, minor, first):
+        def region(sel, half):
+            start = (first + sel[major] * 4) * 192
+            if sel[minor] is None:
+                return slab.at[pl.ds(start + half * 384, 384)]
+            return slab.at[pl.ds(start + sel[minor] * 192 + half * 96, 96)]
+
+        return region
+
     tables = [
-        Spread(
-            net,
-            place,
-            ("x", "z"),
-            [(lambda sel, part: slab_x.at[pick(sel["z"]), pick(sel["x"]), pl.ds(*part)], rows)],
-            False,
-        ),
-        Spread(
-            net,
-            place,
-            ("z", "x"),
-            [(lambda sel, part: slab_z.at[pick(sel["x"]), pick(sel["z"]), pl.ds(*part)], rows)],
-            False,
-        ),
+        Spread(net, place, ("x", "z"), [(in_slab("z", "x", 0), (0, 1))], False),
+        Spread(net, place, ("z", "x"), [(in_slab("x", "z", 16), (0, 1))], False),
     ]
     weights = [
         Spread(net, place, axes, items, True)
@@ -275,99 +273,65 @@
             for spread in spreads:
                 getattr(spread, step)()
 
-    base = (place["y"] * 2 + place["c"]) * (16 * 384)
-
-    def look_up(slab, index, kind, start, initial):
-        @pl.loop(0, 16)
-        def _(r):
-            part = pl.ds(pl.multiple_of(r * 128, 128), 128)
-            wanted = ids[part, :] - start
-            chosen[part, :] = (marks[kind : kind + 1, :] == wanted).astype(F32).astype(BF16)
-
-        @pl.loop(0, 8)
-        def _(k):
-            part = pl.ds(pl.multiple_of(lax.div(k, 4) * 1024, 1024), 1024)
-            lanes = pl.ds(pl.multiple_of(lax.rem(k, 4) * 256, 256), 256)
-            block = slab[index, :, :, lanes].reshape(768, 256)
-            found = jnp.dot(chosen[part, :], block, preferred_element_type=F32)
-            total[part, lanes] = found if initial else total[part, lanes] + found
-
-    def by_x(step, initial=False):
-        z = lax.rem(place["z"] + step, 4)
-        look_up(slab_x, z, 0, base + z * (4 * 384), initial)
-
-    def by_z(step):
-        x = lax.rem(place["x"] + step, 4)
-        look_up(slab_z, x, 1, base + x * 384 + 192, False)
-
     each(tables, "begin")
     each(weights, "begin")
     each(tables, "relay")
     each(weights, "relay")
     each(tables, "near", "far", "begin")
     each(weights, "near", "far", "begin")
-    by_x(0, True)
-    by_z(0)
     each(tables, "relay")
     each(weights, "relay", "near", "far", "begin")
-    each(tables, "near")
-    by_x(1)
-    by_x(3)
+    each(tables, "near", "far")
+
+    @pl.loop(0, 128)
+    def _(block):
+        for k in range(16):
+            token = block * 16 + k
+            packed[token] = slab[ids[token]]
+
+    swap = net.put(
+        packed.at[pl.ds((1 - place["c"]) * 1024, 1024)], theirs, other_core(place)
+    )
     each(weights, "relay")
-    by_z(1)
-    by_z(3)
-    each(tables, "far")
-    by_x(2)
-    each(weights, "near")
-    by_z(2)
-    for y in range(4):
-        for c in range(2):
-            packed[c, y] = total[(y * 2 + c) * 256 : (y * 2 + c + 1) * 256, :].astype(BF16)
-    swap = net.put(packed.at[1 - place["c"]], theirs, other_core(place))
     swap.wait_recv()
-    mine = packed.at[place["c"]]
-    for y in range(4):
-        add_up(theirs.at[y], [mine.at[y], theirs.at[y]])
-    halves = (pl.ds(0, 128), pl.ds(128, 128))
+    add_up(theirs, [packed.at[pl.ds(place["c"] * 1024, 1024)], theirs])
     ring = Ring(
         net,
         place,
         "y",
-        lambda k, half: theirs.at[k, halves[half]],
+        lambda k, half: theirs.at[pl.ds(k * 256 + half * 128, 128)],
         lambda k: got.at[k],
-        lambda half: x0.at[halves[half]],
+        lambda half: x0.at[pl.ds(half * 128, 128)],
     )
     ring.send_all()
+    each(weights, "near")
+    ring.pass_on()
     each(weights, "far")
-    ring.pass_on()
     ring.close()
     each(weights, "end")
     net.finish()
 
 
-def fetch(gi, go, gg, gd, meta, table, ids, marks):
+def fetch(gi, go, gg, gd, meta, table, ids):
     shapes = [
         jax.ShapeDtypeStruct((4, 4, RI, DP), BF16),
         jax.ShapeDtypeStruct((2, 4, 2, RO, DP), BF16),
         jax.ShapeDtypeStruct((2, 2, 2, 4, 160, DP), BF16),
         jax.ShapeDtypeStruct((2, 4, 2, 160, DP), BF16),
         jax.ShapeDtypeStruct((4, 4, 4, 2, 8, 128), jnp.int32),
-        jax.ShapeDtypeStruct((256, DP), BF16),
-    ]
-    count = 210
+        jax.ShapeDtypeStruct((256, 8, 128), BF16),
+    ]
+    count = 202
     return pl.pallas_call(
         fetch_kernel,
         out_shape=shapes,
-        in_specs=[ANY] * 6 + [VMEM] * 2,
+        in_specs=[ANY] * 6 + [pl.BlockSpec(memory_space=pltpu.SMEM)],
         out_specs=[ANY] * 5 + [VMEM],
         scratch_shapes=[
-            pltpu.VMEM((4, 4, 192, DP), BF16),
-            pltpu.VMEM((4, 4, 192, DP), BF16),
-            pltpu.VMEM((2048, DP), F32),
-            pltpu.VMEM((2048, 768), BF16),
-            pltpu.VMEM((2, 4, 256, DP), BF16),
-            pltpu.VMEM((4, 256, DP), BF16),
-            pltpu.VMEM((6, 128, DP), BF16),
+            pltpu.VMEM((6152, 8, 128), BF16),
+            pltpu.VMEM((2048, 8, 128), BF16),
+            pltpu.VMEM((1024, 8, 128), BF16),
+            pltpu.VMEM((6, 128, 8, 128), BF16),
             pltpu.SemaphoreType.DMA((count,)),
             pltpu.SemaphoreType.DMA((count,)),
             pltpu.SemaphoreType.DMA((8,)),
@@ -376,7 +340,7 @@
             collective_id=0, has_side_effects=True, vmem_limit_bytes=56 << 20
         ),
         name="fetch",
-    )(gi, go, gg, gd, meta, table, ids, marks)
+    )(gi, go, gg, gd, meta, table, ids)
 
 
 LANE_PARTS = ((0, 384), (384, 384), (768, 256))
@@ -427,46 +391,49 @@
     )(own)
 
 
-HOPS = (("c", 2), ("x", 4), ("y", 4), ("z", 4))
-
-
-def small_kernel(combine, last, own, out, held, slots, send, recv):
+def small_kernel(combine, last, own, out, held, narrow_slots, wide_slots, send, recv):
     place = my_place()
-    peers = [other_core(place)] + [
-        at_step(place, axis, step) for axis, _ in HOPS[1:] for step in (1, 2, 3)
-    ]
-    greet(peers)
-    held[0] = own[...]
+    plane = [
+        at_step(at_step(place, "z", k // 4), "x", k % 4) for k in range(1, 16)
+    ]
+    column = [
+        {**at_step(place, "y", k // 2), "c": lax.rem(place["c"] + k % 2, 2)} for k in range(1, 8)
+    ]
+    greet(plane + column)
     net = Net(send, recv)
-    for hop, (axis, size) in enumerate(HOPS):
-        targets = (
-            [other_core(place)]
-            if axis == "c"
-            else [at_step(place, axis, step) for step in (1, 2, 3)]
+    value = own
+    for number, (slots, index, targets) in enumerate(
+        (
+            (narrow_slots, place["z"] * 4 + place["x"], plane),
+            (wide_slots, place["y"] * 2 + place["c"], column),
         )
-        copies = [net.put(held.at[hop], slots.at[hop, place[axis]], target) for target in targets]
-        slots[hop, place[axis]] = held[hop]
+    ):
+        copies = [net.put(value, slots.at[index], target) for target in targets]
+        slots[index] = value[...]
         for copy in copies:
             copy.wait_recv()
-        total = slots[hop, 0]
-        for index in range(1, size):
-            total = combine(total, slots[hop, index])
-        held[hop + 1] = total
-    out[...] = last(held[len(HOPS)])
+        total = slots[0]
+        for k in range(1, slots.shape[0]):
+            total = combine(total, slots[k])
+        if number == 0:
+            held[...] = total
+            value = held
+    out[...] = last(total)
     net.finish()
 
 
 def small_all(value, combine, last, out_shape, collective_id, name):
     shape = value.shape
-    count = 10
+    count = 22
     return pl.pallas_call(
         functools.partial(small_kernel, combine, last),
         out_shape=jax.ShapeDtypeStruct(out_shape, F32),
         in_specs=[VMEM],
         out_specs=VMEM,
         scratch_shapes=[
-            pltpu.VMEM((len(HOPS) + 1,) + shape, F32),
-            pltpu.VMEM((len(HOPS), 4) + shape, F32),
+            pltpu.VMEM(shape, F32),
+            pltpu.VMEM((16,) + shape, F32),
+            pltpu.VMEM((8,) + shape, F32),
             pltpu.SemaphoreType.DMA((count,)),
             pltpu.SemaphoreType.DMA((count,)),
         ],
@@ -487,13 +454,15 @@
 
 def add_up(dst, parts):
     if len(dst.shape) == 3:
-
-        @pl.loop(0, dst.shape[0])
+        step = max(1, min(dst.shape[0], 32768 // (dst.shape[1] * dst.shape[2])))
+
+        @pl.loop(0, dst.shape[0] // step)
         def _(k):
-            total = parts[0][k].astype(F32)
+            block = pl.ds(k * step, step)
+            total = parts[0][block].astype(F32)
             for part in parts[1:]:
-                total = total + part[k].astype(F32)
-            dst[k] = total.astype(dst.dtype)
+                total = total + part[block].astype(F32)
+            dst[block] = total.astype(dst.dtype)
 
         return
     total = parts[0][...].astype(F32)
@@ -756,13 +725,8 @@
             @pl.loop(0, 4)
             def _(l):
                 lanes = pl.ds(pl.multiple_of(l * 256, 256), 256)
-                total = jnp.zeros((384, 256), F32)
-                for w in range(8):
-                    total = total + jnp.dot(
-                        chosen[:, pl.ds(w * 256, 256)],
-                        rows[w // 2, w % 2, :, lanes],
-                        preferred_element_type=F32,
-                    )
+                values = rows[:, :, :, lanes].reshape(2048, 256)
+                total = jnp.dot(chosen[...], values, preferred_element_type=F32)
                 table[z, x, :, lanes] = total.astype(BF16)
 
     def further(axis, step):
@@ -1018,12 +982,132 @@
     )(pieces)
 
 
+def split(value, count):
+    parts = []
+    for _ in range(count):
+        parts.append(value.astype(BF16))
+        value = value - parts[-1].astype(F32)
+    return parts
+
+
+def product(left, right):
+    count = len(left)
+    total = None
+    for order in range(count):
+        for k in range(order + 1):
+            term = jnp.dot(left[k], right[order - k], preferred_element_type=F32)
+            total = term if total is None else total + term
+    return total
+
+
+def newton_kernel(gram, turned, out, power, *scratch):
+    a_parts, q_parts, t_parts = scratch[0:3], scratch[3:6], scratch[6:8]
+
+    def blocks(k):
+        return pl.ds(pl.multiple_of(k * 256, 256), 256)
+
+    def put(parts, i, j, value, count):
+        for ref, part in zip(parts, split(value, count)):
+            ref[blocks(i), blocks(j)] = part
+
+    def mirrored(left, right, count, emit):
+        @pl.loop(0, 10)
+        def _(p):
+            i = (p >= 4).astype(jnp.int32) + (p >= 7).astype(jnp.int32) + (p >= 9).astype(jnp.int32)
+            j = p - lax.div(i * (7 - i), 2)
+            value = product(
+                [ref[blocks(i), :] for ref in left[:count]],
+                [ref[:, blocks(j)] for ref in right[:count]],
+            )
+            emit(i, j, value)
+
+    def diagonal(i, j):
+        rows = lax.broadcasted_iota(jnp.int32, (256, 256), 0) + i * 256
+        columns = lax.broadcasted_iota(jnp.int32, (256, 256), 1) + j * 256
+        return rows == columns
+
+    trace = jnp.zeros((), F32)
+    for k in range(4):
+        block = gram[k * 256 : (k + 1) * 256, k * 256 : (k + 1) * 256]
+        trace = trace + jnp.sum(jnp.where(diagonal(0, 0), block, 0.0))
+    scale = 1.0 / (jnp.sqrt(jnp.full((1, 1), trace, F32)) + 1e-07)
+
+    @pl.loop(0, 16)
+    def _(p):
+        i, j = lax.div(p, 4), lax.rem(p, 4)
+        value = gram[blocks(i), blocks(j)] * scale * scale
+        power[blocks(i), blocks(j)] = value
+        put(a_parts, i, j, value, 3)
+
+    out[...] = turned[...] * scale
+
+    for step in range(ITERS - 1):
+        count = 3 if step == 0 else 2
+
+        def emit_step(i, j, value):
+            value = NS_B * power[blocks(i), blocks(j)] + NS_C * value
+            value = value + jnp.where(diagonal(i, j), NS_A, 0.0)
+            put(q_parts, i, j, value, count)
+            put(q_parts, j, i, value.T, count)
+
+        def emit_half(i, j, value):
+            put(t_parts, i, j, value, 2)
+            put(t_parts, j, i, value.T, 2)
+
+        def emit_power(i, j, value):
+            power[blocks(i), blocks(j)] = value
+            put(a_parts, i, j, value, 2)
+            put(a_parts, j, i, value.T, 2)
+
+        mirrored(a_parts, a_parts, 2, emit_step)
+        mirrored(q_parts, a_parts, count, emit_half)
+        mirrored(t_parts, q_parts, 2, emit_power)
+        current = split(out[...], 2)
+
+        @pl.loop(0, 4)
+        def _(j):
+            out[:, blocks(j)] = product(current, [ref[:, blocks(j)] for ref in q_parts[:2]])
+
+    current = split(out[...], 2)
+    once = power
+
+    @pl.loop(0, 4)
+    def _(j):
+        once[0:160, blocks(j)] = product(current, [ref[:, blocks(j)] for ref in a_parts[:2]])
+
+    applied = split(once[0:160, :], 2)
+
+    @pl.loop(0, 4)
+    def _(j):
+        twice = product(applied, [ref[:, blocks(j)] for ref in a_parts[:2]])
+        out[:, blocks(j)] = (
+            NS_A * out[:, blocks(j)] + NS_B * once[0:160, blocks(j)] + NS_C * twice
+        )
+
+
+def newton(gram, turned):
+    return pl.pallas_call(
+        newton_kernel,
+        out_shape=jax.ShapeDtypeStruct((160, DP), F32),
+        in_specs=[VMEM, VMEM],
+        out_specs=VMEM,
+        scratch_shapes=[pltpu.VMEM((DP, DP), F32)] + [pltpu.VMEM((DP, DP), BF16)] * 8,
+        compiler_params=pltpu.CompilerParams(vmem_limit_bytes=48 << 20),
+        name="newton",
+    )(gram, turned)
+
+
 def pad_features(values):
     lead = values.shape[:-1]
     blocks = values.reshape(lead + (4, 2, 2, 60))
     blocks = jnp.moveaxis(blocks, -3, -4)
     blocks = jnp.pad(blocks, [(0, 0)] * (len(lead) + 3) + [(0, 4)])
     return blocks.reshape(lead + (DP,))
+
+
+def unpad_features(values):
+    blocks = values.reshape(values.shape[0], 2, 4, 2, 64)[..., :60]
+    return blocks.transpose(0, 2, 1, 3, 4).reshape(values.shape[0], D)
 
 
 def feature_table():
@@ -1145,12 +1229,16 @@
         to_shard(master.astype(BF16), rows) for master, rows in zip(masters, (RI, RO, RG, RD))
     ]
     ordered = tokens.reshape(MB, 8, ROWS).swapaxes(0, 1).reshape(2048)
-    mark = jnp.arange(768)
-    marks = jnp.stack([mark // 192 * 384, mark // 192 * 1536]) + mark % 192
+    by_core = tokens.reshape(MB, 4, 2, ROWS).transpose(2, 1, 0, 3).reshape(2048)
+    local_ids = by_core - wide * (16 * 384)
+    holder, row = local_ids // 384, local_ids % 384
+    swapped = holder % 4 * 4 + holder // 4
+    found = jnp.where(row < 192, holder * 192 + row, (15 + swapped) * 192 + row)
+    found = jnp.where((local_ids >= 0) & (local_ids < 16 * 384), found, 6144).astype(jnp.int32)
     wi, wo, wg, wd, info, x0 = fetch(
-        *shards, meta, table_low, ordered[:, None], marks.astype(jnp.int32)
+        *shards, meta, table_low.reshape(384, 8, 128), found
     )
-    x0 = x0.astype(F32)
+    x0 = x0.reshape(256, DP).astype(F32)
     wi = wi.reshape(16, RI, DP)[:, :100].reshape(QKV, DP)
     wo = wo.reshape(DP, DP)
     wg = wg.reshape(2 * FF, DP)
@@ -1311,16 +1399,17 @@
         summed_grads[2, :160],
     )
 
-    table_grad = dot(table_grad + table_grad_rows, features, 1, 1, HIGHEST)
+    table_grad = table_grad + table_grad_rows
 
     squares = sum(jnp.sum(shard * shard) for shard in grad_shards) + jnp.sum(
         table_grad * table_grad
     )
+    table_grad = dot(table_grad, features, 1, 1, HIGH)
     gain_grads = jnp.stack([d_gain_attn, d_gain_mlp, d_gain_final]).reshape(24, 128)
     scalars = jnp.pad(jnp.stack([squares, hit_sum, logit_sum]), (0, 125))
     packed = jnp.pad(jnp.concatenate([gain_grads, scalars[None]]), ((0, 7), (0, 0)))
     summed = small_all(packed, jnp.add, lambda v: v, (32, 128), 5, "global_sums")
-    gain_grad = dot(summed[:24].reshape(3, DP), features, 1, 1, HIGHEST)
+    gain_grad = unpad_features(summed[:24].reshape(3, DP))
     loss_total = loss_known - (1.0 - SMOOTH) * summed[24, 1] - SMOOTH / V * summed[24, 2]
     grad_norm = jnp.sqrt(summed[24, 0] + jnp.sum(gain_grad * gain_grad)) / token_count
     factor = jnp.minimum(1.0, CLIP_NORM / grad_norm) / token_count
@@ -1333,20 +1422,7 @@
     turned, gram = gram_of(pieces)
     gram = gram.reshape(DP, DP)
     turned = lax.dynamic_slice_in_dim(turned, core * 160, 160)
-    norm = jnp.sqrt(jnp.trace(gram)) + 1e-07
-    current = turned / norm
-    gram = gram / norm / norm
-    identity = jnp.eye(DP, dtype=F32)
-    for ns_step in range(ITERS):
-        if ns_step < ITERS - 1:
-            fine = HIGHEST if ns_step == 0 else HIGH
-            square = dot(gram, gram, 1, 0, fine)
-            step_matrix = NS_A * identity + NS_B * gram + NS_C * square
-            current = dot(current, step_matrix, 1, 0, HIGH)
-            gram = dot(dot(step_matrix, gram, 1, 0, fine), step_matrix, 1, 0, fine)
-        else:
-            applied = dot(current, gram, 1, 0, HIGH)
-            current = NS_A * current + NS_B * applied + NS_C * dot(applied, gram, 1, 0, HIGH)
+    current = newton(gram, turned)
     pieces = current.reshape(160, 2, 4, 128).transpose(2, 1, 0, 3).reshape(8, 160, 128)
     pieces = lax.all_to_all(pieces, "wide", split_axis=0, concat_axis=0)
     pieces = pieces.reshape(4, 320, 128)

time: 938 us -> 926 us (0.987)
  matrix products: 245 us -> 126 us
  Pallas kernels: 523 us -> 628 us
    dot_general x39 -> x20, matrix products: 211 us -> 95 us  [dot(): lax.dot_general(left, right, (((left_axis,), (right_axis,)), ((), ())), p...]
    pallas_call x1 -> x2, Pallas kernels: 183 us -> 276 us  [the longest x1 176 us: fetch(): pl.pallas_call(fetch_kernel, out_shape=shapes, in_specs=[ANY] * 6 + [pl.B...]
    unnamed x296 -> x250, local copies, waits for them, and re-layouts: 23.2 us -> 23.7 us
  transfers between devices with their start and end apart: 11 -> 11, of which waited for: 0 -> 0; matrix products, arithmetic and copies ran while one was open for 22% -> 17% of each run, Pallas kernels for 31% -> 11%
where the time goes in v4:
time: 926 us; the launch traced here: 918 us
  Pallas kernels  628 us (68%)
  matrix products  126 us (14%)
  other arithmetic  75.2 us (8%)
  local copies, waits for them, and re-layouts  68 us (7%)
  between operations  14.3 us (2%)
    pallas_call x1, Pallas kernels, fetch(): pl.pallas_call(fetch_kernel, out_shape=shapes, in_specs=[ANY] * 6 + [pl.B...  176 us
    pallas_call x1, Pallas kernels, scatter_grads(): pl.pallas_call(grads_kernel, out_shape=[jax.ShapeDtypeStruct((384, DP), F...  155 us
    pallas_call x1, Pallas kernels, newton(): pl.pallas_call(newton_kernel, out_shape=jax.ShapeDtypeStruct((160, DP), F...  99.9 us
    dot_general x20, matrix products, dot(): lax.dot_general(left, right, (((left_axis,), (right_axis,)), ((), ())), p...  95 us
    pallas_call x1, Pallas kernels, gram_of(): pl.pallas_call(gram_kernel, out_shape=[jax.ShapeDtypeStruct((320, DP), F3...  59.9 us
    pallas_call x2, Pallas kernels, small_all(): pl.pallas_call(functools.partial(small_kernel, combine, last), out_shape=...  34.5 us
    pallas_call x1, Pallas kernels, gather_rows(): pl.pallas_call(rows_kernel, out_shape=jax.ShapeDtypeStruct((4, 4, 4, 2, 3...  32.7 us
    pallas_call x1, Pallas kernels, scatter_rows(): pl.pallas_call(row_sums_kernel, out_shape=jax.ShapeDtypeStruct((32, DP),...  31.4 us
  transfers between devices with their start and end apart: 11, of which 0 were waited for; matrix products, arithmetic and copies ran while one was open for 17% of the time, Pallas kernels for 11%

profile of v4, /device:TPU:1, one launch (start us, length us, event | category | flops | bytes accessed | tf_op | source)
XLA Modules:
  0.0 917.7 jit_solution(11662453421189674263)
XLA Ops:
  14.2 4.8 convolution_convert_fusion.4
  22.2 176.2 %fetch.1 = (bf16[4,4,112,1024]{3,2,1,0:T(8,128)(2,1)}, bf16[2,4,2,64,1024]{4,3,2,1,0:T(8,128)(2,1)}, bf16[2,2,2,4,160,1024]{5,4,3,2,1,0:T(8,128)(2,1)}, bf16[2,4...) custom-call(bf16[112,128]{1,0:T(8,128)(2,1)} %copy.63.gi, ...), custom_call_target="tpu_custom_call" | custom-call | tf_op jit(solution)/shard_map/fetch/pallas_call | solution.py:325
  213.6 18.5 %gather_keys.1 = bf16[4,320,1024]{2,1,0:T(8,128)(2,1)S(1)} custom-call(bf16[4,320,128]{2,1,0:T(8,128)(2,1)S(1)} %pad_maximum_fusion.5.own), custom_call_target="tpu_custom_call" | custom-call | tf_op jit(solution)/shard_map/gather_keys/pallas_call | solution.py:825
  251.6 6.0 fusion.172
  263.2 4.5 multiply_reduce_fusion.8
  269.5 32.7 %gather_rows.1 = bf16[4,4,4,2,32,1024]{5,4,3,2,1,0:T(8,128)(2,1)S(1)} custom-call(bf16[32,1024]{1,0:T(8,128)(2,1)S(1)} %gather_fusion), custom_call_target="tpu_custom_call" | custom-call | tf_op jit(solution)/shard_map/gather_rows/pallas_call | solution.py:377
  305.4 7.7 fusion.171
  313.3 6.0 multiply_reduce_fusion.1
  320.0 18.7 %row_totals.1 = f32[32,128]{1,0:T(8,128)} custom-call(f32[2,32,128]{2,1,0:T(8,128)} %pad_maximum_fusion.10.own), custom_call_target="tpu_custom_call" | custom-call | tf_op jit(solution)/shard_map/row_totals/pallas_call | solution.py:428
  339.4 7.7 multiply_convert_fusion
  375.8 3.5 fusion.173
  379.3 4.0 add_convert_fusion
  383.3 31.4 %scatter_rows.1 = f32[32,1024]{1,0:T(8,128)S(1)} custom-call(bf16[4,4,4,32,1024]{4,3,2,1,0:T(8,128)(2,1)S(1)} %bitcast.413), custom_call_target="tpu_custom_call" | custom-call | tf_op jit(solution)/shard_map/scatter_rows/pallas_call | solution.py:643
  417.5 6.6 fusion.67
  426.2 5.5 multiply_reduce_fusion.4
  433.0 3.8 convolution_convert_fusion.7
  436.9 8.1 fusion.4
  445.0 4.7 fusion.34
  449.7 4.9 fusion.1
  456.0 7.2 fusion.6
  464.5 9.4 %fusion.3 = bf16[5,3,128,1024]{2,3,1,0:T(8,128)(2,1)} fusion(f32[5,1024,128,3]{2,1,3,0:T(8,128)} %get-tuple-element.169, f32[5,3,128,1024]{2,3,1,0:T(8,128)} %copy-done.1, f32[5,3,128]{2,1,0:T(4,128)S(1)} %get-tuple-element.168, f32[5,3,128]{2,1,0:T(4,128)S(1)} %copy-done.55), kind=kLoop, calls=%fused_computation.14 | loop fusion | flops 7864320 | bytes 19676160 | tf_op jit(solution)/shard_map/convert_element_type | solution.py:1345
  477.5 19.3 %sum_keys.1 = f32[4,320,128]{2,1,0:T(8,128)S(1)} custom-call(f32[320,1024]{1,0:T(8,128)S(1)} %bitcast.414, f32[320,1024]{1,0:T(8,128)S(1)} %bitcast.415, f32[320,1024]{1,0:T(8,128)S(1)} %bitcast.416, f32[320,1024]{1,0:T(8,128)S(1)} %bitcast.417), custom_call_target="tpu_custom_call" | custom-call | tf_op jit(solution)/shard_map/sum_keys/pallas_call | solution.py:885
  502.4 3.7 fusion.51
  510.7 4.8 convolution_convert_fusion.1
  519.0 3.9 convolution_convert_fusion.2
  522.9 7.8 convolution_convert_fusion
  530.7 155.1 %scatter_grads.1 = (f32[384,1024]{1,0:T(8,128)}, f32[3,224,128]{2,1,0:T(8,128)}) custom-call(bf16[256,1024]{1,0:T(8,128)(2,1)} %get-tuple-element.105.dx, s32[1,2048]{1,0:T(1,128)} %bitcast.496, bf16[4,4,112,512]{3,2,1,0:T(8,128)(2,1)} %bitcast.453, bf16[2,4,2,64,512]{4,3,2,1,0:T(8,128)(2,1)} %bitcast.460, bf16[2,2,2,4,160,512]{5,4,3,2,1,0:T(8,128)(2,1)} %bitcast.432, ...), custom_call_target="tpu_custom_call" | custom-call | tf_op jit(solution)/shard_map/scatter_grads/pallas_call | solution.py:789
  689.6 9.0 multiply_reduce_fusion.2
  705.0 15.8 %global_sums.1 = f32[32,128]{1,0:T(8,128)} custom-call(f32[32,128]{1,0:T(8,128)} %select_maximum_fusion.own), custom_call_target="tpu_custom_call" | custom-call | tf_op jit(solution)/shard_map/global_sums/pallas_call | solution.py:428
  731.2 59.9 %gram_sums.1 = (f32[320,1024]{1,0:T(8,128)S(1)}, f32[2,4,4,32,1024]{4,3,2,1,0:T(8,128)S(1)}) custom-call(f32[4,320,128]{2,1,0:T(8,128)S(1)} %pad_maximum_fusion.2.pieces), custom_call_target="tpu_custom_call" | custom-call | tf_op jit(solution)/shard_map/gram_sums/pallas_call | solution.py:969
  791.2 99.9 %newton.1 = f32[160,1024]{1,0:T(8,128)S(1)} custom-call(f32[1024,1024]{1,0:T(8,128)S(1)} %bitcast.418, f32[160,1024]{1,0:T(8,128)S(1)} %constant_dynamic-slice_fusion.turned), custom_call_target="tpu_custom_call" | custom-call | tf_op jit(solution)/shard_map/newton/pallas_call | solution.py:1089
  896.1 8.8 fusion.156
  (498 shorter events, 143.6 us)
Async XLA Ops:
  0.7 247.4 %copy-start.95 = (s32[960]{0:T(1024)}, s32[960]{0:T(1024)S(1)}, u32[]{:S(2)}) copy-start(s32[960]{0:T(1024)S(1)} %get-tuple-element.175) | copy-start | bytes 11524
  0.7 247.4 %copy-start.97 = (s32[960]{0:T(1024)}, s32[960]{0:T(1024)S(1)}, u32[]{:S(2)}) copy-start(s32[960]{0:T(1024)S(1)} %get-tuple-element.176) | copy-start | bytes 11524
  0.7 247.4 %copy-start.99 = (s32[960]{0:T(1024)}, s32[960]{0:T(1024)S(1)}, u32[]{:S(2)}) copy-start(s32[960]{0:T(1024)S(1)} %get-tuple-element.177) | copy-start | bytes 11524
  0.7 247.4 %copy-start.101 = (s32[960]{0:T(1024)}, s32[960]{0:T(1024)S(1)}, u32[]{:S(2)}) copy-start(s32[960]{0:T(1024)S(1)} %get-tuple-element.178) | copy-start | bytes 11524
  0.7 247.4 %copy-start.106 = (pred[960]{0:T(1024)(128)(4,1)}, pred[960]{0:T(1024)(128)(4,1)S(1)}, u32[]{:S(2)}) copy-start(pred[960]{0:T(1024)(128)(4,1)S(1)} %get-tuple-element.173) | copy-start | bytes 2884
  0.7 247.4 %copy-start.108 = (pred[960]{0:T(1024)(128)(4,1)}, pred[960]{0:T(1024)(128)(4,1)S(1)}, u32[]{:S(2)}) copy-start(pred[960]{0:T(1024)(128)(4,1)S(1)} %get-tuple-element.174) | copy-start | bytes 2884
  211.8 38.6 %copy-start.8 = (f32[32,8,8,128]{3,2,1,0:T(8,128)}, f32[32,8,8,128]{3,2,1,0:T(8,128)S(1)}, u32[]{:S(2)}) copy-start(f32[32,8,8,128]{3,2,1,0:T(8,128)S(1)} %bitcast_convert_fusion) | copy-start | bytes 3145732
  261.8 248.3 %collective-permute-start.8 = (bf16[256,2560]{1,0:T(8,128)(2,1)}, bf16[256,2560]{1,0:T(8,128)(2,1)}, u32[]{:S(2)}, u32[]{:S(2)}) collective-permute-start(bf16[256,2560]{1,0:T(8,128)(2,1)} %multiply_convert_fusion.1), channel_id=1, source_target_pairs={{0,16},{16,0},{32,48},{48,32},{64,80},{80,64},{96,112},{112,96},{1... | collective-permute-start | bytes 3932168 | tf_op jit(solution)/shard_map/ppermute | solution.py:1179
  267.7 34.5 %copy-start.93 = (f32[256]{0:T(256)}, f32[256]{0:T(256)S(1)}, u32[]{:S(2)}) copy-start(f32[256]{0:T(256)S(1)} %get-tuple-element.161) | copy-start | bytes 3076
  267.8 34.4 %copy-start.59 = (f32[1024]{0:T(1024)}, f32[1024]{0:T(1024)S(1)}, u32[]{:S(2)}) copy-start(f32[1024]{0:T(1024)S(1)} %mul.923) | copy-start | bytes 12292
  267.8 34.4 %copy-start.73 = (f32[256]{0:T(256)}, f32[256]{0:T(256)S(1)}, u32[]{:S(2)}) copy-start(f32[256]{0:T(256)S(1)} %fusion.139) | copy-start | bytes 3076
  268.0 34.2 %copy-start.110 = (s32[32]{0:T(128)}, s32[32]{0:T(128)S(1)}, u32[]{:S(2)}) copy-start(s32[32]{0:T(128)S(1)} %fusion.140) | copy-start | bytes 388
  349.6 29.7 %collective-permute-start = (bf16[2048,384]{1,0:T(8,128)(2,1)}, bf16[2048,384]{1,0:T(8,128)(2,1)}, u32[]{:S(2)}, u32[]{:S(2)}) collective-permute-start(bf16[2048,384]{1,0:T(8,128)(2,1)} %bitcast.66), channel_id=1, source_target_pairs={{0,16},{16,0},{32,48},{48,32},{64,80},{80,64},{96,112},{112,96},{1... | collective-permute-start | bytes 4718600 | tf_op jit(solution)/shard_map/ppermute | solution.py:1179
  349.9 29.4 %collective-permute-start.1 = (bf16[384,1024]{0,1:T(8,128)(2,1)}, bf16[384,1024]{0,1:T(8,128)(2,1)}, u32[]{:S(2)}, u32[]{:S(2)}) collective-permute-start(bf16[384,1024]{0,1:T(8,128)(2,1)} %bitcast.12), channel_id=1, source_target_pairs={{0,16},{16,0},{32,48},{48,32},{64,80},{80,64},{96,112},{112,96},{1... | collective-permute-start | bytes 2359304 | tf_op jit(solution)/shard_map/ppermute | solution.py:1179
  383.3 33.9 %copy-start.94 = (f32[256]{0:T(256)S(1)}, f32[256]{0:T(256)}, u32[]{:S(2)}) copy-start(f32[256]{0:T(256)} %copy-done.93) | copy-start | bytes 3076
  499.0 17.0 %collective-permute-start.4 = (bf16[256,1024]{1,0:T(8,128)(2,1)}, bf16[256,1024]{1,0:T(8,128)(2,1)}, u32[]{:S(2)}, u32[]{:S(2)}) collective-permute-start(bf16[256,1024]{1,0:T(8,128)(2,1)} %get-tuple-element.90), channel_id=1, source_target_pairs={{0,16},{16,0},{32,48},{48,32},{64,80},{80,64},{96,112},{112,96},{1... | collective-permute-start | bytes 1572872 | tf_op jit(solution)/shard_map/ppermute | solution.py:1179
  499.1 23.8 %collective-permute-start.6 = (bf16[256,5120]{1,0:T(8,128)(2,1)}, bf16[256,5120]{1,0:T(8,128)(2,1)}, u32[]{:S(2)}, u32[]{:S(2)}) collective-permute-start(bf16[256,5120]{1,0:T(8,128)(2,1)} %add_convert_fusion.1), channel_id=1, source_target_pairs={{0,16},{16,0},{32,48},{48,32},{64,80},{80,64},{96,112},{112,96},{1... | collective-permute-start | bytes 7864328 | tf_op jit(solution)/shard_map/ppermute | solution.py:1179
  506.1 12.9 %collective-permute-start.2 = (bf16[256,1792]{1,0:T(8,128)(2,1)}, bf16[256,1792]{1,0:T(8,128)(2,1)}, u32[]{:S(2)}, u32[]{:S(2)}) collective-permute-start(bf16[256,1792]{1,0:T(8,128)(2,1)} %fusion.51), channel_id=1, source_target_pairs={{0,16},{16,0},{32,48},{48,32},{64,80},{80,64},{96,112},{112,96},{1... | collective-permute-start | bytes 2752520 | tf_op jit(solution)/shard_map/ppermute | solution.py:1179
  506.9 3.4 collective-permute-start.9
  510.1 5.4 collective-permute-start.5
  510.3 8.7 collective-permute-start.3
  515.5 7.4 collective-permute-start.7
  530.7 158.8 %copy-start.5 = (bf16[4096,384]{1,0:T(8,128)(2,1)S(1)}, bf16[4096,384]{1,0:T(8,128)(2,1)}, u32[]{:S(2)}) copy-start(bf16[4096,384]{1,0:T(8,128)(2,1)} %copy-done.4) | copy-start | bytes 9437188
  689.6 36.9 %copy-start.52 = (f32[112,128]{1,0:T(8,128)S(1)}, f32[112,128]{1,0:T(8,128)}, u32[]{:S(2)}) copy-start(f32[112,128]{1,0:T(8,128)} %copy.85) | copy-start | bytes 172036
  791.2 104.7 %copy-start.39 = (f32[384,1024]{1,0:T(8,128)S(1)}, f32[384,1024]{1,0:T(8,128)}, u32[]{:S(2)}) copy-start(f32[384,1024]{1,0:T(8,128)} %get-tuple-element.39) | copy-start | bytes 4718596
  791.2 104.7 %copy-start.96 = (s32[960]{0:T(1024)S(1)}, s32[960]{0:T(1024)}, u32[]{:S(2)}) copy-start(s32[960]{0:T(1024)} %copy-done.95) | copy-start | bytes 11524
  791.2 104.7 %copy-start.98 = (s32[960]{0:T(1024)S(1)}, s32[960]{0:T(1024)}, u32[]{:S(2)}) copy-start(s32[960]{0:T(1024)} %copy-done.97) | copy-start | bytes 11524
  791.2 104.7 %copy-start.100 = (s32[960]{0:T(1024)S(1)}, s32[960]{0:T(1024)}, u32[]{:S(2)}) copy-start(s32[960]{0:T(1024)} %copy-done.99) | copy-start | bytes 11524
  791.2 104.7 %copy-start.102 = (s32[960]{0:T(1024)S(1)}, s32[960]{0:T(1024)}, u32[]{:S(2)}) copy-start(s32[960]{0:T(1024)} %copy-done.101) | copy-start | bytes 11524
  791.2 104.7 %copy-start.107 = (pred[960]{0:T(1024)(128)(4,1)S(1)}, pred[960]{0:T(1024)(128)(4,1)}, u32[]{:S(2)}) copy-start(pred[960]{0:T(1024)(128)(4,1)} %copy-done.106) | copy-start | bytes 2884
  791.2 104.7 %copy-start.109 = (pred[960]{0:T(1024)(128)(4,1)S(1)}, pred[960]{0:T(1024)(128)(4,1)}, u32[]{:S(2)}) copy-start(pred[960]{0:T(1024)(128)(4,1)} %copy-done.108) | copy-start | bytes 2884
  892.4 16.0 %all-to-all-start = ((f32[8,160,128]{2,1,0:T(8,128)}), f32[8,160,128]{2,1,0:T(8,128)S(1)}, u32[]{:S(2)}, u32[]{:S(2)}) async-start(f32[8,160,128]{2,1,0:T(8,128)} %bitcast.144), calls=%async_computation | async-start | bytes 1310720 | tf_op jit(solution)/shard_map/all_to_all | solution.py:1427
  (95 other events, 702.8 us)

commit v5 on v4

--- a/solution.py
+++ b/solution.py
@@ -261,10 +261,8 @@
         for axes, items in (
             (("x", "z", "y"), [(in_wg(0), halved(0, 160)), (in_wo, halved(0, 64))]),
             (("z", "x", "y"), [(in_wg(1), halved(0, 160)), (in_wi, halved(0, 64))]),
-            (
-                ("y", "z", "x"),
-                [(in_wd, halved(0, 160)), (in_wi, halved(64, 112)), (in_info, ((0, 8), None))],
-            ),
+            (("z", "y", "x"), [(in_wd, halved(0, 80)), (in_wi, halved(64, 112))]),
+            (("x", "y", "z"), [(in_wd, halved(80, 160)), (in_info, ((0, 8), None))]),
         )
     ]
 
@@ -278,10 +276,12 @@
     each(tables, "relay")
     each(weights, "relay")
     each(tables, "near", "far", "begin")
-    each(weights, "near", "far", "begin")
+    each(weights, "near", "far", "begin", "relay", "near", "far", "begin")
     each(tables, "relay")
-    each(weights, "relay", "near", "far", "begin")
-    each(tables, "near", "far")
+    each(weights, "relay")
+    each(tables, "near")
+    each(weights, "near")
+    each(tables, "far")
 
     @pl.loop(0, 128)
     def _(block):
@@ -292,7 +292,7 @@
     swap = net.put(
         packed.at[pl.ds((1 - place["c"]) * 1024, 1024)], theirs, other_core(place)
     )
-    each(weights, "relay")
+    each(weights, "far")
     swap.wait_recv()
     add_up(theirs, [packed.at[pl.ds(place["c"] * 1024, 1024)], theirs])
     ring = Ring(
@@ -304,9 +304,7 @@
         lambda half: x0.at[pl.ds(half * 128, 128)],
     )
     ring.send_all()
-    each(weights, "near")
     ring.pass_on()
-    each(weights, "far")
     ring.close()
     each(weights, "end")
     net.finish()
@@ -321,7 +319,7 @@
         jax.ShapeDtypeStruct((4, 4, 4, 2, 8, 128), jnp.int32),
         jax.ShapeDtypeStruct((256, 8, 128), BF16),
     ]
-    count = 202
+    count = 226
     return pl.pallas_call(
         fetch_kernel,
         out_shape=shapes,
@@ -562,11 +560,13 @@
             stream["first"][far].send_down()
 
 
-def finish_scatter(streams, passed=False):
-    if not passed:
-        for far in FAR_FIRST:
-            for stream in streams:
-                stream["first"][far].pass_on()
+def pass_first(streams):
+    for far in FAR_FIRST:
+        for stream in streams:
+            stream["first"][far].pass_on()
+
+
+def close_first(streams):
     for far in FAR_FIRST:
         for stream in streams:
             stream["first"][far].close()
@@ -577,14 +577,26 @@
                 following.send_up()
             if far == 3:
                 following.send_down()
-    for number in range(max(len(stream["rest"]) for stream in streams)):
-        active = [stream["rest"] for stream in streams if number < len(stream["rest"])]
-        for rest in active:
-            rest[number].pass_on()
-        for rest in active:
-            rest[number].close()
-            if number + 1 < len(rest):
-                rest[number + 1].send_all()
+
+
+def pass_rest(streams, number):
+    for stream in streams:
+        stream["rest"][number].pass_on()
+
+
+def close_rest(streams, number):
+    for stream in streams:
+        stream["rest"][number].close()
+        if number + 1 < len(stream["rest"]):
+            stream["rest"][number + 1].send_all()
+
+
+def finish_scatter(streams):
+    pass_first(streams)
+    close_first(streams)
+    for number in range(len(streams[0]["rest"])):
+        pass_rest(streams, number)
+        close_rest(streams, number)
 
 
 def got_shapes(depth, rows, lanes, first, later):
@@ -653,16 +665,21 @@
     )(part)
 
 
-GRAD_ORDERS = (("y", "x", "z"), ("y", "z", "x"), ("x", "z", "y"))
+GRAD_STREAMS = (
+    (("y", "x", "z"), 0, 0, 224),
+    (("y", "z", "x"), 1, 0, 224),
+    (("x", "y", "z"), 2, 0, 128),
+    (("z", "y", "x"), 2, 128, 96),
+)
 
 
 def grads_kernel(dx, ids, di, do, dg, dd, out, weights_out, *scratch):
     rows, table, chosen = scratch[:3]
     held = scratch[3:6]
     gots = scratch[6:10]
-    weight_gots = scratch[10:19]
-    accs = scratch[19:22]
-    send, recv, local = scratch[22:]
+    weight_gots = scratch[10:22]
+    accs = scratch[22:26]
+    send, recv, local = scratch[26:]
     place = my_place()
     moves = [(dx, rows.at[place["y"], place["c"]])]
     for y in range(4):
@@ -696,17 +713,23 @@
     spread.begin()
     for copy in copies[1:]:
         copy.wait()
-    weight_streams = [
+    weights = [
         start_scatter(
-            net, place, order, held[k], weight_gots[3 * k : 3 * k + 3], weights_out.at[k], accs[k]
+            net,
+            place,
+            order,
+            held[which].at[:, :, :, pl.ds(first, count)],
+            weight_gots[3 * k : 3 * k + 3],
+            weights_out.at[which, pl.ds(first, count)],
+            accs[k],
         )
-        for k, order in enumerate(GRAD_ORDERS)
-    ]
-    send_first(weight_streams[2:])
+        for k, (order, which, first, count) in enumerate(GRAD_STREAMS)
+    ]
+    send_first(weights[2:])
     spread.relay()
     spread.near()
     spread.far()
-    send_first(weight_streams[:2])
+    send_first(weights[:2])
     spread.end()
     base = (place["y"] * 2 + place["c"]) * 16
 
@@ -755,23 +778,37 @@
     by_x[2].send_down()
     by_z[2].send_up()
     by_z[2].send_down()
-    for step in FAR_FIRST:
-        weight_streams[2]["first"][step].pass_on()
-    parts(9, lambda k: (further("z", lax.div(k, 3) + 3), further("x", lax.rem(k, 3) + 3)))
-    for step in (1, 3, 0):
-        by_x[step].send_up()
-        by_x[step].send_down()
-        by_z[step].send_up()
-        by_z[step].send_down()
-    for step in FAR_FIRST:
-        for stream in streams + weight_streams[:2]:
-            stream["first"][step].pass_on()
-    finish_scatter(streams + weight_streams, passed=True)
+    pass_first(weights[2:])
+    third = lambda dz: parts(3, lambda k: (further("z", dz), further("x", k + 3)))
+    third(1)
+    for ring in (by_x[1], by_z[1], by_z[3], by_z[0]):
+        ring.send_up()
+    by_x[1].send_down()
+    pass_first(weights[:2])
+    close_first(weights[2:])
+    third(3)
+    for ring in (by_x[3], by_z[1], by_z[3], by_z[0]):
+        ring.send_down()
+    by_x[3].send_up()
+    close_first(weights[:2])
+    third(0)
+    by_x[0].send_up()
+    by_x[0].send_down()
+    pass_first(streams)
+    pass_rest(weights[2:], 0)
+    close_rest(weights[2:], 0)
+    pass_rest(weights[:2], 0)
+    close_rest(weights[:2], 0)
+    close_first(streams)
+    pass_rest(weights, 1)
+    close_rest(weights, 1)
+    pass_rest(streams, 0)
+    close_rest(streams, 0)
     net.finish()
 
 
 def scatter_grads(dx, ids, di, do, dg, dd):
-    count = 3 * 36 + 2 * 30 + 16
+    count = 4 * 36 + 2 * 30 + 14
     scratch = [
         pltpu.VMEM((4, 2, 256, DP), BF16),
         pltpu.VMEM((4, 4, 384, DP), BF16),
@@ -779,8 +816,9 @@
     ]
     scratch += [pltpu.VMEM((4, 4, 4, 224, 128), BF16)] * 3
     scratch += got_shapes(2, 192, DP, BF16, BF16) * 2
-    scratch += got_shapes(3, 224, 128, BF16, F32) * 3
-    scratch += [pltpu.VMEM((4, 4, 224, 128), F32)] * 3
+    for _, _, _, rows in GRAD_STREAMS:
+        scratch += got_shapes(3, rows, 128, BF16, F32)
+    scratch += [pltpu.VMEM((4, 4, rows, 128), F32) for _, _, _, rows in GRAD_STREAMS]
     scratch += [
         pltpu.SemaphoreType.DMA((count,)),
         pltpu.SemaphoreType.DMA((count,)),
@@ -1006,20 +1044,24 @@
     def blocks(k):
         return pl.ds(pl.multiple_of(k * 256, 256), 256)
 
-    def put(parts, i, j, value, count):
+    def put(parts, i, j, value, count, mirror=True):
         for ref, part in zip(parts, split(value, count)):
             ref[blocks(i), blocks(j)] = part
+            if mirror:
+                ref[blocks(j), blocks(i)] = part.T
 
     def mirrored(left, right, count, emit):
-        @pl.loop(0, 10)
-        def _(p):
-            i = (p >= 4).astype(jnp.int32) + (p >= 7).astype(jnp.int32) + (p >= 9).astype(jnp.int32)
-            j = p - lax.div(i * (7 - i), 2)
-            value = product(
-                [ref[blocks(i), :] for ref in left[:count]],
-                [ref[:, blocks(j)] for ref in right[:count]],
-            )
-            emit(i, j, value)
+        @pl.loop(0, 2)
+        def _(half):
+            for k in range(5):
+                p = half * 5 + k
+                i = sum((p >= edge).astype(jnp.int32) for edge in (4, 7, 9))
+                j = p - lax.div(i * (7 - i), 2)
+                value = product(
+                    [ref[blocks(i), :] for ref in left[:count]],
+                    [ref[:, blocks(j)] for ref in right[:count]],
+                )
+                emit(i, j, value)
 
     def diagonal(i, j):
         rows = lax.broadcasted_iota(jnp.int32, (256, 256), 0) + i * 256
@@ -1037,27 +1079,21 @@
         i, j = lax.div(p, 4), lax.rem(p, 4)
         value = gram[blocks(i), blocks(j)] * scale * scale
         power[blocks(i), blocks(j)] = value
-        put(a_parts, i, j, value, 3)
+        put(a_parts, i, j, value, 3, False)
 
     out[...] = turned[...] * scale
 
-    for step in range(ITERS - 1):
-        count = 3 if step == 0 else 2
-
+    def advance(count):
         def emit_step(i, j, value):
             value = NS_B * power[blocks(i), blocks(j)] + NS_C * value
-            value = value + jnp.where(diagonal(i, j), NS_A, 0.0)
-            put(q_parts, i, j, value, count)
-            put(q_parts, j, i, value.T, count)
+            put(q_parts, i, j, value + jnp.where(diagonal(i, j), NS_A, 0.0), count)
 
         def emit_half(i, j, value):
             put(t_parts, i, j, value, 2)
-            put(t_parts, j, i, value.T, 2)
 
         def emit_power(i, j, value):
             power[blocks(i), blocks(j)] = value
             put(a_parts, i, j, value, 2)
-            put(a_parts, j, i, value.T, 2)
 
         mirrored(a_parts, a_parts, 2, emit_step)
         mirrored(q_parts, a_parts, count, emit_half)
@@ -1067,6 +1103,12 @@
         @pl.loop(0, 4)
         def _(j):
             out[:, blocks(j)] = product(current, [ref[:, blocks(j)] for ref in q_parts[:2]])
+
+    advance(3)
+
+    @pl.loop(0, ITERS - 2)
+    def _(_step):
+        advance(2)
 
     current = split(out[...], 2)
     once = power

time: 926 us -> 885 us (0.956)
  Pallas kernels: 628 us -> 585 us
    pallas_call x1, Pallas kernels: 176 us -> 152 us  [fetch(): pl.pallas_call(fetch_kernel, out_shape=shapes, in_specs=[ANY] * 6 + [pl.B...]
    pallas_call x1, Pallas kernels: 99.9 us -> 82.4 us  [newton(): pl.pallas_call(newton_kernel, out_shape=jax.ShapeDtypeStruct((160, DP), F...]
  transfers between devices with their start and end apart: 11 -> 11, of which waited for: 0 -> 0; matrix products, arithmetic and copies ran while one was open for 17% -> 18% of each run, Pallas kernels for 11% -> 12%
where the time goes in v5:
time: 885 us; the launch traced here: 876 us
  Pallas kernels  585 us (66%)
  matrix products  126 us (14%)
  other arithmetic  75.2 us (8%)
  local copies, waits for them, and re-layouts  68 us (8%)
  between operations  14.5 us (2%)
    pallas_call x1, Pallas kernels, scatter_grads(): pl.pallas_call(grads_kernel, out_shape=[jax.ShapeDtypeStruct((384, DP), F...  153 us
    pallas_call x1, Pallas kernels, fetch(): pl.pallas_call(fetch_kernel, out_shape=shapes, in_specs=[ANY] * 6 + [pl.B...  152 us
    dot_general x20, matrix products, dot(): lax.dot_general(left, right, (((left_axis,), (right_axis,)), ((), ())), p...  94.9 us
    pallas_call x1, Pallas kernels, newton(): pl.pallas_call(newton_kernel, out_shape=jax.ShapeDtypeStruct((160, DP), F...  82.4 us
    pallas_call x1, Pallas kernels, gram_of(): pl.pallas_call(gram_kernel, out_shape=[jax.ShapeDtypeStruct((320, DP), F3...  59.7 us
    pallas_call x2, Pallas kernels, small_all(): pl.pallas_call(functools.partial(small_kernel, combine, last), out_shape=...  32.7 us
    pallas_call x1, Pallas kernels, gather_rows(): pl.pallas_call(rows_kernel, out_shape=jax.ShapeDtypeStruct((4, 4, 4, 2, 3...  32.7 us
    pallas_call x1, Pallas kernels, scatter_rows(): pl.pallas_call(row_sums_kernel, out_shape=jax.ShapeDtypeStruct((32, DP),...  31.5 us
  transfers between devices with their start and end apart: 11, of which 0 were waited for; matrix products, arithmetic and copies ran while one was open for 18% of the time, Pallas kernels for 12%

profile of v5, /device:TPU:1, one launch (start us, length us, event | category | flops | bytes accessed | tf_op | source)
XLA Modules:
  0.0 875.8 jit_solution(11241085547665898249)
XLA Ops:
  14.2 4.8 convolution_convert_fusion.4
  22.2 151.9 %fetch.1 = (bf16[4,4,112,1024]{3,2,1,0:T(8,128)(2,1)}, bf16[2,4,2,64,1024]{4,3,2,1,0:T(8,128)(2,1)}, bf16[2,2,2,4,160,1024]{5,4,3,2,1,0:T(8,128)(2,1)}, bf16[2,4...) custom-call(bf16[112,128]{1,0:T(8,128)(2,1)} %copy.63.gi, ...), custom_call_target="tpu_custom_call" | custom-call | tf_op jit(solution)/shard_map/fetch/pallas_call | solution.py:323
  189.2 22.0 %gather_keys.1 = bf16[4,320,1024]{2,1,0:T(8,128)(2,1)S(1)} custom-call(bf16[4,320,128]{2,1,0:T(8,128)(2,1)S(1)} %pad_maximum_fusion.5.own), custom_call_target="tpu_custom_call" | custom-call | tf_op jit(solution)/shard_map/gather_keys/pallas_call | solution.py:863
  230.8 6.0 fusion.172
  242.3 4.5 multiply_reduce_fusion.8
  248.6 32.7 %gather_rows.1 = bf16[4,4,4,2,32,1024]{5,4,3,2,1,0:T(8,128)(2,1)S(1)} custom-call(bf16[32,1024]{1,0:T(8,128)(2,1)S(1)} %gather_fusion), custom_call_target="tpu_custom_call" | custom-call | tf_op jit(solution)/shard_map/gather_rows/pallas_call | solution.py:375
  284.6 7.7 fusion.171
  292.4 6.0 multiply_reduce_fusion.1
  299.1 18.5 %row_totals.1 = f32[32,128]{1,0:T(8,128)} custom-call(f32[2,32,128]{2,1,0:T(8,128)} %pad_maximum_fusion.10.own), custom_call_target="tpu_custom_call" | custom-call | tf_op jit(solution)/shard_map/row_totals/pallas_call | solution.py:426
  318.3 7.7 multiply_convert_fusion
  358.2 4.0 add_convert_fusion
  362.2 31.5 %scatter_rows.1 = f32[32,1024]{1,0:T(8,128)S(1)} custom-call(bf16[4,4,4,32,1024]{4,3,2,1,0:T(8,128)(2,1)S(1)} %bitcast.413), custom_call_target="tpu_custom_call" | custom-call | tf_op jit(solution)/shard_map/scatter_rows/pallas_call | solution.py:655
  396.5 6.6 fusion.67
  405.2 5.5 multiply_reduce_fusion.4
  412.0 3.8 convolution_convert_fusion.7
  415.9 8.1 fusion.4
  424.0 4.7 fusion.34
  428.7 4.9 fusion.1
  435.0 7.2 fusion.6
  443.5 9.4 %fusion.3 = bf16[5,3,128,1024]{2,3,1,0:T(8,128)(2,1)} fusion(f32[5,1024,128,3]{2,1,3,0:T(8,128)} %get-tuple-element.169, f32[5,3,128,1024]{2,3,1,0:T(8,128)} %copy-done.1, f32[5,3,128]{2,1,0:T(4,128)S(1)} %get-tuple-element.168, f32[5,3,128]{2,1,0:T(4,128)S(1)} %copy-done.55), kind=kLoop, calls=%fused_computation.14 | loop fusion | flops 7864320 | bytes 19676160 | tf_op jit(solution)/shard_map/convert_element_type | solution.py:1387
  456.4 19.2 %sum_keys.1 = f32[4,320,128]{2,1,0:T(8,128)S(1)} custom-call(f32[320,1024]{1,0:T(8,128)S(1)} %bitcast.414, f32[320,1024]{1,0:T(8,128)S(1)} %bitcast.415, f32[320,1024]{1,0:T(8,128)S(1)} %bitcast.416, f32[320,1024]{1,0:T(8,128)S(1)} %bitcast.417), custom_call_target="tpu_custom_call" | custom-call | tf_op jit(solution)/shard_map/sum_keys/pallas_call | solution.py:923
  481.3 3.7 fusion.51
  489.5 4.8 convolution_convert_fusion.1
  497.8 3.9 convolution_convert_fusion.2
  501.8 7.8 convolution_convert_fusion
  509.6 153.4 %scatter_grads.1 = (f32[384,1024]{1,0:T(8,128)}, f32[3,224,128]{2,1,0:T(8,128)}) custom-call(bf16[256,1024]{1,0:T(8,128)(2,1)} %get-tuple-element.105.dx, s32[1,2048]{1,0:T(1,128)} %bitcast.496, bf16[4,4,112,512]{3,2,1,0:T(8,128)(2,1)} %bitcast.453, bf16[2,4,2,64,512]{4,3,2,1,0:T(8,128)(2,1)} %bitcast.460, bf16[2,2,2,4,160,512]{5,4,3,2,1,0:T(8,128)(2,1)} %bitcast.432, ...), custom_call_target="tpu_custom_call" | custom-call | tf_op jit(solution)/shard_map/scatter_grads/pallas_call | solution.py:827
  666.7 9.0 %multiply_reduce_fusion.2 = (f32[]{:T(128)}, f32[384,1024]{1,0:T(8,128)}) fusion(f32[384,1024]{1,0:T(8,128)} %get-tuple-element.39, bf16[4096,384]{1,0:T(8,128)(2,1)S(1)} %copy-done.5, bf16[4096,1024]{1,0:T(8,128)(2,1)} %bitcast.412), kind=kOutput, calls=%fused_computation.97 | convolution fusion | flops 3222405120 | bytes 14680068 | tf_op jit(solution)/shard_map/dot_general | solution.py:1181
  682.2 14.2 %global_sums.1 = f32[32,128]{1,0:T(8,128)} custom-call(f32[32,128]{1,0:T(8,128)} %select_maximum_fusion.own), custom_call_target="tpu_custom_call" | custom-call | tf_op jit(solution)/shard_map/global_sums/pallas_call | solution.py:426
  706.7 59.7 %gram_sums.1 = (f32[320,1024]{1,0:T(8,128)S(1)}, f32[2,4,4,32,1024]{4,3,2,1,0:T(8,128)S(1)}) custom-call(f32[4,320,128]{2,1,0:T(8,128)S(1)} %pad_maximum_fusion.2.pieces), custom_call_target="tpu_custom_call" | custom-call | tf_op jit(solution)/shard_map/gram_sums/pallas_call | solution.py:1007
  766.6 82.4 %newton.1 = f32[160,1024]{1,0:T(8,128)S(1)} custom-call(f32[1024,1024]{1,0:T(8,128)S(1)} %bitcast.418, f32[160,1024]{1,0:T(8,128)S(1)} %constant_dynamic-slice_fusion.turned), custom_call_target="tpu_custom_call" | custom-call | tf_op jit(solution)/shard_map/newton/pallas_call | solution.py:1131
  850.3 3.6 all-to-all-start
  854.0 8.8 %fusion.156 = (bf16[384,960]{0,1:T(8,128)(2,1)}, f32[384,960]{0,1:T(8,128)}, f32[384,960]{0,1:T(8,128)}, f32[384,960]{0,1:T(8,128)}) fusion(f32[384,960]{0,1:T(8,128)} %param.27, f32[384,960]{0,1:T(8,128)} %param.33, f32[384,960]{0,1:T(8,128)} %param.32, s32[960]{0:T(1024)S(1)} %copy-done.98, s32[960]{0:T(1024)S(1)} %copy-done.100, ...), kind=kOutput, calls=%fused_computation.368 | convolution fusion | flops 2310537216 | bytes 12747652 | tf_op jit(solution)/shard_map/dot_general | solution.py:1181
  (498 shorter events, 143.6 us)
Async XLA Ops:
  0.7 226.6 %copy-start.95 = (s32[960]{0:T(1024)}, s32[960]{0:T(1024)S(1)}, u32[]{:S(2)}) copy-start(s32[960]{0:T(1024)S(1)} %get-tuple-element.175) | copy-start | bytes 11524
  0.7 226.6 %copy-start.97 = (s32[960]{0:T(1024)}, s32[960]{0:T(1024)S(1)}, u32[]{:S(2)}) copy-start(s32[960]{0:T(1024)S(1)} %get-tuple-element.176) | copy-start | bytes 11524
  0.7 226.6 %copy-start.99 = (s32[960]{0:T(1024)}, s32[960]{0:T(1024)S(1)}, u32[]{:S(2)}) copy-start(s32[960]{0:T(1024)S(1)} %get-tuple-element.177) | copy-start | bytes 11524
  0.7 226.6 %copy-start.101 = (s32[960]{0:T(1024)}, s32[960]{0:T(1024)S(1)}, u32[]{:S(2)}) copy-start(s32[960]{0:T(1024)S(1)} %get-tuple-element.178) | copy-start | bytes 11524
  0.7 226.5 %copy-start.106 = (pred[960]{0:T(1024)(128)(4,1)}, pred[960]{0:T(1024)(128)(4,1)S(1)}, u32[]{:S(2)}) copy-start(pred[960]{0:T(1024)(128)(4,1)S(1)} %get-tuple-element.173) | copy-start | bytes 2884
  0.7 226.5 %copy-start.108 = (pred[960]{0:T(1024)(128)(4,1)}, pred[960]{0:T(1024)(128)(4,1)S(1)}, u32[]{:S(2)}) copy-start(pred[960]{0:T(1024)(128)(4,1)S(1)} %get-tuple-element.174) | copy-start | bytes 2884
  187.5 42.1 %copy-start.8 = (f32[32,8,8,128]{3,2,1,0:T(8,128)}, f32[32,8,8,128]{3,2,1,0:T(8,128)S(1)}, u32[]{:S(2)}) copy-start(f32[32,8,8,128]{3,2,1,0:T(8,128)S(1)} %bitcast_convert_fusion) | copy-start | bytes 3145732
  240.9 248.0 %collective-permute-start.8 = (bf16[256,2560]{1,0:T(8,128)(2,1)}, bf16[256,2560]{1,0:T(8,128)(2,1)}, u32[]{:S(2)}, u32[]{:S(2)}) collective-permute-start(bf16[256,2560]{1,0:T(8,128)(2,1)} %multiply_convert_fusion.1), channel_id=1, source_target_pairs={{0,16},{16,0},{32,48},{48,32},{64,80},{80,64},{96,112},{112,96},{1... | collective-permute-start | bytes 3932168 | tf_op jit(solution)/shard_map/ppermute | solution.py:1221
  246.9 34.4 %copy-start.93 = (f32[256]{0:T(256)}, f32[256]{0:T(256)S(1)}, u32[]{:S(2)}) copy-start(f32[256]{0:T(256)S(1)} %get-tuple-element.161) | copy-start | bytes 3076
  246.9 34.4 %copy-start.59 = (f32[1024]{0:T(1024)}, f32[1024]{0:T(1024)S(1)}, u32[]{:S(2)}) copy-start(f32[1024]{0:T(1024)S(1)} %mul.923) | copy-start | bytes 12292
  247.0 34.4 %copy-start.73 = (f32[256]{0:T(256)}, f32[256]{0:T(256)S(1)}, u32[]{:S(2)}) copy-start(f32[256]{0:T(256)S(1)} %fusion.139) | copy-start | bytes 3076
  247.2 34.1 %copy-start.110 = (s32[32]{0:T(128)}, s32[32]{0:T(128)S(1)}, u32[]{:S(2)}) copy-start(s32[32]{0:T(128)S(1)} %fusion.140) | copy-start | bytes 388
  328.4 29.7 %collective-permute-start = (bf16[2048,384]{1,0:T(8,128)(2,1)}, bf16[2048,384]{1,0:T(8,128)(2,1)}, u32[]{:S(2)}, u32[]{:S(2)}) collective-permute-start(bf16[2048,384]{1,0:T(8,128)(2,1)} %bitcast.66), channel_id=1, source_target_pairs={{0,16},{16,0},{32,48},{48,32},{64,80},{80,64},{96,112},{112,96},{1... | collective-permute-start | bytes 4718600 | tf_op jit(solution)/shard_map/ppermute | solution.py:1221
  328.5 29.6 %collective-permute-start.1 = (bf16[384,1024]{0,1:T(8,128)(2,1)}, bf16[384,1024]{0,1:T(8,128)(2,1)}, u32[]{:S(2)}, u32[]{:S(2)}) collective-permute-start(bf16[384,1024]{0,1:T(8,128)(2,1)} %bitcast.12), channel_id=1, source_target_pairs={{0,16},{16,0},{32,48},{48,32},{64,80},{80,64},{96,112},{112,96},{1... | collective-permute-start | bytes 2359304 | tf_op jit(solution)/shard_map/ppermute | solution.py:1221
  362.2 34.0 %copy-start.94 = (f32[256]{0:T(256)S(1)}, f32[256]{0:T(256)}, u32[]{:S(2)}) copy-start(f32[256]{0:T(256)} %copy-done.93) | copy-start | bytes 3076
  477.9 17.0 %collective-permute-start.4 = (bf16[256,1024]{1,0:T(8,128)(2,1)}, bf16[256,1024]{1,0:T(8,128)(2,1)}, u32[]{:S(2)}, u32[]{:S(2)}) collective-permute-start(bf16[256,1024]{1,0:T(8,128)(2,1)} %get-tuple-element.90), channel_id=1, source_target_pairs={{0,16},{16,0},{32,48},{48,32},{64,80},{80,64},{96,112},{112,96},{1... | collective-permute-start | bytes 1572872 | tf_op jit(solution)/shard_map/ppermute | solution.py:1221
  478.0 23.8 %collective-permute-start.6 = (bf16[256,5120]{1,0:T(8,128)(2,1)}, bf16[256,5120]{1,0:T(8,128)(2,1)}, u32[]{:S(2)}, u32[]{:S(2)}) collective-permute-start(bf16[256,5120]{1,0:T(8,128)(2,1)} %add_convert_fusion.1), channel_id=1, source_target_pairs={{0,16},{16,0},{32,48},{48,32},{64,80},{80,64},{96,112},{112,96},{1... | collective-permute-start | bytes 7864328 | tf_op jit(solution)/shard_map/ppermute | solution.py:1221
  484.9 12.9 %collective-permute-start.2 = (bf16[256,1792]{1,0:T(8,128)(2,1)}, bf16[256,1792]{1,0:T(8,128)(2,1)}, u32[]{:S(2)}, u32[]{:S(2)}) collective-permute-start(bf16[256,1792]{1,0:T(8,128)(2,1)} %fusion.51), channel_id=1, source_target_pairs={{0,16},{16,0},{32,48},{48,32},{64,80},{80,64},{96,112},{112,96},{1... | collective-permute-start | bytes 2752520 | tf_op jit(solution)/shard_map/ppermute | solution.py:1221
  485.8 3.4 collective-permute-start.9
  488.9 5.4 collective-permute-start.5
  489.1 8.7 collective-permute-start.3
  494.4 7.4 collective-permute-start.7
  509.6 157.1 %copy-start.5 = (bf16[4096,384]{1,0:T(8,128)(2,1)S(1)}, bf16[4096,384]{1,0:T(8,128)(2,1)}, u32[]{:S(2)}) copy-start(bf16[4096,384]{1,0:T(8,128)(2,1)} %copy-done.4) | copy-start | bytes 9437188
  666.7 35.3 %copy-start.52 = (f32[112,128]{1,0:T(8,128)S(1)}, f32[112,128]{1,0:T(8,128)}, u32[]{:S(2)}) copy-start(f32[112,128]{1,0:T(8,128)} %copy.85) | copy-start | bytes 172036
  766.5 87.3 %copy-start.39 = (f32[384,1024]{1,0:T(8,128)S(1)}, f32[384,1024]{1,0:T(8,128)}, u32[]{:S(2)}) copy-start(f32[384,1024]{1,0:T(8,128)} %get-tuple-element.39) | copy-start | bytes 4718596
  766.5 87.3 %copy-start.96 = (s32[960]{0:T(1024)S(1)}, s32[960]{0:T(1024)}, u32[]{:S(2)}) copy-start(s32[960]{0:T(1024)} %copy-done.95) | copy-start | bytes 11524
  766.5 87.3 %copy-start.98 = (s32[960]{0:T(1024)S(1)}, s32[960]{0:T(1024)}, u32[]{:S(2)}) copy-start(s32[960]{0:T(1024)} %copy-done.97) | copy-start | bytes 11524
  766.5 87.3 %copy-start.100 = (s32[960]{0:T(1024)S(1)}, s32[960]{0:T(1024)}, u32[]{:S(2)}) copy-start(s32[960]{0:T(1024)} %copy-done.99) | copy-start | bytes 11524
  766.6 87.3 %copy-start.102 = (s32[960]{0:T(1024)S(1)}, s32[960]{0:T(1024)}, u32[]{:S(2)}) copy-start(s32[960]{0:T(1024)} %copy-done.101) | copy-start | bytes 11524
  766.6 87.3 %copy-start.107 = (pred[960]{0:T(1024)(128)(4,1)S(1)}, pred[960]{0:T(1024)(128)(4,1)}, u32[]{:S(2)}) copy-start(pred[960]{0:T(1024)(128)(4,1)} %copy-done.106) | copy-start | bytes 2884
  766.6 87.3 %copy-start.109 = (pred[960]{0:T(1024)(128)(4,1)S(1)}, pred[960]{0:T(1024)(128)(4,1)}, u32[]{:S(2)}) copy-start(pred[960]{0:T(1024)(128)(4,1)} %copy-done.108) | copy-start | bytes 2884
  850.3 16.0 %all-to-all-start = ((f32[8,160,128]{2,1,0:T(8,128)}), f32[8,160,128]{2,1,0:T(8,128)S(1)}, u32[]{:S(2)}, u32[]{:S(2)}) async-start(f32[8,160,128]{2,1,0:T(8,128)} %bitcast.144), calls=%async_computation | async-start | bytes 1310720 | tf_op jit(solution)/shard_map/all_to_all | solution.py:1469
  (95 other events, 708.1 us)

commit v6 on v5

--- a/solution.py
+++ b/solution.py
@@ -389,16 +389,16 @@
     )(own)
 
 
-def small_kernel(combine, last, own, out, held, narrow_slots, wide_slots, send, recv):
-    place = my_place()
-    plane = [
-        at_step(at_step(place, "z", k // 4), "x", k % 4) for k in range(1, 16)
-    ]
+def small_peers(place):
+    plane = [at_step(at_step(place, "z", k // 4), "x", k % 4) for k in range(1, 16)]
     column = [
         {**at_step(place, "y", k // 2), "c": lax.rem(place["c"] + k % 2, 2)} for k in range(1, 8)
     ]
-    greet(plane + column)
-    net = Net(send, recv)
+    return plane, column
+
+
+def combine_all(net, place, combine, own, held, narrow_slots, wide_slots):
+    plane, column = small_peers(place)
     value = own
     for number, (slots, index, targets) in enumerate(
         (
@@ -416,7 +416,15 @@
         if number == 0:
             held[...] = total
             value = held
-    out[...] = last(total)
+    return total
+
+
+def small_kernel(combine, last, own, out, held, narrow_slots, wide_slots, send, recv):
+    place = my_place()
+    plane, column = small_peers(place)
+    greet(plane + column)
+    net = Net(send, recv)
+    out[...] = last(combine_all(net, place, combine, own, held, narrow_slots, wide_slots))
     net.finish()
 
 
@@ -451,6 +459,13 @@
 
 
 def add_up(dst, parts):
+    if len(dst.shape) == 4:
+
+        @pl.loop(0, dst.shape[0])
+        def _(k):
+            add_up(dst.at[k], [part.at[k] for part in parts])
+
+        return
     if len(dst.shape) == 3:
         step = max(1, min(dst.shape[0], 32768 // (dst.shape[1] * dst.shape[2])))
 
@@ -509,7 +524,7 @@
 FAR_FIRST = (2, 1, 3, 0)
 
 
-def start_scatter(net, place, order, source, gots, out, acc=None):
+def start_scatter(net, place, order, source, gots, out, acc=None, parts=4):
     rows = out.shape[0] // 2
     halves = (pl.ds(0, rows), pl.ds(rows, rows))
     lead = ("z", "x", "y")[: len(order)]
@@ -520,11 +535,12 @@
     def summed(sel, half):
         if acc is None:
             return block({order[0]: place[order[0]], **sel}, half)
-        return acc.at[tuple(pick(sel.get(axis)) for axis in order[1:]) + (halves[half],)]
+        rest = [axis for axis in lead if axis != order[0]]
+        return acc.at[tuple(pick(sel.get(axis)) for axis in rest) + (halves[half],)]
 
     stream = {"first": {}, "rest": []}
     one, two = order[:2]
-    for sub, far in enumerate(FAR_FIRST):
+    for sub, far in enumerate(FAR_FIRST if parts == 4 else ()):
         at_two = at_step(place, two, far)[two]
         stream["first"][far] = Ring(
             net,
@@ -533,6 +549,17 @@
             lambda k, half, at_two=at_two: block({one: k, two: at_two}, half),
             lambda k, sub=sub: gots[0].at[sub, k],
             lambda half, at_two=at_two: summed({two: at_two}, half),
+        )
+    if parts == 1:
+        stream["rest"].append(
+            Ring(
+                net,
+                place,
+                one,
+                lambda k, half: block({one: k}, half),
+                lambda k: gots[0].at[k],
+                lambda half: summed({}, half),
+            )
         )
     for number in range(1, len(order)):
         done = {axis: place[axis] for axis in order[1:number]}
@@ -591,23 +618,27 @@
             stream["rest"][number + 1].send_all()
 
 
-def finish_scatter(streams):
-    pass_first(streams)
-    close_first(streams)
+def send_whole(streams):
+    for stream in streams:
+        stream["rest"][0].send_all()
+
+
+def finish_whole(streams):
     for number in range(len(streams[0]["rest"])):
         pass_rest(streams, number)
         close_rest(streams, number)
 
 
-def got_shapes(depth, rows, lanes, first, later):
+def got_shapes(depth, rows, lanes, first, later, parts=4):
     half = rows // 2
-    return [
-        pltpu.VMEM(
-            ((4, 6) if number == 0 else (6,)) + (4,) * (depth - max(number, 1) - 1) + (half, lanes),
-            later if number else first,
-        )
-        for number in range(depth)
-    ]
+    shapes = []
+    for number in range(depth):
+        if number == 0 and parts == 4:
+            lead = (4, 6) + (4,) * (depth - 2)
+        else:
+            lead = (6,) + (4,) * (depth - 1 - number)
+        shapes.append(pltpu.VMEM(lead + (half, lanes), later if number else first))
+    return shapes
 
 
 def row_sums_kernel(part, out, *scratch):
@@ -634,22 +665,23 @@
             scratch[3 + 3 * k : 6 + 3 * k],
             out.at[:, pl.ds(*lanes)],
             accs[k],
+            1,
         )
         for k, (order, lanes) in enumerate(zip(ORDERS, LANE_PARTS))
     ]
-    send_first(streams)
-    finish_scatter(streams)
+    send_whole(streams)
+    finish_whole(streams)
     net.finish()
 
 
 def scatter_rows(part):
     scratch = [pltpu.VMEM((4, 4, 4, 32, lanes), part.dtype) for _, lanes in LANE_PARTS]
     for _, lanes in LANE_PARTS:
-        scratch += got_shapes(3, 32, lanes, part.dtype, F32)
+        scratch += got_shapes(3, 32, lanes, part.dtype, F32, 1)
     scratch += [pltpu.VMEM((4, 4, 32, lanes), F32) for _, lanes in LANE_PARTS]
     scratch += [
-        pltpu.SemaphoreType.DMA((108,)),
-        pltpu.SemaphoreType.DMA((108,)),
+        pltpu.SemaphoreType.DMA((54,)),
+        pltpu.SemaphoreType.DMA((54,)),
         pltpu.SemaphoreType.DMA((3,)),
     ]
     return pl.pallas_call(
@@ -665,21 +697,16 @@
     )(part)
 
 
-GRAD_STREAMS = (
-    (("y", "x", "z"), 0, 0, 224),
-    (("y", "z", "x"), 1, 0, 224),
-    (("x", "y", "z"), 2, 0, 128),
-    (("z", "y", "x"), 2, 128, 96),
-)
+GRAD_ORDERS = (("y", "x", "z"), ("y", "z", "x"), ("x", "z", "y"))
 
 
 def grads_kernel(dx, ids, di, do, dg, dd, out, weights_out, *scratch):
     rows, table, chosen = scratch[:3]
     held = scratch[3:6]
     gots = scratch[6:10]
-    weight_gots = scratch[10:22]
-    accs = scratch[22:26]
-    send, recv, local = scratch[26:]
+    weight_gots = scratch[10:19]
+    accs = scratch[19:22]
+    send, recv, local = scratch[22:]
     place = my_place()
     moves = [(dx, rows.at[place["y"], place["c"]])]
     for y in range(4):
@@ -699,9 +726,7 @@
             moves.append((di.at[z, :, pl.ds(0, 64), lanes], held[1].at[z, :, y, pl.ds(160, 64)]))
             moves.append((di.at[z, :, pl.ds(64, 48), lanes], held[2].at[z, :, y, pl.ds(160, 48)]))
     copies = [pltpu.make_async_copy(src, dst, local.at[k]) for k, (src, dst) in enumerate(moves)]
-    for copy in copies:
-        copy.start()
-    held[2][:, :, :, 208:224, :] = jnp.zeros((4, 4, 4, 16, 128), BF16)
+    copies[0].start()
     greet(neighbours(place))
     copies[0].wait()
 
@@ -711,6 +736,10 @@
     net = Net(send, recv)
     spread = Spread(net, place, ("y",), [(in_rows, ((0, 128), (128, 128)))], True)
     spread.begin()
+    for copy in copies[1:]:
+        copy.start()
+    held[2][:, :, :, 208:224, :] = jnp.zeros((4, 4, 4, 16, 128), BF16)
+    spread.relay()
     for copy in copies[1:]:
         copy.wait()
     weights = [
@@ -718,18 +747,17 @@
             net,
             place,
             order,
-            held[which].at[:, :, :, pl.ds(first, count)],
+            held[k],
             weight_gots[3 * k : 3 * k + 3],
-            weights_out.at[which, pl.ds(first, count)],
+            weights_out.at[k],
             accs[k],
+            1,
         )
-        for k, (order, which, first, count) in enumerate(GRAD_STREAMS)
-    ]
-    send_first(weights[2:])
-    spread.relay()
+        for k, order in enumerate(GRAD_ORDERS)
+    ]
     spread.near()
     spread.far()
-    send_first(weights[:2])
+    send_whole(weights)
     spread.end()
     base = (place["y"] * 2 + place["c"]) * 16
 
@@ -778,37 +806,33 @@
     by_x[2].send_down()
     by_z[2].send_up()
     by_z[2].send_down()
-    pass_first(weights[2:])
     third = lambda dz: parts(3, lambda k: (further("z", dz), further("x", k + 3)))
     third(1)
     for ring in (by_x[1], by_z[1], by_z[3], by_z[0]):
         ring.send_up()
     by_x[1].send_down()
-    pass_first(weights[:2])
-    close_first(weights[2:])
+    pass_rest(weights, 0)
     third(3)
     for ring in (by_x[3], by_z[1], by_z[3], by_z[0]):
         ring.send_down()
     by_x[3].send_up()
-    close_first(weights[:2])
     third(0)
     by_x[0].send_up()
     by_x[0].send_down()
     pass_first(streams)
-    pass_rest(weights[2:], 0)
-    close_rest(weights[2:], 0)
-    pass_rest(weights[:2], 0)
-    close_rest(weights[:2], 0)
+    close_rest(weights, 0)
     close_first(streams)
     pass_rest(weights, 1)
     close_rest(weights, 1)
     pass_rest(streams, 0)
+    pass_rest(weights, 2)
     close_rest(streams, 0)
+    close_rest(weights, 2)
     net.finish()
 
 
 def scatter_grads(dx, ids, di, do, dg, dd):
-    count = 4 * 36 + 2 * 30 + 14
+    count = 3 * 18 + 2 * 30 + 14
     scratch = [
         pltpu.VMEM((4, 2, 256, DP), BF16),
         pltpu.VMEM((4, 4, 384, DP), BF16),
@@ -816,9 +840,8 @@
     ]
     scratch += [pltpu.VMEM((4, 4, 4, 224, 128), BF16)] * 3
     scratch += got_shapes(2, 192, DP, BF16, BF16) * 2
-    for _, _, _, rows in GRAD_STREAMS:
-        scratch += got_shapes(3, rows, 128, BF16, F32)
-    scratch += [pltpu.VMEM((4, 4, rows, 128), F32) for _, _, _, rows in GRAD_STREAMS]
+    scratch += got_shapes(3, 224, 128, BF16, F32, 1) * 3
+    scratch += [pltpu.VMEM((4, 4, 224, 128), F32)] * 3
     scratch += [
         pltpu.SemaphoreType.DMA((count,)),
         pltpu.SemaphoreType.DMA((count,)),
@@ -939,27 +962,36 @@
     )(*parts)
 
 
-def gram_kernel(pieces, turned, gram, part, *scratch):
+def gram_kernel(own, moments, grads, summed, new, turned, gram, part, *scratch):
     gots = scratch[:4]
-    send, recv, local = scratch[4:]
+    held, narrow_slots, wide_slots, send, recv = scratch[4:]
     place = my_place()
-    wides = [
-        {**at_step(place, "y", step), "c": core}
-        for step in (2, 1, 3, 0)
-        for core in (place["c"], 1 - place["c"])
-    ][:-2] + [other_core(place)]
-    greet(wides + neighbours(place, ("x", "z"), False))
+    plane, column = small_peers(place)
+    greet(plane + column)
     net = Net(send, recv)
-
-    def lanes_from(who):
-        return pl.ds(pl.multiple_of((who["c"] * 4 + who["y"]) * 128, 128), 128)
-
-    arrivals = [net.put(pieces.at[who["y"]], turned.at[:, lanes_from(place)], who) for who in wides]
-    copy = pltpu.make_async_copy(pieces.at[place["y"]], turned.at[:, lanes_from(place)], local)
-    copy.start()
-    copy.wait()
+    total = combine_all(net, place, jnp.add, own, held, narrow_slots, wide_slots)
+    summed[...] = total
+    count = total[24:25, 3:4] * (1.0 / 128.0)
+    squares = total[24:25, 0:1] + jnp.sum(total[:24] * total[:24], keepdims=True)
+    factor = jnp.minimum(1.0, CLIP_NORM / (jnp.sqrt(squares) / count)) / count
+
+    @pl.loop(0, 4)
+    def _(k):
+        new[k] = MOMENTUM * moments[k] + factor * grads[k]
+
+    def lanes_from(y, c):
+        return pl.ds(pl.multiple_of((c * 4 + y) * 128, 128), 128)
+
+    mine = lanes_from(place["y"], place["c"])
+    arrivals = []
+    for step in (2, 1, 3):
+        who = at_step(place, "y", step)
+        arrivals.append(net.put(new.at[who["y"]], turned.at[:, mine], who))
+    turned[:, mine] = new[place["y"]]
     for arrival in arrivals:
         arrival.wait_recv()
+    half = turned.at[:, pl.ds(pl.multiple_of(place["c"] * 512, 512), 512)]
+    net.put(half, half, other_core(place)).wait_recv()
     @pl.loop(0, 4)
     def _(k):
         rows = pl.ds(pl.multiple_of(place["c"] * 512 + k * 128, 128), 128)
@@ -975,12 +1007,19 @@
     mine = gram.at[place["c"], place["z"], place["x"]]
     streams = [
         start_scatter(
-            net, place, order, part.at[:, :, :, lane], gots[2 * k : 2 * k + 2], mine.at[:, lane]
+            net,
+            place,
+            order,
+            part.at[:, :, :, lane],
+            gots[2 * k : 2 * k + 2],
+            mine.at[:, lane],
+            None,
+            1,
         )
         for k, (order, lane) in enumerate(zip(orders, lanes))
     ]
-    send_first(streams)
-    finish_scatter(streams)
+    send_whole(streams)
+    finish_whole(streams)
 
     def in_gram(lane):
         def region(sel, rows):
@@ -995,29 +1034,33 @@
     net.finish()
 
 
-def gram_of(pieces):
-    count = 7 + 2 * 30 + 44
+def gram_of(packed, moments, grads):
+    count = 22 + 4 + 2 * 12 + 40
     scratch = [pltpu.VMEM((4, 4, 32, DP), F32)]
-    scratch += got_shapes(2, 32, 512, F32, F32) * 2
+    scratch += got_shapes(2, 32, 512, F32, F32, 1) * 2
     scratch += [
+        pltpu.VMEM((32, 128), F32),
+        pltpu.VMEM((16, 32, 128), F32),
+        pltpu.VMEM((8, 32, 128), F32),
         pltpu.SemaphoreType.DMA((count,)),
         pltpu.SemaphoreType.DMA((count,)),
-        pltpu.SemaphoreType.DMA,
     ]
     return pl.pallas_call(
         gram_kernel,
         out_shape=[
+            jax.ShapeDtypeStruct((32, 128), F32),
+            jax.ShapeDtypeStruct((4, 320, 128), F32),
             jax.ShapeDtypeStruct((320, DP), F32),
             jax.ShapeDtypeStruct((2, 4, 4, 32, DP), F32),
         ],
-        in_specs=[VMEM],
-        out_specs=[VMEM, VMEM],
+        in_specs=[VMEM] * 3,
+        out_specs=[VMEM] * 4,
         scratch_shapes=scratch,
         compiler_params=pltpu.CompilerParams(
             collective_id=7, has_side_effects=True, vmem_limit_bytes=40 << 20
         ),
         name="gram_sums",
-    )(pieces)
+    )(packed, moments, grads)
 
 
 def split(value, count):
@@ -1441,27 +1484,22 @@
         summed_grads[2, :160],
     )
 
+    def stacked(shards):
+        return jnp.stack([jnp.pad(s, ((0, 320 - s.shape[0]), (0, 0))) for s in shards])
+
     table_grad = table_grad + table_grad_rows
-
-    squares = sum(jnp.sum(shard * shard) for shard in grad_shards) + jnp.sum(
-        table_grad * table_grad
-    )
+    squares = jnp.sum(summed_grads * summed_grads) + jnp.sum(table_grad * table_grad)
     table_grad = dot(table_grad, features, 1, 1, HIGH)
     gain_grads = jnp.stack([d_gain_attn, d_gain_mlp, d_gain_final]).reshape(24, 128)
-    scalars = jnp.pad(jnp.stack([squares, hit_sum, logit_sum]), (0, 125))
+    scalars = jnp.pad(jnp.stack([squares, hit_sum, logit_sum, token_count]), (0, 124))
     packed = jnp.pad(jnp.concatenate([gain_grads, scalars[None]]), ((0, 7), (0, 0)))
-    summed = small_all(packed, jnp.add, lambda v: v, (32, 128), 5, "global_sums")
+    old_moments = stacked([to_shard(m, rows) for m, rows in zip(moments, (RI, RO, RG, RD))])
+
+    summed, new_shards, turned, gram = gram_of(packed, old_moments, stacked(grad_shards))
     gain_grad = unpad_features(summed[:24].reshape(3, DP))
     loss_total = loss_known - (1.0 - SMOOTH) * summed[24, 1] - SMOOTH / V * summed[24, 2]
     grad_norm = jnp.sqrt(summed[24, 0] + jnp.sum(gain_grad * gain_grad)) / token_count
     factor = jnp.minimum(1.0, CLIP_NORM / grad_norm) / token_count
-
-    new_shards = [
-        MOMENTUM * to_shard(moment, rows) + factor * grad
-        for moment, rows, grad in zip(moments, (RI, RO, RG, RD), grad_shards)
-    ]
-    pieces = jnp.stack([jnp.pad(s, ((0, 320 - s.shape[0]), (0, 0))) for s in new_shards])
-    turned, gram = gram_of(pieces)
     gram = gram.reshape(DP, DP)
     turned = lax.dynamic_slice_in_dim(turned, core * 160, 160)
     current = newton(gram, turned)

time: 885 us -> 864 us (0.976)
  Pallas kernels: 585 us -> 572 us
    pallas_call x2 -> x1, Pallas kernels: 32.7 us -> 18.4 us  [small_all(): pl.pallas_call(functools.partial(small_kernel, combine, last), out_shape=...]
    pallas_call x1, Pallas kernels: 153 us -> 140 us  [scatter_grads(): pl.pallas_call(grads_kernel, out_shape=[jax.ShapeDtypeStruct((384, DP), F...]
    pallas_call x1, Pallas kernels: 59.7 us -> 73 us  [gram_of(): pl.pallas_call(gram_kernel, out_shape=[jax.ShapeDtypeStruct((32, 128), F3...]
    unnamed x250 -> x230, local copies, waits for them, and re-layouts: 23.7 us -> 27.6 us
where the time goes in v6:
time: 864 us; the launch traced here: 856 us
  Pallas kernels  572 us (66%)
  matrix products  128 us (15%)
  local copies, waits for them, and re-layouts  68.7 us (8%)
  other arithmetic  67.5 us (8%)
  between operations  12.5 us (1%)
    pallas_call x1, Pallas kernels, fetch(): pl.pallas_call(fetch_kernel, out_shape=shapes, in_specs=[ANY] * 6 + [pl.B...  152 us
    pallas_call x1, Pallas kernels, scatter_grads(): pl.pallas_call(grads_kernel, out_shape=[jax.ShapeDtypeStruct((384, DP), F...  140 us
    dot_general x20, matrix products, dot(): lax.dot_general(left, right, (((left_axis,), (right_axis,)), ((), ())), p...  95 us
    pallas_call x1, Pallas kernels, newton(): pl.pallas_call(newton_kernel, out_shape=jax.ShapeDtypeStruct((160, DP), F...  82.2 us
    pallas_call x1, Pallas kernels, gram_of(): pl.pallas_call(gram_kernel, out_shape=[jax.ShapeDtypeStruct((32, 128), F3...  73 us
    pallas_call x1, Pallas kernels, gather_rows(): pl.pallas_call(rows_kernel, out_shape=jax.ShapeDtypeStruct((4, 4, 4, 2, 3...  32.9 us
    pallas_call x1, Pallas kernels, scatter_rows(): pl.pallas_call(row_sums_kernel, out_shape=jax.ShapeDtypeStruct((32, DP),...  31.9 us
    unnamed x230, local copies, waits for them, and re-layouts  27.6 us
  transfers between devices with their start and end apart: 11, of which 0 were waited for; matrix products, arithmetic and copies ran while one was open for 18% of the time, Pallas kernels for 12%

profile of v6, /device:TPU:1, one launch (start us, length us, event | category | flops | bytes accessed | tf_op | source)
XLA Modules:
  0.0 855.7 jit_solution(12552394730401577424)
XLA Ops:
  14.2 4.8 convolution_convert_fusion.4
  22.2 151.9 %fetch.1 = (bf16[4,4,112,1024]{3,2,1,0:T(8,128)(2,1)}, bf16[2,4,2,64,1024]{4,3,2,1,0:T(8,128)(2,1)}, bf16[2,2,2,4,160,1024]{5,4,3,2,1,0:T(8,128)(2,1)}, bf16[2,4...) custom-call(bf16[112,128]{1,0:T(8,128)(2,1)} %copy.63.gi, ...), custom_call_target="tpu_custom_call" | custom-call | tf_op jit(solution)/shard_map/fetch/pallas_call | solution.py:323
  189.2 22.0 %gather_keys.1 = bf16[4,320,1024]{2,1,0:T(8,128)(2,1)S(1)} custom-call(bf16[4,320,128]{2,1,0:T(8,128)(2,1)S(1)} %pad_maximum_fusion.6.own), custom_call_target="tpu_custom_call" | custom-call | tf_op jit(solution)/shard_map/gather_keys/pallas_call | solution.py:886
  230.6 6.0 fusion.169
  242.1 4.5 multiply_reduce_fusion.8
  248.4 32.9 %gather_rows.1 = bf16[4,4,4,2,32,1024]{5,4,3,2,1,0:T(8,128)(2,1)S(1)} custom-call(bf16[32,1024]{1,0:T(8,128)(2,1)S(1)} %gather_fusion), custom_call_target="tpu_custom_call" | custom-call | tf_op jit(solution)/shard_map/gather_rows/pallas_call | solution.py:375
  284.6 7.7 fusion.168
  292.4 6.0 multiply_reduce_fusion.1
  299.1 18.4 %row_totals.1 = f32[32,128]{1,0:T(8,128)} custom-call(f32[2,32,128]{2,1,0:T(8,128)} %pad_maximum_fusion.9.own), custom_call_target="tpu_custom_call" | custom-call | tf_op jit(solution)/shard_map/row_totals/pallas_call | solution.py:434
  318.3 7.7 multiply_convert_fusion
  346.2 3.5 fusion.170
  349.8 4.0 add_convert_fusion
  353.8 31.9 %scatter_rows.1 = f32[32,1024]{1,0:T(8,128)S(1)} custom-call(bf16[4,4,4,32,1024]{4,3,2,1,0:T(8,128)(2,1)S(1)} %bitcast.422), custom_call_target="tpu_custom_call" | custom-call | tf_op jit(solution)/shard_map/scatter_rows/pallas_call | solution.py:687
  387.7 6.6 fusion.67
  396.2 4.8 multiply_reduce_fusion.4
  402.7 3.9 convolution_convert_fusion.7
  406.7 8.1 fusion.4
  414.8 4.7 fusion.34
  419.5 4.9 fusion.1
  425.8 9.3 %fusion.6 = bf16[5,3,128,1024]{2,3,1,0:T(8,128)(2,1)} fusion(f32[5,1024,128,3]{2,1,3,0:T(8,128)} %get-tuple-element.167, f32[5,3,128,1024]{2,3,1,0:T(8,128)} %copy-done.4, f32[5,3,128]{2,1,0:T(4,128)S(1)} %get-tuple-element.166, f32[5,3,128]{2,1,0:T(4,128)S(1)} %log_add_fusion.1), kind=kLoop, calls=%fused_computation.19 | loop fusion | flops 7864320 | bytes 19676160 | tf_op jit(solution)/shard_map/convert_element_type | solution.py:1430
  438.5 9.4 %fusion.3 = bf16[5,3,128,1024]{2,3,1,0:T(8,128)(2,1)} fusion(f32[5,1024,128,3]{2,1,3,0:T(8,128)} %get-tuple-element.169, f32[5,3,128,1024]{2,3,1,0:T(8,128)} %copy-done.3, f32[5,3,128]{2,1,0:T(4,128)S(1)} %get-tuple-element.168, f32[5,3,128]{2,1,0:T(4,128)S(1)} %log_add_fusion), kind=kLoop, calls=%fused_computation.14 | loop fusion | flops 7864320 | bytes 19676160 | tf_op jit(solution)/shard_map/convert_element_type | solution.py:1430
  451.4 20.1 %sum_keys.1 = f32[4,320,128]{2,1,0:T(8,128)S(1)} custom-call(f32[320,1024]{1,0:T(8,128)S(1)} %bitcast.423, f32[320,1024]{1,0:T(8,128)S(1)} %bitcast.424, f32[320,1024]{1,0:T(8,128)S(1)} %bitcast.425, f32[320,1024]{1,0:T(8,128)S(1)} %bitcast.426), custom_call_target="tpu_custom_call" | custom-call | tf_op jit(solution)/shard_map/sum_keys/pallas_call | solution.py:946
  477.2 3.7 fusion.51
  484.9 4.8 convolution_convert_fusion.1
  492.8 3.9 convolution_convert_fusion.2
  496.7 7.8 convolution_convert_fusion
  504.5 139.9 %scatter_grads.1 = (f32[384,1024]{1,0:T(8,128)}, f32[3,224,128]{2,1,0:T(8,128)}) custom-call(bf16[256,1024]{1,0:T(8,128)(2,1)} %get-tuple-element.107.dx, s32[1,2048]{1,0:T(1,128)} %bitcast.503, bf16[4,4,112,512]{3,2,1,0:T(8,128)(2,1)} %bitcast.462, bf16[2,4,2,64,512]{4,3,2,1,0:T(8,128)(2,1)} %bitcast.467, bf16[2,2,2,4,160,512]{5,4,3,2,1,0:T(8,128)(2,1)} %bitcast.441, ...), custom_call_target="tpu_custom_call" | custom-call | tf_op jit(solution)/shard_map/scatter_grads/pallas_call | solution.py:850
  648.5 10.0 %multiply_reduce_fusion.2 = (f32[]{:T(128)}, f32[384,1024]{1,0:T(8,128)}) fusion(f32[384,1024]{1,0:T(8,128)} %get-tuple-element.41, bf16[4096,384]{1,0:T(8,128)(2,1)} %copy-done.7, bf16[4096,1024]{1,0:T(8,128)(2,1)} %bitcast.421), kind=kOutput, calls=%fused_computation.97 | convolution fusion | flops 3222405120 | bytes 14680068 | tf_op jit(solution)/shard_map/dot_general | solution.py:1224
  661.9 73.0 %gram_sums.1 = (f32[32,128]{1,0:T(8,128)S(1)}, f32[4,320,128]{2,1,0:T(8,128)S(1)}, f32[320,1024]{1,0:T(8,128)S(1)}, f32[2,4,4,32,1024]{4,3,2,1,0:T(8,128)S(1)}) custom-call(f32[32,128]{1,0:T(8,128)S(1)} %select_maximum_fusion.1.own, f32[4,320,128]{2,1,0:T(8,128)S(1)} %pad_maximum_fusion.2.moments, f32[4,320,128]{2,1,0:T(8,128)S(1)} %pad_maximum_fusion.3.grads), custom_call_target="tpu_custom_call" | custom-call | tf_op jit(solution)/shard_map/gram_sums/pallas_call | solution.py:1048
  741.8 82.2 %newton.1 = f32[160,1024]{1,0:T(8,128)S(1)} custom-call(f32[1024,1024]{1,0:T(8,128)S(1)} %bitcast.427, f32[160,1024]{1,0:T(8,128)S(1)} %constant_dynamic-slice_fusion.turned), custom_call_target="tpu_custom_call" | custom-call | tf_op jit(solution)/shard_map/newton/pallas_call | solution.py:1174
  825.4 3.7 all-to-all-start
  829.8 8.6 %fusion.154 = (bf16[384,960]{0,1:T(8,128)(2,1)}, f32[384,960]{0,1:T(8,128)}, f32[384,960]{0,1:T(8,128)}, f32[384,960]{0,1:T(8,128)}) fusion(f32[384,960]{0,1:T(8,128)} %param.27, f32[384,960]{0,1:T(8,128)} %param.33, f32[384,960]{0,1:T(8,128)} %param.32, s32[960]{0:T(1024)} %copy-done.89, s32[960]{0:T(1024)} %copy-done.91, s32[960]{0:T(1024)} %copy-done.87, ...), kind=kOutput, calls=%fused_computation.359 | convolution fusion | flops 2310537216 | bytes 12747652 | tf_op jit(solution)/shard_map/dot_general | solution.py:1224
  (476 shorter events, 132.9 us)
Async XLA Ops:
  0.7 226.4 %copy-start.87 = (s32[960]{0:T(1024)}, s32[960]{0:T(1024)S(1)}, u32[]{:S(2)}) copy-start(s32[960]{0:T(1024)S(1)} %get-tuple-element.175) | copy-start | bytes 11524
  0.7 226.4 %copy-start.89 = (s32[960]{0:T(1024)}, s32[960]{0:T(1024)S(1)}, u32[]{:S(2)}) copy-start(s32[960]{0:T(1024)S(1)} %get-tuple-element.176) | copy-start | bytes 11524
  0.7 226.3 %copy-start.91 = (s32[960]{0:T(1024)}, s32[960]{0:T(1024)S(1)}, u32[]{:S(2)}) copy-start(s32[960]{0:T(1024)S(1)} %get-tuple-element.177) | copy-start | bytes 11524
  0.7 226.3 %copy-start.93 = (s32[960]{0:T(1024)}, s32[960]{0:T(1024)S(1)}, u32[]{:S(2)}) copy-start(s32[960]{0:T(1024)S(1)} %get-tuple-element.178) | copy-start | bytes 11524
  0.7 226.3 %copy-start.96 = (pred[960]{0:T(1024)(128)(4,1)}, pred[960]{0:T(1024)(128)(4,1)S(1)}, u32[]{:S(2)}) copy-start(pred[960]{0:T(1024)(128)(4,1)S(1)} %get-tuple-element.173) | copy-start | bytes 2884
  0.7 226.3 %copy-start.98 = (pred[960]{0:T(1024)(128)(4,1)}, pred[960]{0:T(1024)(128)(4,1)S(1)}, u32[]{:S(2)}) copy-start(pred[960]{0:T(1024)(128)(4,1)S(1)} %get-tuple-element.174) | copy-start | bytes 2884
  187.5 41.9 %copy-start.10 = (f32[32,8,8,128]{3,2,1,0:T(8,128)}, f32[32,8,8,128]{3,2,1,0:T(8,128)S(1)}, u32[]{:S(2)}) copy-start(f32[32,8,8,128]{3,2,1,0:T(8,128)S(1)} %bitcast_convert_fusion) | copy-start | bytes 3145732
  187.7 24.9 %copy-start.35 = (f32[256,64]{0,1:T(8,128)}, f32[256,64]{0,1:T(8,128)S(1)}, u32[]{:S(2)}) copy-start(f32[256,64]{0,1:T(8,128)S(1)} %get-tuple-element.179) | copy-start | bytes 196612
  187.8 24.9 %copy-start.37 = (f32[256,64]{0,1:T(8,128)}, f32[256,64]{0,1:T(8,128)S(1)}, u32[]{:S(2)}) copy-start(f32[256,64]{0,1:T(8,128)S(1)} %get-tuple-element.180) | copy-start | bytes 196612
  213.0 17.3 %copy-start.67 = (f32[1024]{0:T(1024)}, f32[1024]{0:T(1024)S(1)}, u32[]{:S(2)}) copy-start(f32[1024]{0:T(1024)S(1)} %mul.812) | copy-start | bytes 12292
  240.7 243.6 %collective-permute-start.8 = (bf16[256,2560]{1,0:T(8,128)(2,1)}, bf16[256,2560]{1,0:T(8,128)(2,1)}, u32[]{:S(2)}, u32[]{:S(2)}) collective-permute-start(bf16[256,2560]{1,0:T(8,128)(2,1)} %multiply_convert_fusion.1), channel_id=1, source_target_pairs={{0,16},{16,0},{32,48},{48,32},{64,80},{80,64},{96,112},{112,96},{1... | collective-permute-start | bytes 3932168 | tf_op jit(solution)/shard_map/ppermute | solution.py:1264
  246.6 34.7 %copy-start.85 = (f32[256]{0:T(256)}, f32[256]{0:T(256)S(1)}, u32[]{:S(2)}) copy-start(f32[256]{0:T(256)S(1)} %get-tuple-element.161) | copy-start | bytes 3076
  246.7 34.6 %copy-start.54 = (f32[1024]{0:T(1024)}, f32[1024]{0:T(1024)S(1)}, u32[]{:S(2)}) copy-start(f32[1024]{0:T(1024)S(1)} %mul.821) | copy-start | bytes 12292
  246.7 34.6 %copy-start.69 = (f32[256]{0:T(256)}, f32[256]{0:T(256)S(1)}, u32[]{:S(2)}) copy-start(f32[256]{0:T(256)S(1)} %fusion.137) | copy-start | bytes 3076
  247.0 34.4 %copy-start.100 = (s32[32]{0:T(128)}, s32[32]{0:T(128)S(1)}, u32[]{:S(2)}) copy-start(s32[32]{0:T(128)S(1)} %fusion.138) | copy-start | bytes 388
  328.4 21.3 %collective-permute-start = (bf16[2048,384]{1,0:T(8,128)(2,1)}, bf16[2048,384]{1,0:T(8,128)(2,1)}, u32[]{:S(2)}, u32[]{:S(2)}) collective-permute-start(bf16[2048,384]{1,0:T(8,128)(2,1)} %bitcast.66), channel_id=1, source_target_pairs={{0,16},{16,0},{32,48},{48,32},{64,80},{80,64},{96,112},{112,96},{1... | collective-permute-start | bytes 4718600 | tf_op jit(solution)/shard_map/ppermute | solution.py:1264
  328.5 21.2 %collective-permute-start.1 = (bf16[384,1024]{0,1:T(8,128)(2,1)}, bf16[384,1024]{0,1:T(8,128)(2,1)}, u32[]{:S(2)}, u32[]{:S(2)}) collective-permute-start(bf16[384,1024]{0,1:T(8,128)(2,1)} %bitcast.12), channel_id=1, source_target_pairs={{0,16},{16,0},{32,48},{48,32},{64,80},{80,64},{96,112},{112,96},{1... | collective-permute-start | bytes 2359304 | tf_op jit(solution)/shard_map/ppermute | solution.py:1264
  353.7 33.3 %copy-start.9 = (f32[256,1024]{1,0:T(8,128)S(1)}, f32[256,1024]{1,0:T(8,128)}, u32[]{:S(2)}) copy-start(f32[256,1024]{1,0:T(8,128)} %copy-done.8) | copy-start | bytes 3145732
  353.8 33.3 %copy-start.55 = (f32[1024]{0:T(1024)S(1)}, f32[1024]{0:T(1024)}, u32[]{:S(2)}) copy-start(f32[1024]{0:T(1024)} %copy-done.54) | copy-start | bytes 12292
  353.8 33.3 %copy-start.70 = (f32[256]{0:T(256)S(1)}, f32[256]{0:T(256)}, u32[]{:S(2)}) copy-start(f32[256]{0:T(256)} %copy-done.69) | copy-start | bytes 3076
  353.8 33.6 %copy-start.86 = (f32[256]{0:T(256)S(1)}, f32[256]{0:T(256)}, u32[]{:S(2)}) copy-start(f32[256]{0:T(256)} %copy-done.85) | copy-start | bytes 3076
  451.4 20.9 %copy-start.6 = (bf16[5,3,128,1024]{2,3,1,0:T(8,128)(2,1)S(1)}, bf16[5,3,128,1024]{2,3,1,0:T(8,128)(2,1)}, u32[]{:S(2)}) copy-start(bf16[5,3,128,1024]{2,3,1,0:T(8,128)(2,1)} %fusion.3) | copy-start | bytes 11796484
  451.4 20.9 %copy-start.18 = (bf16[1,320,1024]{2,1,0:T(8,128)(2,1)S(1)}, bf16[1,320,1024]{2,1,0:T(8,128)(2,1)}, u32[]{:S(2)}) copy-start(bf16[1,320,1024]{2,1,0:T(8,128)(2,1)} %copy-done.17) | copy-start | bytes 1966084
  474.7 15.2 %collective-permute-start.4 = (bf16[256,1024]{1,0:T(8,128)(2,1)}, bf16[256,1024]{1,0:T(8,128)(2,1)}, u32[]{:S(2)}, u32[]{:S(2)}) collective-permute-start(bf16[256,1024]{1,0:T(8,128)(2,1)} %get-tuple-element.92), channel_id=1, source_target_pairs={{0,16},{16,0},{32,48},{48,32},{64,80},{80,64},{96,112},{112,96},{1... | collective-permute-start | bytes 1572872 | tf_op jit(solution)/shard_map/ppermute | solution.py:1264
  474.8 21.9 %collective-permute-start.6 = (bf16[256,5120]{1,0:T(8,128)(2,1)}, bf16[256,5120]{1,0:T(8,128)(2,1)}, u32[]{:S(2)}, u32[]{:S(2)}) collective-permute-start(bf16[256,5120]{1,0:T(8,128)(2,1)} %add_convert_fusion.1), channel_id=1, source_target_pairs={{0,16},{16,0},{32,48},{48,32},{64,80},{80,64},{96,112},{112,96},{1... | collective-permute-start | bytes 7864328 | tf_op jit(solution)/shard_map/ppermute | solution.py:1264
  480.8 11.9 %collective-permute-start.2 = (bf16[256,1792]{1,0:T(8,128)(2,1)}, bf16[256,1792]{1,0:T(8,128)(2,1)}, u32[]{:S(2)}, u32[]{:S(2)}) collective-permute-start(bf16[256,1792]{1,0:T(8,128)(2,1)} %fusion.51), channel_id=1, source_target_pairs={{0,16},{16,0},{32,48},{48,32},{64,80},{80,64},{96,112},{112,96},{1... | collective-permute-start | bytes 2752520 | tf_op jit(solution)/shard_map/ppermute | solution.py:1264
  481.0 3.5 collective-permute-start.9
  484.3 5.4 collective-permute-start.5
  484.5 8.3 collective-permute-start.3
  489.7 7.0 collective-permute-start.7
  741.8 87.9 %copy-start.39 = (f32[384,1024]{1,0:T(8,128)S(1)}, f32[384,1024]{1,0:T(8,128)}, u32[]{:S(2)}) copy-start(f32[384,1024]{1,0:T(8,128)} %get-tuple-element.41) | copy-start | bytes 4718596
  825.4 20.8 %all-to-all-start = ((f32[8,160,128]{2,1,0:T(8,128)}), f32[8,160,128]{2,1,0:T(8,128)S(1)}, u32[]{:S(2)}, u32[]{:S(2)}) async-start(f32[8,160,128]{2,1,0:T(8,128)} %bitcast.148), calls=%async_computation | async-start | bytes 1310720 | tf_op jit(solution)/shard_map/all_to_all | solution.py:1507
  (85 other events, 441.1 us)

commit v7 on v6

--- a/solution.py
+++ b/solution.py
@@ -811,16 +811,20 @@
     for ring in (by_x[1], by_z[1], by_z[3], by_z[0]):
         ring.send_up()
     by_x[1].send_down()
+    for ring in (by_x[2], by_z[2], by_x[1]):
+        ring.pass_on()
     pass_rest(weights, 0)
     third(3)
     for ring in (by_x[3], by_z[1], by_z[3], by_z[0]):
         ring.send_down()
     by_x[3].send_up()
+    for ring in (by_z[1], by_x[3], by_z[3], by_z[0]):
+        ring.pass_on()
+    close_rest(weights, 0)
     third(0)
     by_x[0].send_up()
     by_x[0].send_down()
-    pass_first(streams)
-    close_rest(weights, 0)
+    by_x[0].pass_on()
     close_first(streams)
     pass_rest(weights, 1)
     close_rest(weights, 1)
@@ -962,7 +966,7 @@
     )(*parts)
 
 
-def gram_kernel(own, moments, grads, summed, new, turned, gram, part, *scratch):
+def gram_kernel(own, moments, grads, summed, new, chosen, gram, turned, part, *scratch):
     gots = scratch[:4]
     held, narrow_slots, wide_slots, send, recv = scratch[4:]
     place = my_place()
@@ -992,6 +996,7 @@
         arrival.wait_recv()
     half = turned.at[:, pl.ds(pl.multiple_of(place["c"] * 512, 512), 512)]
     net.put(half, half, other_core(place)).wait_recv()
+    chosen[...] = turned[pl.ds(pl.multiple_of(place["c"] * 160, 160), 160), :]
     @pl.loop(0, 4)
     def _(k):
         rows = pl.ds(pl.multiple_of(place["c"] * 512 + k * 128, 128), 128)
@@ -1036,7 +1041,7 @@
 
 def gram_of(packed, moments, grads):
     count = 22 + 4 + 2 * 12 + 40
-    scratch = [pltpu.VMEM((4, 4, 32, DP), F32)]
+    scratch = [pltpu.VMEM((320, DP), F32), pltpu.VMEM((4, 4, 32, DP), F32)]
     scratch += got_shapes(2, 32, 512, F32, F32, 1) * 2
     scratch += [
         pltpu.VMEM((32, 128), F32),
@@ -1050,7 +1055,7 @@
         out_shape=[
             jax.ShapeDtypeStruct((32, 128), F32),
             jax.ShapeDtypeStruct((4, 320, 128), F32),
-            jax.ShapeDtypeStruct((320, DP), F32),
+            jax.ShapeDtypeStruct((160, DP), F32),
             jax.ShapeDtypeStruct((2, 4, 4, 32, DP), F32),
         ],
         in_specs=[VMEM] * 3,
@@ -1126,48 +1131,49 @@
 
     out[...] = turned[...] * scale
 
-    def advance(count):
-        def emit_step(i, j, value):
+    def emit_step(count):
+        def emit(i, j, value):
             value = NS_B * power[blocks(i), blocks(j)] + NS_C * value
             put(q_parts, i, j, value + jnp.where(diagonal(i, j), NS_A, 0.0), count)
 
-        def emit_half(i, j, value):
-            put(t_parts, i, j, value, 2)
-
-        def emit_power(i, j, value):
-            power[blocks(i), blocks(j)] = value
-            put(a_parts, i, j, value, 2)
-
-        mirrored(a_parts, a_parts, 2, emit_step)
+        return emit
+
+    def emit_half(i, j, value):
+        put(t_parts, i, j, value, 2)
+
+    def emit_power(i, j, value):
+        power[blocks(i), blocks(j)] = value
+        put(a_parts, i, j, value, 2)
+
+    def applied(target, rows, source, matrix):
+        current = split(source, 2)
+
+        @pl.loop(0, 4)
+        def _(j):
+            target[rows, blocks(j)] = product(current, [ref[:, blocks(j)] for ref in matrix[:2]])
+
+    everything = pl.ds(0, 160)
+
+    def advance(count):
+        mirrored(a_parts, a_parts, 2, emit_step(count))
         mirrored(q_parts, a_parts, count, emit_half)
         mirrored(t_parts, q_parts, 2, emit_power)
-        current = split(out[...], 2)
-
-        @pl.loop(0, 4)
-        def _(j):
-            out[:, blocks(j)] = product(current, [ref[:, blocks(j)] for ref in q_parts[:2]])
+        applied(out, everything, out[...], q_parts)
 
     advance(3)
 
-    @pl.loop(0, ITERS - 2)
+    @pl.loop(0, ITERS - 3)
     def _(_step):
         advance(2)
 
-    current = split(out[...], 2)
-    once = power
-
-    @pl.loop(0, 4)
-    def _(j):
-        once[0:160, blocks(j)] = product(current, [ref[:, blocks(j)] for ref in a_parts[:2]])
-
-    applied = split(once[0:160, :], 2)
-
-    @pl.loop(0, 4)
-    def _(j):
-        twice = product(applied, [ref[:, blocks(j)] for ref in a_parts[:2]])
-        out[:, blocks(j)] = (
-            NS_A * out[:, blocks(j)] + NS_B * once[0:160, blocks(j)] + NS_C * twice
-        )
+    mirrored(a_parts, a_parts, 2, emit_step(2))
+    applied(out, everything, out[...], q_parts)
+    once, twice, work = pl.ds(0, 160), pl.ds(160, 160), pl.ds(320, 160)
+    for source, result in ((None, once), (once, twice)):
+        applied(power, work, out[...] if source is None else power[source, :], q_parts)
+        applied(power, result, power[work, :], a_parts)
+        applied(power, result, power[result, :], q_parts)
+    out[...] = NS_A * out[...] + NS_B * power[once, :] + NS_C * power[twice, :]
 
 
 def newton(gram, turned):
@@ -1398,7 +1404,7 @@
             - SMOOTH / V
         )
     ).astype(BF16)
-    table_grad_rows = dot(d_logits, all_rows, 0, 0)
+    table_grad_rows = lax.optimization_barrier(dot(d_logits, all_rows, 0, 0))
     d_by_core = d_logits.reshape(64, 2, 32, 384)
     d_mine = lax.dynamic_index_in_dim(d_by_core, core, 1, keepdims=False).reshape(2048, 384)
     d_theirs = lax.dynamic_index_in_dim(d_by_core, 1 - core, 1, keepdims=False).reshape(2048, 384)
@@ -1501,7 +1507,6 @@
     grad_norm = jnp.sqrt(summed[24, 0] + jnp.sum(gain_grad * gain_grad)) / token_count
     factor = jnp.minimum(1.0, CLIP_NORM / grad_norm) / token_count
     gram = gram.reshape(DP, DP)
-    turned = lax.dynamic_slice_in_dim(turned, core * 160, 160)
     current = newton(gram, turned)
     pieces = current.reshape(160, 2, 4, 128).transpose(2, 1, 0, 3).reshape(8, 160, 128)
     pieces = lax.all_to_all(pieces, "wide", split_axis=0, concat_axis=0)

time: 864 us -> 842 us (0.975)
  matrix products: 128 us -> 117 us
  Pallas kernels: 572 us -> 562 us
    dot_general x20, matrix products: 95 us -> 84.2 us  [dot(): lax.dot_general(left, right, (((left_axis,), (right_axis,)), ((), ())), p...]
    unnamed x230 -> x244, local copies, waits for them, and re-layouts: 27.6 us -> 24.2 us
  transfers between devices with their start and end apart: 11 -> 11, of which waited for: 0 -> 0; matrix products, arithmetic and copies ran while one was open for 18% -> 24% of each run, Pallas kernels for 12% -> 33%
where the time goes in v7:
time: 842 us; the launch traced here: 833 us
  Pallas kernels  562 us (67%)
  matrix products  117 us (14%)
  other arithmetic  68 us (8%)
  local copies, waits for them, and re-layouts  61.4 us (7%)
  between operations  12.1 us (1%)
  starting transfers between devices  11.6 us (1%)
    pallas_call x1, Pallas kernels, fetch(): pl.pallas_call(fetch_kernel, out_shape=shapes, in_specs=[ANY] * 6 + [pl.B...  154 us
    pallas_call x1, Pallas kernels, scatter_grads(): pl.pallas_call(grads_kernel, out_shape=[jax.ShapeDtypeStruct((384, DP), F...  140 us
    dot_general x20, matrix products, dot(): lax.dot_general(left, right, (((left_axis,), (right_axis,)), ((), ())), p...  84.2 us
    pallas_call x1, Pallas kernels, newton(): pl.pallas_call(newton_kernel, out_shape=jax.ShapeDtypeStruct((160, DP), F...  79.8 us
    pallas_call x1, Pallas kernels, gram_of(): pl.pallas_call(gram_kernel, out_shape=[jax.ShapeDtypeStruct((32, 128), F3...  68.9 us
    pallas_call x1, Pallas kernels, gather_rows(): pl.pallas_call(rows_kernel, out_shape=jax.ShapeDtypeStruct((4, 4, 4, 2, 3...  33.6 us
    pallas_call x1, Pallas kernels, scatter_rows(): pl.pallas_call(row_sums_kernel, out_shape=jax.ShapeDtypeStruct((32, DP),...  32.3 us
    unnamed x244, local copies, waits for them, and re-layouts  24.2 us
  transfers between devices with their start and end apart: 11, of which 0 were waited for; matrix products, arithmetic and copies ran while one was open for 24% of the time, Pallas kernels for 33%

profile of v7, /device:TPU:1, one launch (start us, length us, event | category | flops | bytes accessed | tf_op | source)
XLA Modules:
  0.0 832.6 jit_solution(14887542230689503262)
XLA Ops:
  0.9 4.8 convolution_convert_fusion.4
  18.3 153.9 %fetch.1 = (bf16[4,4,112,1024]{3,2,1,0:T(8,128)(2,1)}, bf16[2,4,2,64,1024]{4,3,2,1,0:T(8,128)(2,1)}, bf16[2,2,2,4,160,1024]{5,4,3,2,1,0:T(8,128)(2,1)}, bf16[2,4...) custom-call(bf16[112,128]{1,0:T(8,128)(2,1)} %copy.63.gi, ...), custom_call_target="tpu_custom_call" | custom-call | tf_op jit(solution)/shard_map/fetch/pallas_call | solution.py:323
  188.8 18.4 %gather_keys.1 = bf16[4,320,1024]{2,1,0:T(8,128)(2,1)S(1)} custom-call(bf16[4,320,128]{2,1,0:T(8,128)(2,1)S(1)} %pad_maximum_fusion.6.own), custom_call_target="tpu_custom_call" | custom-call | tf_op jit(solution)/shard_map/gather_keys/pallas_call | solution.py:890
  235.3 4.5 multiply_reduce_fusion.8
  240.6 33.6 %gather_rows.1 = bf16[4,4,4,2,32,1024]{5,4,3,2,1,0:T(8,128)(2,1)S(1)} custom-call(bf16[32,1024]{1,0:T(8,128)(2,1)S(1)} %gather_fusion), custom_call_target="tpu_custom_call" | custom-call | tf_op jit(solution)/shard_map/gather_rows/pallas_call | solution.py:375
  274.3 6.3 fusion.168
  283.3 5.2 multiply_reduce_fusion.1
  289.1 18.3 %row_totals.1 = f32[32,128]{1,0:T(8,128)} custom-call(f32[2,32,128]{2,1,0:T(8,128)} %pad_maximum_fusion.9.own), custom_call_target="tpu_custom_call" | custom-call | tf_op jit(solution)/shard_map/row_totals/pallas_call | solution.py:434
  308.2 8.1 multiply_convert_fusion
  319.6 4.6 fusion.171
  341.4 4.0 fusion.170
  345.4 4.0 add_convert_fusion
  349.4 32.3 %scatter_rows.1 = f32[32,1024]{1,0:T(8,128)S(1)} custom-call(bf16[4,4,4,32,1024]{4,3,2,1,0:T(8,128)(2,1)S(1)} %bitcast.422), custom_call_target="tpu_custom_call" | custom-call | tf_op jit(solution)/shard_map/scatter_rows/pallas_call | solution.py:687
  386.6 6.4 fusion.67
  395.1 3.7 multiply_reduce_fusion.4
  400.4 3.8 convolution_convert_fusion.7
  404.2 4.1 collective-permute-start.4
  408.6 4.7 fusion.32
  413.3 7.9 fusion.1
  421.1 7.2 fusion.3
  431.2 3.9 fusion.57
  436.5 4.6 fusion.4
  441.2 9.3 %fusion.6 = bf16[5,3,128,1024]{2,3,1,0:T(8,128)(2,1)} fusion(f32[5,1024,128,3]{2,1,3,0:T(8,128)} %get-tuple-element.167, f32[5,3,128,1024]{2,3,1,0:T(8,128)} %copy-done.2, f32[5,3,128]{2,1,0:T(4,128)S(1)} %get-tuple-element.166, f32[5,3,128]{2,1,0:T(4,128)S(1)} %log_add_fusion.1), kind=kLoop, calls=%fused_computation.19 | loop fusion | flops 7864320 | bytes 19676160 | tf_op jit(solution)/shard_map/convert_element_type | solution.py:1436
  455.2 17.4 %sum_keys.1 = f32[4,320,128]{2,1,0:T(8,128)S(1)} custom-call(f32[320,1024]{1,0:T(8,128)S(1)} %bitcast.424, f32[320,1024]{1,0:T(8,128)S(1)} %bitcast.423, f32[320,1024]{1,0:T(8,128)S(1)} %bitcast.426, f32[320,1024]{1,0:T(8,128)S(1)} %bitcast.425), custom_call_target="tpu_custom_call" | custom-call | tf_op jit(solution)/shard_map/sum_keys/pallas_call | solution.py:950
  474.5 3.7 fusion.51
  481.7 4.9 convolution_convert_fusion.1
  490.0 4.0 convolution_convert_fusion.2
  494.0 7.0 convolution_convert_fusion
  501.0 139.7 %scatter_grads.1 = (f32[384,1024]{1,0:T(8,128)}, f32[3,224,128]{2,1,0:T(8,128)}) custom-call(bf16[256,1024]{1,0:T(8,128)(2,1)} %get-tuple-element.107.dx, s32[1,2048]{1,0:T(1,128)} %bitcast.503, bf16[4,4,112,512]{3,2,1,0:T(8,128)(2,1)} %bitcast.462, bf16[2,4,2,64,512]{4,3,2,1,0:T(8,128)(2,1)} %bitcast.467, bf16[2,2,2,4,160,512]{5,4,3,2,1,0:T(8,128)(2,1)} %bitcast.441, ...), custom_call_target="tpu_custom_call" | custom-call | tf_op jit(solution)/shard_map/scatter_grads/pallas_call | solution.py:854
  650.8 68.9 %gram_sums.1 = (f32[32,128]{1,0:T(8,128)S(1)}, f32[4,320,128]{2,1,0:T(8,128)S(1)}, f32[160,1024]{1,0:T(8,128)S(1)}, f32[2,4,4,32,1024]{4,3,2,1,0:T(8,128)S(1)}) custom-call(f32[32,128]{1,0:T(8,128)S(1)} %select_maximum_fusion.1.own, f32[4,320,128]{2,1,0:T(8,128)S(1)} %pad_maximum_fusion.2.moments, f32[4,320,128]{2,1,0:T(8,128)S(1)} %pad_maximum_fusion.3.grads), custom_call_target="tpu_custom_call" | custom-call | tf_op jit(solution)/shard_map/gram_sums/pallas_call | solution.py:1053
  720.3 79.8 %newton.1 = f32[160,1024]{1,0:T(8,128)S(1)} custom-call(f32[1024,1024]{1,0:T(8,128)S(1)} %bitcast.427, f32[160,1024]{1,0:T(8,128)S(1)} %get-tuple-element.45.turned), custom_call_target="tpu_custom_call" | custom-call | tf_op jit(solution)/shard_map/newton/pallas_call | solution.py:1180
  807.7 8.6 %fusion.154 = (bf16[384,960]{0,1:T(8,128)(2,1)}, f32[384,960]{0,1:T(8,128)}, f32[384,960]{0,1:T(8,128)}, f32[384,960]{0,1:T(8,128)}) fusion(f32[384,960]{0,1:T(8,128)} %param.27, f32[384,960]{0,1:T(8,128)} %param.33, f32[384,960]{0,1:T(8,128)} %param.32, s32[960]{0:T(1024)} %copy-done.93, s32[960]{0:T(1024)S(1)} %copy-done.88, s32[960]{0:T(1024)} %copy-done.91, ...), kind=kOutput, calls=%fused_computation.358 | convolution fusion | flops 2310537216 | bytes 12747652 | tf_op jit(solution)/shard_map/dot_general | solution.py:1230
  (491 shorter events, 133.1 us)
Async XLA Ops:
  0.7 220.5 %copy-start.87 = (s32[960]{0:T(1024)}, s32[960]{0:T(1024)S(1)}, u32[]{:S(2)}) copy-start(s32[960]{0:T(1024)S(1)} %get-tuple-element.175) | copy-start | bytes 11524
  0.8 11.7 %copy-start.38 = (f32[1,120,160]{1,2,0:T(8,128)S(1)}, f32[1,120,160]{1,2,0:T(8,128)}, u32[]{:S(2)}) copy-start(f32[1,120,160]{1,2,0:T(8,128)} %param.25) | copy-start | bytes 230404
  0.8 12.6 %copy-start.48 = (f32[1,120,100]{1,0,2:T(1,128)S(1)}, f32[1,120,100]{1,0,2:T(1,128)}, u32[]{:S(2)}) copy-start(f32[1,120,100]{1,0,2:T(1,128)} %param.22) | copy-start | bytes 144004
  0.8 13.5 %copy-start.35 = (f32[1,120,320]{1,2,0:T(8,128)S(1)}, f32[1,120,320]{1,2,0:T(8,128)}, u32[]{:S(2)}) copy-start(f32[1,120,320]{1,2,0:T(8,128)} %param.24) | copy-start | bytes 460804
  5.7 339.7 %collective-permute-start.1 = (bf16[384,1024]{0,1:T(8,128)(2,1)}, bf16[384,1024]{0,1:T(8,128)(2,1)}, u32[]{:S(2)}, u32[]{:S(2)}) collective-permute-start(bf16[384,1024]{0,1:T(8,128)(2,1)} %bitcast.12), channel_id=1, source_target_pairs={{0,16},{16,0},{32,48},{48,32},{64,80},{80,64},{96,112},{112,96},{1... | collective-permute-start | bytes 2359304 | tf_op jit(solution)/shard_map/ppermute | solution.py:1270
  10.1 166.4 %copy-start.58 = (f32[3,960]{1,0:T(4,128)S(1)}, f32[3,960]{1,0:T(4,128)}, u32[]{:S(2)}) copy-start(f32[3,960]{1,0:T(4,128)} %param.26) | copy-start | bytes 34564
  187.5 37.6 %copy-start.63 = (f32[1024]{0:T(1024)}, f32[1024]{0:T(1024)S(1)}, u32[]{:S(2)}) copy-start(f32[1024]{0:T(1024)S(1)} %mul.809) | copy-start | bytes 12292
  188.6 20.5 %copy-start.19 = (bf16[128,15,64]{0,2,1:T(8,128)(2,1)}, bf16[128,15,64]{0,2,1:T(8,128)(2,1)S(1)}, u32[]{:S(2)}) copy-start(bf16[128,15,64]{0,2,1:T(8,128)(2,1)S(1)} %get-tuple-element.125) | copy-start | bytes 737284
  188.7 26.4 %copy-start.17 = (bf16[128,15,64]{0,2,1:T(8,128)(2,1)}, bf16[128,15,64]{0,2,1:T(8,128)(2,1)S(1)}, u32[]{:S(2)}) copy-start(bf16[128,15,64]{0,2,1:T(8,128)(2,1)S(1)} %get-tuple-element.124) | copy-start | bytes 737284
  233.3 247.8 %collective-permute-start.8 = (bf16[256,2560]{1,0:T(8,128)(2,1)}, bf16[256,2560]{1,0:T(8,128)(2,1)}, u32[]{:S(2)}, u32[]{:S(2)}) collective-permute-start(bf16[256,2560]{1,0:T(8,128)(2,1)} %multiply_convert_fusion.1), channel_id=1, source_target_pairs={{0,16},{16,0},{32,48},{48,32},{64,80},{80,64},{96,112},{112,96},{1... | collective-permute-start | bytes 3932168 | tf_op jit(solution)/shard_map/ppermute | solution.py:1270
  239.8 34.5 %copy-start.86 = (f32[256]{0:T(256)}, f32[256]{0:T(256)S(1)}, u32[]{:S(2)}) copy-start(f32[256]{0:T(256)S(1)} %get-tuple-element.161) | copy-start | bytes 3076
  239.8 34.4 %copy-start.66 = (f32[256]{0:T(256)}, f32[256]{0:T(256)S(1)}, u32[]{:S(2)}) copy-start(f32[256]{0:T(256)S(1)} %fusion.137) | copy-start | bytes 3076
  308.2 11.4 %copy-start.1 = (bf16[4,4,4,2,32,1024]{5,4,3,2,1,0:T(8,128)(2,1)S(1)}, bf16[4,4,4,2,32,1024]{5,4,3,2,1,0:T(8,128)(2,1)}, u32[]{:S(2)}) copy-start(bf16[4,4,4,2,32,1024]{5,4,3,2,1,0:T(8,128)(2,1)} %copy-done) | copy-start | bytes 25165828
  318.4 27.0 %collective-permute-start = (bf16[2048,384]{1,0:T(8,128)(2,1)}, bf16[2048,384]{1,0:T(8,128)(2,1)}, u32[]{:S(2)}, u32[]{:S(2)}) collective-permute-start(bf16[2048,384]{1,0:T(8,128)(2,1)} %bitcast.66), channel_id=1, source_target_pairs={{0,16},{16,0},{32,48},{48,32},{64,80},{80,64},{96,112},{112,96},{1... | collective-permute-start | bytes 4718600 | tf_op jit(solution)/shard_map/ppermute | solution.py:1270
  324.2 12.8 %copy-start.29 = (bf16[256,1024]{1,0:T(8,128)(2,1)S(1)}, bf16[256,1024]{1,0:T(8,128)(2,1)}, u32[]{:S(2)}) copy-start(bf16[256,1024]{1,0:T(8,128)(2,1)} %copy-done.28) | copy-start | bytes 1572868
  383.3 11.1 %slice-start.5 = ((s8[10485760]{0:T(1024)(128)(4,1)}), s8[4194304]{0:T(1024)(128)(4,1)S(1)}, s32[]{:S(2)}) async-start(s8[10485760]{0:T(1024)(128)(4,1)} %bitcast.519), calls=%async_computation.6 | async-start | bytes 8388608
  404.2 82.8 %collective-permute-start.4 = (bf16[256,1024]{1,0:T(8,128)(2,1)}, bf16[256,1024]{1,0:T(8,128)(2,1)}, u32[]{:S(2)}, u32[]{:S(2)}) collective-permute-start(bf16[256,1024]{1,0:T(8,128)(2,1)} %get-tuple-element.92), channel_id=1, source_target_pairs={{0,16},{16,0},{32,48},{48,32},{64,80},{80,64},{96,112},{112,96},{1... | collective-permute-start | bytes 1572872 | tf_op jit(solution)/shard_map/ppermute | solution.py:1270
  408.2 85.7 %collective-permute-start.6 = (bf16[256,5120]{1,0:T(8,128)(2,1)}, bf16[256,5120]{1,0:T(8,128)(2,1)}, u32[]{:S(2)}, u32[]{:S(2)}) collective-permute-start(bf16[256,5120]{1,0:T(8,128)(2,1)} %copy-done.25), channel_id=1, source_target_pairs={{0,16},{16,0},{32,48},{48,32},{64,80},{80,64},{96,112},{112,96},{1... | collective-permute-start | bytes 7864328 | tf_op jit(solution)/shard_map/ppermute | solution.py:1270
  455.2 17.5 %copy-start.46 = (bf16[256,512]{1,0:T(8,128)(2,1)S(1)}, bf16[256,512]{1,0:T(8,128)(2,1)}, u32[]{:S(2)}) copy-start(bf16[256,512]{1,0:T(8,128)(2,1)} %get-tuple-element.113) | copy-start | bytes 786436
  455.2 18.5 %copy-start.33 = (f32[256,64]{0,1:T(8,128)S(1)}, f32[256,64]{0,1:T(8,128)}, u32[]{:S(2)}) copy-start(f32[256,64]{0,1:T(8,128)} %copy-done.32) | copy-start | bytes 196612
  472.7 8.9 %collective-permute-start.9 = (bf16[256,512]{1,0:T(8,128)(2,1)S(1)}, bf16[256,512]{1,0:T(8,128)(2,1)S(1)}, u32[]{:S(2)}, u32[]{:S(2)}) collective-permute-start(bf16[256,512]{1,0:T(8,128)(2,1)S(1)} %copy-done.46), channel_id=1, source_target_pairs={{0,16},{16,0},{32,48},{48,32},{64,80},{80,64},{96,112},{112,96},{1... | collective-permute-start | bytes 786440 | tf_op jit(solution)/shard_map/ppermute | solution.py:1270
  478.2 11.8 %collective-permute-start.2 = (bf16[256,1792]{1,0:T(8,128)(2,1)}, bf16[256,1792]{1,0:T(8,128)(2,1)}, u32[]{:S(2)}, u32[]{:S(2)}) collective-permute-start(bf16[256,1792]{1,0:T(8,128)(2,1)} %fusion.51), channel_id=1, source_target_pairs={{0,16},{16,0},{32,48},{48,32},{64,80},{80,64},{96,112},{112,96},{1... | collective-permute-start | bytes 2752520 | tf_op jit(solution)/shard_map/ppermute | solution.py:1270
  481.1 5.5 collective-permute-start.5
  481.6 8.3 %collective-permute-start.3 = (bf16[256,512]{1,0:T(8,128)(2,1)S(1)}, bf16[256,512]{1,0:T(8,128)(2,1)S(1)}, u32[]{:S(2)}, u32[]{:S(2)}) collective-permute-start(bf16[256,512]{1,0:T(8,128)(2,1)S(1)} %get-tuple-element.119), channel_id=1, source_target_pairs={{0,16},{16,0},{32,48},{48,32},{64,80},{80,64},{96,112},{112,96},{1... | collective-permute-start | bytes 786440 | tf_op jit(solution)/shard_map/ppermute | solution.py:1270
  486.6 7.3 collective-permute-start.7
  501.0 144.0 %copy-start.13 = (f32[384,1024]{1,0:T(8,128)S(1)}, f32[384,1024]{1,0:T(8,128)}, u32[]{:S(2)}) copy-start(f32[384,1024]{1,0:T(8,128)} %fusion.171) | copy-start | bytes 4718596
  720.3 87.4 %copy-start.88 = (s32[960]{0:T(1024)S(1)}, s32[960]{0:T(1024)}, u32[]{:S(2)}) copy-start(s32[960]{0:T(1024)} %copy-done.87) | copy-start | bytes 11524
  801.4 22.0 %all-to-all-start = ((f32[8,160,128]{2,1,0:T(8,128)}), f32[8,160,128]{2,1,0:T(8,128)S(1)}, u32[]{:S(2)}, u32[]{:S(2)}) async-start(f32[8,160,128]{2,1,0:T(8,128)} %bitcast.148), calls=%async_computation | async-start | bytes 1310720 | tf_op jit(solution)/shard_map/all_to_all | solution.py:1512
  807.7 15.0 %copy-start.59 = (f32[3,960]{1,0:T(4,128)S(1)}, f32[3,960]{1,0:T(4,128)}, u32[]{:S(2)}) copy-start(f32[3,960]{1,0:T(4,128)} %param.26) | copy-start | bytes 34564
  807.7 15.0 %copy-start.70 = (f32[3,960]{1,0:T(4,128)S(1)}, f32[3,960]{1,0:T(4,128)}, u32[]{:S(2)}) copy-start(f32[3,960]{1,0:T(4,128)} %param.35) | copy-start | bytes 34564
  807.7 15.0 %copy-start.71 = (f32[3,960]{1,0:T(4,128)S(1)}, f32[3,960]{1,0:T(4,128)}, u32[]{:S(2)}) copy-start(f32[3,960]{1,0:T(4,128)} %param.34) | copy-start | bytes 34564
  817.2 11.4 %copy-start.34 = (f32[1,120,320]{2,1,0:T(8,128)S(1)}, f32[1,120,320]{2,1,0:T(8,128)}, u32[]{:S(2)}) copy-start(f32[1,120,320]{2,1,0:T(8,128)} %copy.97) | copy-start | bytes 460804
  (92 other events, 372.2 us)
